TPU v7x, 32 devices: a whole 2x2x4 slice. The times are simulated.
32 devices in a mesh: segment: 8 (over z, x), seq: 4 (over y, core).
Axes of the slice: x: 2, y: 2, z: 4, core: 2. Of those that a mesh axis runs over, the one named last changes fastest.
Arguments:
- projected: bfloat16 [8, 256, 6144], P('segment', 'seq'), may hold values from -128 to 128
- stream_before: bfloat16 [8, 256, 2048], P('segment', 'seq'), may hold values from -3 to 3
- out_weight: bfloat16 [8, 2048, 2048], P('segment', 'seq'), may hold values from -0.25 to 0.25
- proj_weight: bfloat16 [8, 2048, 6144], P('segment', None, 'seq'), may hold values from -0.125 to 0.125
- norm_gain: float32 [8, 2048], P('segment'), may hold values from 0.1 to 1.9
- block_mask: int32 [1, 2, 2], replicated, may hold values from 0 to 1, as said below
- token_order: int32 [256], replicated, may hold values from 0 to 255, each once
Outputs:
- incoming: bfloat16 [8, 256, 2048], P('segment', 'seq')
- next_projected: bfloat16 [8, 256, 6144], P('segment', None, 'seq')
Inputs may be any that keep to these rules, and one draw needn't show every extreme that they name: Each query block may always see the key block at its own place in the window (block_mask[w, b, b] = 1).
All inputs are finite; a program needn't handle non-finite values.
Results may differ from a plain program's by a relative error of at most 0.014.
Values may be sent and summed in bfloat16 or wider, within the bound.
No kernel may reach another device: no remote copies, remote signals or barrier semaphores. Data moves between devices by JAX's collectives and lax.ppermute only.
A program may use at most 64 MiB of HBM per device.

v0:
```python
import jax
import jax.numpy as jnp
from jax import lax
from jax.sharding import PartitionSpec as P

HEADS = 16
DH = 128
WIN = 256
BLOCK = 128


def from_behind(x, axis, by):
    size = lax.axis_size(axis)
    return lax.ppermute(x, axis, [(i, (i + by) % size) for i in range(size)])


def normalize(values, gain):
    widened = values.astype(jnp.float32)
    scale = lax.rsqrt(jnp.mean(widened * widened, axis=-1, keepdims=True) + 1e-06)
    return (widened * scale * gain[None, :]).astype(jnp.bfloat16)


def local(projected, stream_before, out_weight, proj_weight, norm_gain, block_mask, token_order):
    group_size = lax.axis_size("seq")
    local_heads = HEADS // group_size
    tok_rows = projected.shape[1]
    all_tokens = tok_rows * group_size
    by_head = lax.all_to_all(projected[0], "seq", split_axis=1, concat_axis=0, tiled=True)
    ordered = by_head.reshape(all_tokens, local_heads, 3, DH)[token_order]
    windows = ordered.reshape(all_tokens // WIN, WIN, local_heads, 3, DH)
    allowed = jnp.repeat(jnp.repeat(block_mask, BLOCK, axis=1), BLOCK, axis=2) > 0
    scores = jnp.einsum(
        "wqhd,wkhd->whqk",
        windows[:, :, :, 0],
        windows[:, :, :, 1],
        preferred_element_type=jnp.float32,
    ) * DH ** (-0.5)
    masked = jnp.where(allowed[:, None], scores, -jnp.inf)
    highest = jnp.max(masked, axis=-1, keepdims=True)
    weights = jnp.exp(masked - highest)
    probs = (weights / jnp.sum(weights, axis=-1, keepdims=True)).astype(jnp.bfloat16)
    attended = jnp.einsum(
        "whqk,wkhd->wqhd", probs, windows[:, :, :, 2], preferred_element_type=jnp.float32
    ).astype(jnp.bfloat16)
    placed = (
        jnp.zeros((all_tokens, local_heads, DH), jnp.bfloat16)
        .at[token_order]
        .set(attended.reshape(all_tokens, local_heads, DH))
    )
    placed = placed.reshape(all_tokens, local_heads * DH)
    branch = lax.psum_scatter(
        jnp.dot(placed, out_weight[0], preferred_element_type=jnp.float32).astype(jnp.bfloat16),
        "seq",
        scatter_dimension=0,
        tiled=True,
    ).astype(jnp.float32)
    stream_after = (stream_before[0].astype(jnp.float32) + branch).astype(jnp.bfloat16)
    incoming = from_behind(stream_after, "segment", 1)
    normed = normalize(incoming, norm_gain[0])
    following = jnp.dot(
        lax.all_gather(normed, "seq", axis=0, tiled=True),
        proj_weight[0],
        preferred_element_type=jnp.float32,
    ).astype(jnp.bfloat16)
    return (incoming[None], following[None])


def solution(mesh):
    placed = (
        P("segment", "seq", None),
        P("segment", "seq", None),
        P("segment", "seq", None),
        P("segment", None, "seq"),
        P("segment", None),
        P(),
        P(),
    )
    return jax.shard_map(
        local,
        mesh=mesh,
        in_specs=placed,
        out_specs=(P("segment", "seq", None), P("segment", None, "seq")),
        check_vma=False,
    )
```

profile of v0, /device:TPU:0, one launch (start us, length us, event | category | flops | bytes accessed | tf_op | source)
XLA Modules:
  0.0 112.3 jit_solution(12092836304062361493)
XLA Ops:
  7.2 2.5 %all_to_all.12 = bf16[64,4,1536]{2,1,0:T(4,128)(2,1)S(1)} reshape(bf16[1,64,6144]{2,1,0:T(8,128)(2,1)} %param.7) | data formatting | bytes 1572864 | tf_op jit(solution)/shard_map/all_to_all | solution.py:28
  9.7 1.0 copy.12
  10.7 4.2 %all-to-all-start = ((bf16[64,4,1536]{2,0,1:T(8,128)(2,1)}), bf16[64,4,1536]{2,0,1:T(8,128)(2,1)S(1)}, u32[]{:S(2)}, u32[]{:S(2)}) async-start(bf16[64,4,1536]{2,0,1:T(8,128)(2,1)} %copy.12), calls=%async_computation | async-start | bytes 1572864 | tf_op jit(solution)/shard_map/all_to_all | solution.py:28
  14.9 0.1 copy.15
  15.1 11.4 %all-to-all-done = bf16[64,4,1536]{2,0,1:T(8,128)(2,1)S(1)} async-done(((bf16[64,4,1536]{2,0,1:T(8,128)(2,1)}), bf16[64,4,1536]{2,0,1:T(8,128)(2,1)S(1)}, u32[]{:S(2)}, u32[]{:S(2)}) %all-to-all-start) | async-done | bytes 786464 | tf_op jit(solution)/shard_map/all_to_all | solution.py:28
  26.6 1.3 %reshape.89 = bf16[256,4,3,128]{3,2,1,0:T(4,128)(2,1)} reshape(bf16[4,64,1536]{2,1,0:T(8,128)(2,1)S(1)} %bitcast.60) | data formatting | bytes 1572864 | tf_op jit(solution)/shard_map/reshape | solution.py:29
  27.9 1.6 %copy.13 = bf16[256,4,3,128]{3,1,2,0:T(4,128)(2,1)S(1)} copy(bf16[256,4,3,128]{3,2,1,0:T(4,128)(2,1)} %reshape.89) | data formatting | bytes 1572864 | tf_op jit(solution)/shard_map/reshape | solution.py:29
  29.5 2.3 %gather_fusion = bf16[256,4,3,128]{3,1,2,0:T(4,128)(2,1)} fusion(bf16[256,4,3,128]{3,1,2,0:T(4,128)(2,1)S(1)} %copy.13, s32[1024]{0:T(1024)S(1)} %pad_clamp_fusion), kind=kCustom, calls=%fused_computation | custom fusion | bytes 1573888 | tf_op jit(solution)/shard_map/gather | solution.py:29
  31.9 1.3 %copy.29 = bf16[256,4,3,128]{3,0,1,2:T(8,128)(2,1)S(1)} copy(bf16[256,4,3,128]{3,1,2,0:T(4,128)(2,1)} %gather_fusion) | data formatting | bytes 1572864 | tf_op jit(solution)/shard_map/gather | solution.py:29
  33.2 1.3 %fusion.12 = f32[4,256,256]{1,2,0:T(8,128)} fusion(pred[256,256]{0,1:T(8,128)(4,1)S(1)} %bitcast.66, bf16[1,256,4,3,128]{4,1,2,3,0:T(8,128)(2,1)S(1)} %bitcast.63), kind=kOutput, calls=%fused_computation.12 | convolution fusion | flops 67633152 | bytes 1638400 | tf_op jit(solution)/shard_map/wqhd,wkhd->whqk/dot_general | solution.py:32
  34.5 0.5 fusion.23
  35.0 2.0 %fusion.13 = bf16[256,4,128]{0,2,1:T(8,128)(2,1)S(1)} fusion(f32[4,256]{1,0:T(4,128)S(1)} %fusion.23, bf16[1,256,4,3,128]{4,1,2,3,0:T(8,128)(2,1)S(1)} %bitcast.65, f32[4,256,256]{1,2,0:T(8,128)} %fusion.12), kind=kOutput, calls=%fused_computation.14 | convolution fusion | flops 68027648 | bytes 2625536 | tf_op jit(solution)/shard_map/whqk,wkhd->wqhd/dot_general | solution.py:42
  36.9 0.2 copy.18
  37.2 7.0 %scatter_fusion = bf16[256,4,128]{2,1,0:T(4,128)(2,1)S(1)} fusion(bf16[256,4,128]{2,1,0:T(4,128)(2,1)S(1)} %broadcast_in_dim.35, s32[256]{0:T(256)S(1)} %compare_select_fusion, bf16[256,4,128]{2,1,0:T(4,128)(2,1)S(1)} %copy.18), kind=kCustom, calls=%fused_computation.1 | custom fusion | bytes 787456 | tf_op jit(solution)/shard_map/scatter | solution.py:48
  44.2 1.7 %convolution_convert_fusion = bf16[256,2048]{1,0:T(8,128)(2,1)} fusion(bf16[1,512,2048]{2,1,0:T(8,128)(2,1)S(1)} %copy-done, bf16[32,8,4,128]{3,2,1,0:T(4,128)(2,1)S(1)} %bitcast.62), kind=kOutput, calls=%fused_computation.5 | convolution fusion | flops 537395200 | bytes 3407872 | tf_op jit(solution)/shard_map/dot_general | solution.py:52
  46.0 25.9 %reduce-scatter.2.cloned.1.call-done = bf16[64,2048]{1,0:T(8,128)(2,1)} async-done(((bf16[256,2048]{1,0:T(8,128)(2,1)}), bf16[64,2048]{1,0:T(8,128)(2,1)}) %reduce-scatter.2.cloned.1.call-update) | async-done | bytes 262160 | tf_op jit(solution)/shard_map/reduce_scatter | solution.py:51
  71.9 1.0 fusion.17
  73.0 1.5 %collective-permute-start = (bf16[64,2048]{1,0:T(8,128)(2,1)S(1)}, bf16[64,2048]{1,0:T(8,128)(2,1)S(1)}, u32[]{:S(2)}, u32[]{:S(2)}) collective-permute-start(bf16[64,2048]{1,0:T(8,128)(2,1)S(1)} %fusion.17), channel_id=1, source_target_pairs={{0,4},{4,8},{8,12},{12,16},{16,20},{20,24},{24,28},{28,0},{1,5},{5... | collective-permute-start | bytes 786440 | tf_op jit(solution)/shard_map/ppermute | solution.py:14
  74.5 9.3 %collective-permute-done = bf16[64,2048]{1,0:T(8,128)(2,1)S(1)} collective-permute-done((bf16[64,2048]{1,0:T(8,128)(2,1)S(1)}, bf16[64,2048]{1,0:T(8,128)(2,1)S(1)}, u32[]{:S(2)}, u32[]{:S(2)}) %collective-permute-start) | collective-permute-done | bytes 262176 | tf_op jit(solution)/shard_map/ppermute | solution.py:14
  83.8 0.2 fusion.14
  83.9 0.8 fusion.16
  84.8 14.2 %all-gather.2.cloned.1.call-done = bf16[256,2048]{1,0:T(8,128)(2,1)} async-done(((bf16[64,2048]{1,0:T(8,128)(2,1)}), bf16[256,2048]{1,0:T(8,128)(2,1)}) %all-gather.2.cloned.1.call-update) | async-done | bytes 1048592 | tf_op jit(solution)/shard_map/all_gather | solution.py:61
  99.0 5.8 %fusion.6 = bf16[1,256,1536]{2,1,0:T(8,128)(2,1)} fusion(bf16[256,2048]{1,0:T(8,128)(2,1)} %all-gather.2.cloned.1.call-done, bf16[1,2048,1536]{2,1,0:T(8,128)(2,1)} %param.10), kind=kOutput, calls=%fused_computation.7 | convolution fusion | flops 1611005952 | bytes 8126464 | tf_op jit(solution)/shard_map/dot_general | solution.py:60
  104.8 0.7 copy.33
  (22 shorter events, 0.3 us)
Async XLA Ops:
  7.2 37.0 %copy-start = (bf16[1,512,2048]{2,1,0:T(8,128)(2,1)S(1)}, bf16[1,512,2048]{2,1,0:T(8,128)(2,1)}, u32[]{:S(2)}) copy-start(bf16[1,512,2048]{2,1,0:T(8,128)(2,1)} %param.9) | copy-start | bytes 6291460
  7.2 7.7 %copy-start.4 = (s32[1,2,2]{2,1,0:T(2,128)S(1)}, s32[1,2,2]{2,1,0:T(2,128)}, u32[]{:S(2)}) copy-start(s32[1,2,2]{2,1,0:T(2,128)} %param.12) | copy-start | bytes 52
  7.2 7.9 %copy-start.3 = (s32[256]{0:T(256)S(1)}, s32[256]{0:T(256)}, u32[]{:S(2)}) copy-start(s32[256]{0:T(256)} %param.13) | copy-start | bytes 3076
  10.7 15.9 %all-to-all-start = ((bf16[64,4,1536]{2,0,1:T(8,128)(2,1)}), bf16[64,4,1536]{2,0,1:T(8,128)(2,1)S(1)}, u32[]{:S(2)}, u32[]{:S(2)}) async-start(bf16[64,4,1536]{2,0,1:T(8,128)(2,1)} %copy.12), calls=%async_computation | async-start | bytes 1572864 | tf_op jit(solution)/shard_map/all_to_all | solution.py:28
  14.9 57.0 %reduce-scatter.2.cloned.1.call-start = ((), (), s32[]{:S(2)}) async-start(), calls=%async_computation.2 | async-start | bytes 1310720 | tf_op jit(solution)/shard_map/reduce_scatter | solution.py:51
  44.2 27.8 %copy-start.1 = (bf16[1,64,2048]{2,1,0:T(8,128)(2,1)S(1)}, bf16[1,64,2048]{2,1,0:T(8,128)(2,1)}, u32[]{:S(2)}) copy-start(bf16[1,64,2048]{2,1,0:T(8,128)(2,1)} %param.8) | copy-start | bytes 786436
  44.2 39.7 %copy-start.2 = (f32[1,2048]{1,0:T(1,128)S(1)}, f32[1,2048]{1,0:T(1,128)}, u32[]{:S(2)}) copy-start(f32[1,2048]{1,0:T(1,128)} %param.11) | copy-start | bytes 24580
  45.9 53.0 %all-gather.2.cloned.1.call-start = ((), (), s32[]{:S(2)}) async-start(), calls=%async_computation.3 | async-start | bytes 1310720 | tf_op jit(solution)/shard_map/all_gather | solution.py:61
  73.0 10.8 %collective-permute-start = (bf16[64,2048]{1,0:T(8,128)(2,1)S(1)}, bf16[64,2048]{1,0:T(8,128)(2,1)S(1)}, u32[]{:S(2)}, u32[]{:S(2)}) collective-permute-start(bf16[64,2048]{1,0:T(8,128)(2,1)S(1)} %fusion.17), channel_id=1, source_target_pairs={{0,4},{4,8},{8,12},{12,16},{16,20},{20,24},{24,28},{28,0},{1,5},{5... | collective-permute-start | bytes 786440 | tf_op jit(solution)/shard_map/ppermute | solution.py:14
Sparse Core Ops, SparseCore 0:
  46.1 25.8 reduce-scatter.1
  84.9 14.0 all-gather.1
where the time goes:
time: 113 us; the launch traced here: 112 us
  waiting for transfers between devices  60.9 us (54%)
  local copies, waits for them, and re-layouts  18.2 us (16%)
  between operations  14.2 us (13%)
  matrix products  11.2 us (10%)
  starting transfers between devices  5.8 us (5%)
  other arithmetic  2.02 us (2%)
    reduce_scatter x1, waiting for transfers between devices, local(): lax.psum_scatter(jnp.dot(placed, out_weight[0], preferred_element_type=jn...  25.9 us
    all_gather x1, waiting for transfers between devices, local(): lax.all_gather(normed, 'seq', axis=0, tiled=True)  14.2 us
    all_to_all x1, waiting for transfers between devices, local(): lax.all_to_all(projected[0], 'seq', split_axis=1, concat_axis=0, tiled=True)  11.4 us
    ppermute x1, waiting for transfers between devices, from_behind(): return lax.ppermute(x, axis, [(i, (i + by) % size) for i in range(size)])  9.28 us
    scatter x1, local copies, waits for them, and re-layouts, local(): placed = jnp.zeros((all_tokens, local_heads, DH), jnp.bfloat16).at[token_...  6.97 us
    dot_general x1, matrix products, local(): jnp.dot(lax.all_gather(normed, 'seq', axis=0, tiled=True), proj_weight[0]...  5.79 us
    all_to_all x1, starting transfers between devices, local(): lax.all_to_all(projected[0], 'seq', split_axis=1, concat_axis=0, tiled=True)  4.24 us
    gather x2, local copies, waits for them, and re-layouts, local(): ordered = by_head.reshape(all_tokens, local_heads, 3, DH)[token_order]  3.6 us
  transfers between devices with their start and end apart: 4, of which 4 were waited for; matrix products, arithmetic and copies ran while one was open for 0% of the time, Pallas kernels for 0%

commit v1 on v0

v1 whole, which is shorter than its diff:
```python
import functools

import jax
import jax.numpy as jnp
from jax import lax
from jax.experimental import pallas as pl
from jax.experimental.pallas import tpu as pltpu
from jax.sharding import PartitionSpec as P

HEADS = 16
DH = 128
WIN = 256
BLOCK = 128
NEG = -1e30
VMEM_LIMIT = 48 * 1024 * 1024

VM = pl.BlockSpec(memory_space=pltpu.VMEM)
ANY = pl.BlockSpec(memory_space=pl.ANY)


def swap(x, by):
    size = lax.axis_size("seq")
    return lax.ppermute(x, "seq", [(i, i ^ by) for i in range(size)])


def onward(x):
    size = lax.axis_size("segment")
    return lax.ppermute(x, "segment", [(i, (i + 1) % size) for i in range(size)])


def cut_kernel(n, src, *refs):
    outs, sems = refs[:n], refs[n]
    width = outs[0].shape[1]
    me = lax.axis_index("seq")
    copies = []
    for j in range(n - 1, -1, -1):
        at = pl.multiple_of((me ^ j) * width, 128)
        copies.append(pltpu.make_async_copy(src.at[0, :, pl.ds(at, width)], outs[j], sems.at[j]))
    for c in copies:
        c.start()
    for c in copies:
        c.wait()


def cut(projected, n):
    _, rows, columns = projected.shape
    width = columns // n
    return pl.pallas_call(
        functools.partial(cut_kernel, n),
        out_shape=[jax.ShapeDtypeStruct((rows, width), projected.dtype)] * n,
        in_specs=[ANY],
        out_specs=[VM] * n,
        scratch_shapes=[pltpu.SemaphoreType.DMA((n,))],
        name="cut_slices",
    )(projected)


def attend_kernel(n, lo, hi, *refs):
    blocks, bias, weight, outs = refs[:n], refs[n], refs[n + 1], refs[n + 2 :]
    rows, width = blocks[0].shape
    heads = width // (3 * DH)
    attended = []
    for h in range(heads):
        c = h * 3 * DH
        q = jnp.concatenate([blocks[j][:, c : c + DH] for j in range(lo, hi)], axis=0)
        k = jnp.concatenate([b[:, c + DH : c + 2 * DH] for b in blocks], axis=0)
        v = jnp.concatenate([b[:, c + 2 * DH : c + 3 * DH] for b in blocks], axis=0)
        s = lax.dot_general(q, k, (((1,), (1,)), ((), ())), preferred_element_type=jnp.float32)
        s = s * DH ** (-0.5) + bias[...]
        m = jnp.max(s, axis=-1, keepdims=True)
        e = jnp.exp(s - m)
        p = (e / jnp.sum(e, axis=-1, keepdims=True)).astype(jnp.bfloat16)
        attended.append(jnp.dot(p, v, preferred_element_type=jnp.float32).astype(jnp.bfloat16))
    attended = jnp.concatenate(attended, axis=1)
    term = jnp.dot(attended, weight[0], preferred_element_type=jnp.float32).astype(jnp.bfloat16)
    for j in range(hi - lo):
        outs[j][...] = term[j * rows : (j + 1) * rows]


def attend(blocks, bias, weight, lo, hi):
    n = len(blocks)
    rows, width = blocks[0].shape
    depth = weight.shape[2]
    heads = width // (3 * DH)
    tokens = n * rows
    return pl.pallas_call(
        functools.partial(attend_kernel, n, lo, hi),
        out_shape=[jax.ShapeDtypeStruct((rows, depth), jnp.bfloat16)] * (hi - lo),
        in_specs=[VM] * (n + 2),
        out_specs=[VM] * (hi - lo),
        compiler_params=pltpu.CompilerParams(vmem_limit_bytes=VMEM_LIMIT),
        cost_estimate=pl.CostEstimate(
            flops=2 * (hi - lo) * rows * heads * DH * (2 * tokens + depth),
            bytes_accessed=2 * heads * DH * depth,
            transcendentals=(hi - lo) * rows * tokens * heads,
        ),
        name="attend_project",
    )(*blocks, bias, weight)


def project_kernel(n, *refs):
    xs, gain, weight, out, normed = refs[:n], refs[n], refs[n + 1], refs[n + 2], refs[n + 3]
    rows = xs[0].shape[0]
    me = lax.axis_index("seq")

    @pl.when(pl.program_id(0) == 0)
    def _():
        for j in range(n):
            x = xs[j][...].astype(jnp.float32)
            scale = lax.rsqrt(jnp.mean(x * x, axis=-1, keepdims=True) + 1e-06)
            at = pl.multiple_of((me ^ j) * rows, rows)
            normed[pl.ds(at, rows), :] = (x * scale * gain[...]).astype(jnp.bfloat16)

    out[0] = jnp.dot(normed[...], weight[0], preferred_element_type=jnp.float32).astype(jnp.bfloat16)


def project(xs, gain, weight):
    n = len(xs)
    rows, depth = xs[0].shape
    width = weight.shape[2]
    tile = 256 if width % 256 == 0 else 128
    return pl.pallas_call(
        functools.partial(project_kernel, n),
        grid=(width // tile,),
        out_shape=jax.ShapeDtypeStruct((1, n * rows, width), jnp.bfloat16),
        in_specs=[VM] * n + [VM, pl.BlockSpec((1, depth, tile), lambda i: (0, 0, i))],
        out_specs=pl.BlockSpec((1, n * rows, tile), lambda i: (0, 0, i)),
        scratch_shapes=[pltpu.VMEM((n * rows, depth), jnp.bfloat16)],
        compiler_params=pltpu.CompilerParams(vmem_limit_bytes=VMEM_LIMIT),
        cost_estimate=pl.CostEstimate(
            flops=2 * n * rows * depth * width, bytes_accessed=2 * depth * width, transcendentals=0
        ),
        name="norm_project",
    )(*xs, gain, weight)


def mask_bias(block_mask, token_order, n, rows):
    tokens = n * rows
    per = block_mask.shape[1]
    count = tokens // BLOCK
    me = lax.axis_index("seq")
    order = jnp.arange(n, dtype=jnp.int32) ^ me
    token = (order[:, None] * rows + jnp.arange(rows, dtype=jnp.int32)[None, :]).reshape(tokens)
    block = jnp.arange(tokens, dtype=jnp.int32) // BLOCK
    own = jnp.sum(jnp.where(token_order[None, :] == token[:, None], block[None, :], 0), axis=1)
    hot = own[:, None] == jnp.arange(count, dtype=jnp.int32)[None, :]
    at = jnp.arange(count)
    full = jnp.where(
        at[:, None] // per == at[None, :] // per,
        jnp.tile(block_mask, (1, 1, count // per)).reshape(count, count),
        0,
    )
    hot = hot.astype(jnp.float32)
    seen = hot @ full.astype(jnp.float32) @ hot.T
    return jnp.where(seen > 0.5, 0.0, NEG)


def local(projected, stream_before, out_weight, proj_weight, norm_gain, block_mask, token_order):
    n = lax.axis_size("seq")
    rows = projected.shape[1]
    cuts = cut(projected, n)
    far = [swap(cuts[j], j) for j in range(n - 1, 1, -1)][::-1]
    blocks = [cuts[0], swap(cuts[1], 1)] + far
    bias = mask_bias(block_mask, token_order, n, rows)
    terms = attend(blocks, bias[2 * rows :], out_weight, 2, n)
    arrived = []
    for k in range(0, n - 2, 2):
        joined = terms[k].astype(jnp.float32) + swap(terms[k + 1], 1).astype(jnp.float32)
        arrived.append(swap(joined.astype(jnp.bfloat16), k + 2))
    near = attend(blocks, bias[: 2 * rows], out_weight, 0, 2)
    total = stream_before[0].astype(jnp.float32) + near[0].astype(jnp.float32) + swap(near[1], 1).astype(jnp.float32)
    for a in arrived:
        total = total + a.astype(jnp.float32)
    incoming = onward(total.astype(jnp.bfloat16))
    xs = [incoming, swap(incoming, 1)]
    for k in range(2, n, 2):
        other = swap(incoming, k)
        xs += [other, swap(other, 1)]
    following = project(xs, norm_gain, proj_weight)
    return (incoming[None], following)


def solution(mesh):
    placed = (
        P("segment", "seq", None),
        P("segment", "seq", None),
        P("segment", "seq", None),
        P("segment", None, "seq"),
        P("segment", None),
        P(),
        P(),
    )
    return jax.shard_map(
        local,
        mesh=mesh,
        in_specs=placed,
        out_specs=(P("segment", "seq", None), P("segment", None, "seq")),
        check_vma=False,
    )
```

time: 113 us -> 58.8 us (0.52)
  waiting for transfers between devices: 60.9 us -> 30.3 us
  between operations: 14.2 us -> 0.71 us
  local copies, waits for them, and re-layouts: 18.2 us -> 4.92 us
  Pallas kernels: 0 us -> 11.6 us
  matrix products: 11.2 us -> 1.04 us
  starting transfers between devices: 5.8 us -> 8.72 us
    reduce_scatter x1 -> x0, waiting for transfers between devices: 25.9 us -> none  [local(): lax.psum_scatter(jnp.dot(placed, out_weight[0], preferred_element_type=jn...]
    ppermute x1 -> x10, waiting for transfers between devices: 9.28 us -> 30.3 us  [the longest x9 21.3 us: swap(): return lax.ppermute(x, 'seq', [(i, i ^ by) for i in range(size)])]
    all_gather x1 -> x0, waiting for transfers between devices: 14.2 us -> none  [local(): lax.all_gather(normed, 'seq', axis=0, tiled=True)]
    pallas_call x0 -> x4, Pallas kernels: none -> 11.6 us  [the longest x1 6.92 us: project(): pl.pallas_call(functools.partial(project_kernel, n), grid=(width // tile,...]
    all_to_all x1 -> x0, waiting for transfers between devices: 11.4 us -> none  [local(): lax.all_to_all(projected[0], 'seq', split_axis=1, concat_axis=0, tiled=True)]
    dot_general x4 -> x1, matrix products: 10.8 us -> 1.04 us  [mask_bias(): seen = hot @ full.astype(jnp.float32) @ hot.T]
    ppermute x1 -> x10, starting transfers between devices: 1.52 us -> 8.72 us  [the longest x9 6.98 us: swap(): return lax.ppermute(x, 'seq', [(i, i ^ by) for i in range(size)])]
    scatter x1 -> x0, local copies, waits for them, and re-layouts: 6.97 us -> none  [local(): placed = jnp.zeros((all_tokens, local_heads, DH), jnp.bfloat16).at[token_...]
  transfers between devices with their start and end apart: 4 -> 10, of which waited for: 4 -> 6; matrix products, arithmetic and copies ran while one was open for 0% -> 4% of each run, Pallas kernels for 0% -> 2%
where the time goes in v1:
time: 58.8 us; the launch traced here: 58.4 us
  waiting for transfers between devices  30.3 us (52%)
  Pallas kernels  11.6 us (20%)
  starting transfers between devices  8.72 us (15%)
  local copies, waits for them, and re-layouts  4.92 us (8%)
  other arithmetic  1.14 us (2%)
  matrix products  1.04 us (2%)
  between operations  0.71 us (1%)
    ppermute x9, waiting for transfers between devices, swap(): return lax.ppermute(x, 'seq', [(i, i ^ by) for i in range(size)])  21.3 us
    ppermute x1, waiting for transfers between devices, onward(): lax.ppermute(x, 'segment', [(i, (i + 1) % size) for i in range(size)])  8.97 us
    ppermute x9, starting transfers between devices, swap(): return lax.ppermute(x, 'seq', [(i, i ^ by) for i in range(size)])  6.98 us
    pallas_call x1, Pallas kernels, project(): pl.pallas_call(functools.partial(project_kernel, n), grid=(width // tile,...  6.92 us
    unnamed x11, local copies, waits for them, and re-layouts  4.82 us
    pallas_call x2, Pallas kernels, attend(): pl.pallas_call(functools.partial(attend_kernel, n, lo, hi), out_shape=[ja...  2.51 us
    pallas_call x1, Pallas kernels, cut(): pl.pallas_call(functools.partial(cut_kernel, n), out_shape=[jax.ShapeDtyp...  2.18 us
    ppermute x1, starting transfers between devices, onward(): lax.ppermute(x, 'segment', [(i, (i + 1) % size) for i in range(size)])  1.75 us
  transfers between devices with their start and end apart: 10, of which 6 were waited for; matrix products, arithmetic and copies ran while one was open for 4% of the time, Pallas kernels for 2%

profile of v1, /device:TPU:0, one launch (start us, length us, event | category | flops | bytes accessed | tf_op | source)
XLA Modules:
  0.0 58.4 jit_solution(4741653293371592267)
XLA Ops:
  0.6 2.2 %cut_slices.1 = (bf16[64,1536]{1,0:T(8,128)(2,1)}, bf16[64,1536]{1,0:T(8,128)(2,1)}, bf16[64,1536]{1,0:T(8,128)(2,1)}, bf16[64,1536]{1,0:T(8,128)(2,1)}) custom-call(bf16[1,64,6144]{2,1,0:T(8,128)(2,1)} %src.1), custom_call_target="tpu_custom_call" | custom-call | tf_op jit(solution)/shard_map/cut_slices/pallas_call | solution.py:48
  2.8 0.5 collective-permute-start
  3.4 2.6 %collective-permute-start.1 = (bf16[64,1536]{1,0:T(8,128)(2,1)}, bf16[64,1536]{1,0:T(8,128)(2,1)S(1)}, u32[]{:S(2)}, u32[]{:S(2)}) collective-permute-start(bf16[64,1536]{1,0:T(8,128)(2,1)} %get-tuple-element.12), channel_id=1, source_target_pairs={{0,2},{1,3},{2,0},{3,1},{4,6},{5,7},{6,4},{7,5},{8,10},{9,11},{10,... | collective-permute-start | bytes 589832 | tf_op jit(solution)/shard_map/ppermute | solution.py:23
  6.2 0.9 %select_reduce_fusion = s32[256]{0:T(256)S(1)} fusion(s32[256]{0:T(256)S(1)} %and_select_fusion.1, s32[256]{0:T(256)} %param.13, s32[256]{0:T(256)S(1)} %add.52), kind=kLoop, calls=%fused_computation.8 | loop fusion | flops 196352 | bytes 4096 | tf_op jit(solution)/shard_map/reduce_sum | solution.py:145
  7.0 1.0 %fusion = f32[256,256]{1,0:T(8,128)S(1)} fusion(s32[256]{0:T(256)S(1)} %select_reduce_fusion, s32[1,2,2]{2,1,0:T(2,128)} %param.12, s32[2]{0:T(128)S(1)} %and_select_fusion), kind=kOutput, calls=%fused_computation.1 | convolution fusion | flops 396300 | bytes 263192 | tf_op jit(solution)/shard_map/dot_general | solution.py:154
  8.1 3.8 %collective-permute-done.1.refs_2_ = bf16[64,1536]{1,0:T(8,128)(2,1)S(1)} collective-permute-done((bf16[64,1536]{1,0:T(8,128)(2,1)}, bf16[64,1536]{1,0:T(8,128)(2,1)S(1)}, u32[]{:S(2)}, u32[]{:S(2)}) %collective-permute-start.1) | collective-permute-done | bytes 196640 | tf_op jit(solution)/shard_map/ppermute | solution.py:23
  11.9 3.7 %collective-permute-done.2.refs_3_ = bf16[64,1536]{1,0:T(8,128)(2,1)S(1)} collective-permute-done((bf16[64,1536]{1,0:T(8,128)(2,1)}, bf16[64,1536]{1,0:T(8,128)(2,1)S(1)}, u32[]{:S(2)}, u32[]{:S(2)}) %collective-permute-start.2) | collective-permute-done | bytes 196640 | tf_op jit(solution)/shard_map/ppermute | solution.py:23
  15.6 1.6 %copy-done = bf16[1,512,2048]{2,1,0:T(8,128)(2,1)S(1)} copy-done((bf16[1,512,2048]{2,1,0:T(8,128)(2,1)S(1)}, bf16[1,512,2048]{2,1,0:T(8,128)(2,1)}, u32[]{:S(2)}) %copy-start) | copy-done | bytes 2097176
  17.2 0.9 %copy-done.2 = bf16[64,1536]{1,0:T(8,128)(2,1)S(1)} copy-done((bf16[64,1536]{1,0:T(8,128)(2,1)S(1)}, bf16[64,1536]{1,0:T(8,128)(2,1)}, u32[]{:S(2)}) %copy-start.2) | copy-done | bytes 196632
  18.1 1.3 %attend_project.3 = (bf16[64,2048]{1,0:T(8,128)(2,1)S(1)}, bf16[64,2048]{1,0:T(8,128)(2,1)S(1)}) custom-call(bf16[64,1536]{1,0:T(8,128)(2,1)S(1)} %copy-done.2, bf16[64,1536]{1,0:T(8,128)(2,1)S(1)} %collective-permute-done.refs_1_, bf16[64,1536]{1,0:T(8,128)(2,1)S(1)} %collective-permute-done.1.refs_2_, bf16[64,1536]{1,0:T(8,128)(2,1)S(1)} %collective-permute-done.2.refs_3_, ...), custom_call_target="tpu_custom_call" | custom-call | flops 335544320 | bytes 2097152 | tf_op jit(solution)/shard_map/attend_project/pallas_call | solution.py:86
  19.4 0.2 collective-permute-start.4
  19.6 1.6 %copy-done.1 = bf16[1,512,2048]{2,1,0:T(8,128)(2,1)S(1)} copy-done((bf16[1,512,2048]{2,1,0:T(8,128)(2,1)S(1)}, bf16[1,512,2048]{2,1,0:T(8,128)(2,1)}, u32[]{:S(2)}) %copy-start.1) | copy-done | bytes 2097176
  21.2 1.3 %attend_project.2 = (bf16[64,2048]{1,0:T(8,128)(2,1)S(1)}, bf16[64,2048]{1,0:T(8,128)(2,1)S(1)}) custom-call(bf16[64,1536]{1,0:T(8,128)(2,1)S(1)} %copy-done.2, bf16[64,1536]{1,0:T(8,128)(2,1)S(1)} %collective-permute-done.refs_1_, bf16[64,1536]{1,0:T(8,128)(2,1)S(1)} %collective-permute-done.1.refs_2_, bf16[64,1536]{1,0:T(8,128)(2,1)S(1)} %collective-permute-done.2.refs_3_, ...), custom_call_target="tpu_custom_call" | custom-call | flops 335544320 | bytes 2097152 | tf_op jit(solution)/shard_map/attend_project/pallas_call | solution.py:86
  22.4 0.5 collective-permute-start.3
  23.0 1.6 %collective-permute-start.5 = (bf16[64,2048]{1,0:T(8,128)(2,1)S(1)}, bf16[64,2048]{1,0:T(8,128)(2,1)S(1)}, u32[]{:S(2)}, u32[]{:S(2)}) collective-permute-start(bf16[64,2048]{1,0:T(8,128)(2,1)S(1)} %add_convert_fusion), channel_id=1, source_target_pairs={{0,2},{1,3},{2,0},{3,1},{4,6},{5,7},{6,4},{7,5},{8,10},{9,11},{10,... | collective-permute-start | bytes 786440 | tf_op jit(solution)/shard_map/ppermute | solution.py:23
  24.6 6.8 %collective-permute-done.5 = bf16[64,2048]{1,0:T(8,128)(2,1)S(1)} collective-permute-done((bf16[64,2048]{1,0:T(8,128)(2,1)S(1)}, bf16[64,2048]{1,0:T(8,128)(2,1)S(1)}, u32[]{:S(2)}, u32[]{:S(2)}) %collective-permute-start.5) | collective-permute-done | bytes 262176 | tf_op jit(solution)/shard_map/ppermute | solution.py:23
  31.3 0.1 fusion.5
  31.5 1.7 %collective-permute-start.6 = (bf16[64,2048]{1,0:T(8,128)(2,1)S(1)}, bf16[64,2048]{1,0:T(8,128)(2,1)S(1)}, u32[]{:S(2)}, u32[]{:S(2)}) collective-permute-start(bf16[64,2048]{1,0:T(8,128)(2,1)S(1)} %fusion.5), channel_id=1, source_target_pairs={{0,4},{4,8},{8,12},{12,16},{16,20},{20,24},{24,28},{28,0},{1,5},{5... | collective-permute-start | bytes 786440 | tf_op jit(solution)/shard_map/ppermute | solution.py:28
  33.2 9.0 %collective-permute-done.6.refs_0_ = bf16[64,2048]{1,0:T(8,128)(2,1)S(1)} collective-permute-done((bf16[64,2048]{1,0:T(8,128)(2,1)S(1)}, bf16[64,2048]{1,0:T(8,128)(2,1)S(1)}, u32[]{:S(2)}, u32[]{:S(2)}) %collective-permute-start.6) | collective-permute-done | bytes 262176 | tf_op jit(solution)/shard_map/ppermute | solution.py:28
  42.2 1.5 %collective-permute-start.8 = (bf16[64,2048]{1,0:T(8,128)(2,1)S(1)}, bf16[64,2048]{1,0:T(8,128)(2,1)S(1)}, u32[]{:S(2)}, u32[]{:S(2)}) collective-permute-start(bf16[64,2048]{1,0:T(8,128)(2,1)S(1)} %collective-permute-done.6.refs_0_), channel_id=1, source_target_pairs={{0,2},{1,3},{2,0},{3,1},{4,6},{5,7},{6,4},{7,5},{8,10},{9,11},{10,... | collective-permute-start | bytes 786440 | tf_op jit(solution)/shard_map/ppermute | solution.py:23
  43.7 5.5 %collective-permute-done.8.refs_2_ = bf16[64,2048]{1,0:T(8,128)(2,1)S(1)} collective-permute-done((bf16[64,2048]{1,0:T(8,128)(2,1)S(1)}, bf16[64,2048]{1,0:T(8,128)(2,1)S(1)}, u32[]{:S(2)}, u32[]{:S(2)}) %collective-permute-start.8) | collective-permute-done | bytes 262176 | tf_op jit(solution)/shard_map/ppermute | solution.py:23
  49.3 1.5 %collective-permute-done.9.refs_3_ = bf16[64,2048]{1,0:T(8,128)(2,1)S(1)} collective-permute-done((bf16[64,2048]{1,0:T(8,128)(2,1)S(1)}, bf16[64,2048]{1,0:T(8,128)(2,1)S(1)}, u32[]{:S(2)}, u32[]{:S(2)}) %collective-permute-start.9) | collective-permute-done | bytes 262176 | tf_op jit(solution)/shard_map/ppermute | solution.py:23
  50.8 6.9 %norm_project.1 = bf16[1,256,1536]{2,1,0:T(8,128)(2,1)} custom-call(bf16[64,2048]{1,0:T(8,128)(2,1)S(1)} %collective-permute-done.6.refs_0_, bf16[64,2048]{1,0:T(8,128)(2,1)S(1)} %collective-permute-done.7.refs_1_, bf16[64,2048]{1,0:T(8,128)(2,1)S(1)} %collective-permute-done.8.refs_2_, bf16[64,2048]{1,0:T(8,128)(2,1)S(1)} %collective-permute-done.9.refs_3_, ...), custom_call_target="tpu_custom_call" | custom-call | flops 1610612736 | bytes 6291456 | tf_op jit(solution)/shard_map/norm_project/pallas_call | solution.py:122
  57.7 0.7 %copy.10 = bf16[1,64,2048]{2,1,0:T(8,128)(2,1)} copy(bf16[1,64,2048]{2,1,0:T(8,128)(2,1)S(1)} %bitcast.10) | data formatting | bytes 524288
  (21 shorter events, 0.4 us)
Async XLA Ops:
  0.6 30.7 %copy-start.4 = (bf16[1,64,2048]{2,1,0:T(8,128)(2,1)S(1)}, bf16[1,64,2048]{2,1,0:T(8,128)(2,1)}, u32[]{:S(2)}) copy-start(bf16[1,64,2048]{2,1,0:T(8,128)(2,1)} %param.8) | copy-start | bytes 786436
  0.6 50.2 %copy-start.3 = (f32[1,2048]{1,0:T(1,128)S(1)}, f32[1,2048]{1,0:T(1,128)}, u32[]{:S(2)}) copy-start(f32[1,2048]{1,0:T(1,128)} %refs_4_.1) | copy-start | bytes 24580
  2.8 5.3 %collective-permute-start = (bf16[64,1536]{1,0:T(8,128)(2,1)}, bf16[64,1536]{1,0:T(8,128)(2,1)S(1)}, u32[]{:S(2)}, u32[]{:S(2)}) collective-permute-start(bf16[64,1536]{1,0:T(8,128)(2,1)} %get-tuple-element.11), channel_id=1, source_target_pairs={{0,1},{1,0},{2,3},{3,2},{4,5},{5,4},{6,7},{7,6},{8,9},{9,8},{10,11... | collective-permute-start | bytes 589832 | tf_op jit(solution)/shard_map/ppermute | solution.py:23
  3.4 8.6 %collective-permute-start.1 = (bf16[64,1536]{1,0:T(8,128)(2,1)}, bf16[64,1536]{1,0:T(8,128)(2,1)S(1)}, u32[]{:S(2)}, u32[]{:S(2)}) collective-permute-start(bf16[64,1536]{1,0:T(8,128)(2,1)} %get-tuple-element.12), channel_id=1, source_target_pairs={{0,2},{1,3},{2,0},{3,1},{4,6},{5,7},{6,4},{7,5},{8,10},{9,11},{10,... | collective-permute-start | bytes 589832 | tf_op jit(solution)/shard_map/ppermute | solution.py:23
  6.0 9.7 %collective-permute-start.2 = (bf16[64,1536]{1,0:T(8,128)(2,1)}, bf16[64,1536]{1,0:T(8,128)(2,1)S(1)}, u32[]{:S(2)}, u32[]{:S(2)}) collective-permute-start(bf16[64,1536]{1,0:T(8,128)(2,1)} %get-tuple-element.13), channel_id=1, source_target_pairs={{0,3},{1,2},{2,1},{3,0},{4,7},{5,6},{6,5},{7,4},{8,11},{9,10},{10,... | collective-permute-start | bytes 589832 | tf_op jit(solution)/shard_map/ppermute | solution.py:23
  15.6 1.6 %copy-start = (bf16[1,512,2048]{2,1,0:T(8,128)(2,1)S(1)}, bf16[1,512,2048]{2,1,0:T(8,128)(2,1)}, u32[]{:S(2)}) copy-start(bf16[1,512,2048]{2,1,0:T(8,128)(2,1)} %refs_5_.4) | copy-start | bytes 6291460
  17.2 0.9 %copy-start.2 = (bf16[64,1536]{1,0:T(8,128)(2,1)S(1)}, bf16[64,1536]{1,0:T(8,128)(2,1)}, u32[]{:S(2)}) copy-start(bf16[64,1536]{1,0:T(8,128)(2,1)} %get-tuple-element.10.refs_0_) | copy-start | bytes 589828
  19.4 3.5 %collective-permute-start.4 = (bf16[64,2048]{1,0:T(8,128)(2,1)S(1)}, bf16[64,2048]{1,0:T(8,128)(2,1)S(1)}, u32[]{:S(2)}, u32[]{:S(2)}) collective-permute-start(bf16[64,2048]{1,0:T(8,128)(2,1)S(1)} %get-tuple-element.17), channel_id=1, source_target_pairs={{0,1},{1,0},{2,3},{3,2},{4,5},{5,4},{6,7},{7,6},{8,9},{9,8},{10,11... | collective-permute-start | bytes 786440 | tf_op jit(solution)/shard_map/ppermute | solution.py:23
  19.6 1.6 %copy-start.1 = (bf16[1,512,2048]{2,1,0:T(8,128)(2,1)S(1)}, bf16[1,512,2048]{2,1,0:T(8,128)(2,1)}, u32[]{:S(2)}) copy-start(bf16[1,512,2048]{2,1,0:T(8,128)(2,1)} %refs_5_.4) | copy-start | bytes 6291460
  22.4 2.2 %collective-permute-start.3 = (bf16[64,2048]{1,0:T(8,128)(2,1)S(1)}, bf16[64,2048]{1,0:T(8,128)(2,1)S(1)}, u32[]{:S(2)}, u32[]{:S(2)}) collective-permute-start(bf16[64,2048]{1,0:T(8,128)(2,1)S(1)} %get-tuple-element.15), channel_id=1, source_target_pairs={{0,1},{1,0},{2,3},{3,2},{4,5},{5,4},{6,7},{7,6},{8,9},{9,8},{10,11... | collective-permute-start | bytes 786440 | tf_op jit(solution)/shard_map/ppermute | solution.py:23
  23.0 8.4 %collective-permute-start.5 = (bf16[64,2048]{1,0:T(8,128)(2,1)S(1)}, bf16[64,2048]{1,0:T(8,128)(2,1)S(1)}, u32[]{:S(2)}, u32[]{:S(2)}) collective-permute-start(bf16[64,2048]{1,0:T(8,128)(2,1)S(1)} %add_convert_fusion), channel_id=1, source_target_pairs={{0,2},{1,3},{2,0},{3,1},{4,6},{5,7},{6,4},{7,5},{8,10},{9,11},{10,... | collective-permute-start | bytes 786440 | tf_op jit(solution)/shard_map/ppermute | solution.py:23
  31.5 10.7 %collective-permute-start.6 = (bf16[64,2048]{1,0:T(8,128)(2,1)S(1)}, bf16[64,2048]{1,0:T(8,128)(2,1)S(1)}, u32[]{:S(2)}, u32[]{:S(2)}) collective-permute-start(bf16[64,2048]{1,0:T(8,128)(2,1)S(1)} %fusion.5), channel_id=1, source_target_pairs={{0,4},{4,8},{8,12},{12,16},{16,20},{20,24},{24,28},{28,0},{1,5},{5... | collective-permute-start | bytes 786440 | tf_op jit(solution)/shard_map/ppermute | solution.py:28
  42.2 7.1 %collective-permute-start.8 = (bf16[64,2048]{1,0:T(8,128)(2,1)S(1)}, bf16[64,2048]{1,0:T(8,128)(2,1)S(1)}, u32[]{:S(2)}, u32[]{:S(2)}) collective-permute-start(bf16[64,2048]{1,0:T(8,128)(2,1)S(1)} %collective-permute-done.6.refs_0_), channel_id=1, source_target_pairs={{0,2},{1,3},{2,0},{3,1},{4,6},{5,7},{6,4},{7,5},{8,10},{9,11},{10,... | collective-permute-start | bytes 786440 | tf_op jit(solution)/shard_map/ppermute | solution.py:23
  43.7 5.6 %collective-permute-start.7 = (bf16[64,2048]{1,0:T(8,128)(2,1)S(1)}, bf16[64,2048]{1,0:T(8,128)(2,1)S(1)}, u32[]{:S(2)}, u32[]{:S(2)}) collective-permute-start(bf16[64,2048]{1,0:T(8,128)(2,1)S(1)} %collective-permute-done.6.refs_0_), channel_id=1, source_target_pairs={{0,1},{1,0},{2,3},{3,2},{4,5},{5,4},{6,7},{7,6},{8,9},{9,8},{10,11... | collective-permute-start | bytes 786440 | tf_op jit(solution)/shard_map/ppermute | solution.py:23
  49.3 1.5 %collective-permute-start.9 = (bf16[64,2048]{1,0:T(8,128)(2,1)S(1)}, bf16[64,2048]{1,0:T(8,128)(2,1)S(1)}, u32[]{:S(2)}, u32[]{:S(2)}) collective-permute-start(bf16[64,2048]{1,0:T(8,128)(2,1)S(1)} %collective-permute-done.8.refs_2_), channel_id=1, source_target_pairs={{0,1},{1,0},{2,3},{3,2},{4,5},{5,4},{6,7},{7,6},{8,9},{9,8},{10,11... | collective-permute-start | bytes 786440 | tf_op jit(solution)/shard_map/ppermute | solution.py:23

commit v2 on v1

--- a/solution.py
+++ b/solution.py
@@ -15,7 +15,7 @@
 VMEM_LIMIT = 48 * 1024 * 1024
 
 VM = pl.BlockSpec(memory_space=pltpu.VMEM)
-ANY = pl.BlockSpec(memory_space=pl.ANY)
+ANY = pl.BlockSpec(memory_space=pltpu.HBM)
 
 
 def swap(x, by):
@@ -28,31 +28,61 @@
     return lax.ppermute(x, "segment", [(i, (i + 1) % size) for i in range(size)])
 
 
-def cut_kernel(n, src, *refs):
-    outs, sems = refs[:n], refs[n]
+def cut_kernel(js, src, *refs):
+    outs, sems = refs[: len(js)], refs[len(js)]
     width = outs[0].shape[1]
     me = lax.axis_index("seq")
     copies = []
-    for j in range(n - 1, -1, -1):
-        at = pl.multiple_of((me ^ j) * width, 128)
-        copies.append(pltpu.make_async_copy(src.at[0, :, pl.ds(at, width)], outs[j], sems.at[j]))
+    for at, j in enumerate(js):
+        first = pl.multiple_of((me ^ j) * width, 128)
+        copies.append(pltpu.make_async_copy(src.at[0, :, pl.ds(first, width)], outs[at], sems.at[at]))
     for c in copies:
         c.start()
     for c in copies:
         c.wait()
 
 
-def cut(projected, n):
+def cut(projected, n, js):
     _, rows, columns = projected.shape
     width = columns // n
     return pl.pallas_call(
-        functools.partial(cut_kernel, n),
-        out_shape=[jax.ShapeDtypeStruct((rows, width), projected.dtype)] * n,
+        functools.partial(cut_kernel, js),
+        out_shape=[jax.ShapeDtypeStruct((rows, width), projected.dtype)] * len(js),
         in_specs=[ANY],
-        out_specs=[VM] * n,
-        scratch_shapes=[pltpu.SemaphoreType.DMA((n,))],
+        out_specs=[VM] * len(js),
+        scratch_shapes=[pltpu.SemaphoreType.DMA((len(js),))],
         name="cut_slices",
     )(projected)
+
+
+def load_kernel(pieces, *refs):
+    count = len(pieces)
+    ins, outs, sems = refs[:count], refs[count : 2 * count], refs[2 * count]
+    copies = []
+    for i, many in enumerate(pieces):
+        step = ins[i].shape[1] // many
+        for p in range(many):
+            part = (slice(None), pl.ds(p * step, step))
+            copies.append(pltpu.make_async_copy(ins[i].at[part], outs[i].at[part], sems.at[len(copies)]))
+    for c in copies:
+        c.start()
+    for c in copies:
+        c.wait()
+
+
+def load(arrays, pieces):
+    return pl.pallas_call(
+        functools.partial(load_kernel, pieces),
+        out_shape=[jax.ShapeDtypeStruct(a.shape, a.dtype) for a in arrays],
+        in_specs=[ANY] * len(arrays),
+        out_specs=[VM] * len(arrays),
+        scratch_shapes=[pltpu.SemaphoreType.DMA((sum(pieces),))],
+        compiler_params=pltpu.CompilerParams(vmem_limit_bytes=VMEM_LIMIT),
+        cost_estimate=pl.CostEstimate(
+            flops=0, bytes_accessed=2 * sum(a.size * a.dtype.itemsize for a in arrays), transcendentals=0
+        ),
+        name="load_weights",
+    )(*arrays)
 
 
 def attend_kernel(n, lo, hi, *refs):
@@ -77,7 +107,8 @@
         outs[j][...] = term[j * rows : (j + 1) * rows]
 
 
-def attend(blocks, bias, weight, lo, hi):
+def attend(blocks, bias, weight, lo):
+    hi = lo + 1
     n = len(blocks)
     rows, width = blocks[0].shape
     depth = weight.shape[2]
@@ -98,20 +129,25 @@
     )(*blocks, bias, weight)
 
 
-def project_kernel(n, *refs):
-    xs, gain, weight, out, normed = refs[:n], refs[n], refs[n + 1], refs[n + 2], refs[n + 3]
+def project_kernel(n, tile, xs, gain, weight, kept, out, normed, made, sems):
     rows = xs[0].shape[0]
+    width = weight.shape[2]
     me = lax.axis_index("seq")
-
-    @pl.when(pl.program_id(0) == 0)
-    def _():
-        for j in range(n):
-            x = xs[j][...].astype(jnp.float32)
-            scale = lax.rsqrt(jnp.mean(x * x, axis=-1, keepdims=True) + 1e-06)
-            at = pl.multiple_of((me ^ j) * rows, rows)
-            normed[pl.ds(at, rows), :] = (x * scale * gain[...]).astype(jnp.bfloat16)
-
-    out[0] = jnp.dot(normed[...], weight[0], preferred_element_type=jnp.float32).astype(jnp.bfloat16)
+    keep = pltpu.make_async_copy(xs[0], kept.at[0], sems.at[0])
+    keep.start()
+    for j in range(n):
+        x = xs[j][...].astype(jnp.float32)
+        scale = lax.rsqrt(jnp.mean(x * x, axis=-1, keepdims=True) + 1e-06)
+        at = pl.multiple_of((me ^ j) * rows, rows)
+        normed[pl.ds(at, rows), :] = (x * scale * gain[...]).astype(jnp.bfloat16)
+    copies = [keep]
+    for i in range(width // tile):
+        part = pl.ds(i * tile, tile)
+        made[:, part] = jnp.dot(normed[...], weight[0, :, part], preferred_element_type=jnp.float32).astype(jnp.bfloat16)
+        copies.append(pltpu.make_async_copy(made.at[:, part], out.at[0, :, part], sems.at[1 + i]))
+        copies[-1].start()
+    for c in copies:
+        c.wait()
 
 
 def project(xs, gain, weight):
@@ -120,18 +156,28 @@
     width = weight.shape[2]
     tile = 256 if width % 256 == 0 else 128
     return pl.pallas_call(
-        functools.partial(project_kernel, n),
-        grid=(width // tile,),
-        out_shape=jax.ShapeDtypeStruct((1, n * rows, width), jnp.bfloat16),
-        in_specs=[VM] * n + [VM, pl.BlockSpec((1, depth, tile), lambda i: (0, 0, i))],
-        out_specs=pl.BlockSpec((1, n * rows, tile), lambda i: (0, 0, i)),
-        scratch_shapes=[pltpu.VMEM((n * rows, depth), jnp.bfloat16)],
+        functools.partial(project_whole, n, tile),
+        out_shape=[
+            jax.ShapeDtypeStruct((1, rows, depth), jnp.bfloat16),
+            jax.ShapeDtypeStruct((1, n * rows, width), jnp.bfloat16),
+        ],
+        in_specs=[VM] * (n + 2),
+        out_specs=[ANY, ANY],
+        scratch_shapes=[
+            pltpu.VMEM((n * rows, depth), jnp.bfloat16),
+            pltpu.VMEM((n * rows, width), jnp.bfloat16),
+            pltpu.SemaphoreType.DMA((1 + width // tile,)),
+        ],
         compiler_params=pltpu.CompilerParams(vmem_limit_bytes=VMEM_LIMIT),
         cost_estimate=pl.CostEstimate(
             flops=2 * n * rows * depth * width, bytes_accessed=2 * depth * width, transcendentals=0
         ),
         name="norm_project",
     )(*xs, gain, weight)
+
+
+def project_whole(n, tile, *refs):
+    project_kernel(n, tile, refs[:n], *refs[n:])
 
 
 def mask_bias(block_mask, token_order, n, rows):
@@ -158,17 +204,23 @@
 def local(projected, stream_before, out_weight, proj_weight, norm_gain, block_mask, token_order):
     n = lax.axis_size("seq")
     rows = projected.shape[1]
-    cuts = cut(projected, n)
-    far = [swap(cuts[j], j) for j in range(n - 1, 1, -1)][::-1]
-    blocks = [cuts[0], swap(cuts[1], 1)] + far
+    far_cut = cut(projected, n, tuple(range(2, n)))
+    far = [swap(far_cut[j - 2], j) for j in range(2, n)]
+    near_cut = cut(projected, n, (0, 1))
+    blocks = [near_cut[0], swap(near_cut[1], 1)] + far
     bias = mask_bias(block_mask, token_order, n, rows)
-    terms = attend(blocks, bias[2 * rows :], out_weight, 2, n)
-    arrived = []
-    for k in range(0, n - 2, 2):
-        joined = terms[k].astype(jnp.float32) + swap(terms[k + 1], 1).astype(jnp.float32)
-        arrived.append(swap(joined.astype(jnp.bfloat16), k + 2))
-    near = attend(blocks, bias[: 2 * rows], out_weight, 0, 2)
-    total = stream_before[0].astype(jnp.float32) + near[0].astype(jnp.float32) + swap(near[1], 1).astype(jnp.float32)
+    stream, out_weight, proj_weight = load((stream_before, out_weight, proj_weight), (1, 4, 8))
+    sums = []
+    for k in range(2, n, 2):
+        (crossing,) = attend(blocks, bias[(k + 1) * rows : (k + 2) * rows], out_weight, k + 1)
+        (staying,) = attend(blocks, bias[k * rows : (k + 1) * rows], out_weight, k)
+        joined = staying.astype(jnp.float32) + swap(crossing, 1).astype(jnp.float32)
+        sums.append(joined.astype(jnp.bfloat16))
+    arrived = [swap(x, 2 * k + 2) for k, x in enumerate(sums)]
+    sums, near_bias = lax.optimization_barrier((sums, bias[: 2 * rows]))
+    (crossing,) = attend(blocks, near_bias[rows:], out_weight, 1)
+    (staying,) = attend(blocks, near_bias[:rows], out_weight, 0)
+    total = stream[0].astype(jnp.float32) + staying.astype(jnp.float32) + swap(crossing, 1).astype(jnp.float32)
     for a in arrived:
         total = total + a.astype(jnp.float32)
     incoming = onward(total.astype(jnp.bfloat16))
@@ -176,8 +228,8 @@
     for k in range(2, n, 2):
         other = swap(incoming, k)
         xs += [other, swap(other, 1)]
-    following = project(xs, norm_gain, proj_weight)
-    return (incoming[None], following)
+    kept, following = project(xs, norm_gain, proj_weight)
+    return (kept, following)
 
 
 def solution(mesh):

time: 58.8 us -> 55.8 us (0.949)
  waiting for transfers between devices: 30.3 us -> 18.9 us
  Pallas kernels: 11.6 us -> 22.3 us
  local copies, waits for them, and re-layouts: 4.92 us -> 2.66 us
    ppermute x9, waiting for transfers between devices: 21.3 us -> 10 us  [swap(): return lax.ppermute(x, 'seq', [(i, i ^ by) for i in range(size)])]
    pallas_call x2 -> x4, Pallas kernels: 9.11 us -> 15.1 us  [the longest x1 5.78 us: project(): pl.pallas_call(functools.partial(project_whole, n, tile), out_shape=[jax....]
    pallas_call x2 -> x4, Pallas kernels: 2.51 us -> 7.25 us  [attend(): pl.pallas_call(functools.partial(attend_kernel, n, lo, hi), out_shape=[ja...]
    unnamed x11 -> x8, local copies, waits for them, and re-layouts: 4.82 us -> 2.55 us
  transfers between devices with their start and end apart: 10 -> 10, of which waited for: 6 -> 4; matrix products, arithmetic and copies ran while one was open for 4% -> 4% of each run, Pallas kernels for 2% -> 23%
where the time goes in v2:
time: 55.8 us; the launch traced here: 55.5 us
  Pallas kernels  22.3 us (40%)
  waiting for transfers between devices  18.9 us (34%)
  starting transfers between devices  8.67 us (16%)
  local copies, waits for them, and re-layouts  2.66 us (5%)
  other arithmetic  1.14 us (2%)
  matrix products  1.04 us (2%)
  between operations  0.77 us (1%)
    ppermute x9, waiting for transfers between devices, swap(): return lax.ppermute(x, 'seq', [(i, i ^ by) for i in range(size)])  10 us
    ppermute x1, waiting for transfers between devices, onward(): lax.ppermute(x, 'segment', [(i, (i + 1) % size) for i in range(size)])  8.91 us
    pallas_call x4, Pallas kernels, attend(): pl.pallas_call(functools.partial(attend_kernel, n, lo, hi), out_shape=[ja...  7.25 us
    ppermute x9, starting transfers between devices, swap(): return lax.ppermute(x, 'seq', [(i, i ^ by) for i in range(size)])  6.98 us
    pallas_call x1, Pallas kernels, project(): pl.pallas_call(functools.partial(project_whole, n, tile), out_shape=[jax....  5.78 us
    pallas_call x1, Pallas kernels, load(): pl.pallas_call(functools.partial(load_kernel, pieces), out_shape=[jax.Sha...  5.73 us
    pallas_call x2, Pallas kernels, cut(): pl.pallas_call(functools.partial(cut_kernel, js), out_shape=[jax.ShapeDty...  3.59 us
    unnamed x8, local copies, waits for them, and re-layouts  2.55 us
  transfers between devices with their start and end apart: 10, of which 4 were waited for; matrix products, arithmetic and copies ran while one was open for 4% of the time, Pallas kernels for 23%

profile of v2, /device:TPU:0, one launch (start us, length us, event | category | flops | bytes accessed | tf_op | source)
XLA Modules:
  0.0 55.5 jit_solution(14087561272819203979)
XLA Ops:
  0.6 1.8 %cut_slices.2 = (bf16[64,1536]{1,0:T(8,128)(2,1)}, bf16[64,1536]{1,0:T(8,128)(2,1)}) custom-call(bf16[1,64,6144]{2,1,0:T(8,128)(2,1)} %src.3), custom_call_target="tpu_custom_call" | custom-call | tf_op jit(solution)/shard_map/cut_slices/pallas_call | solution.py:48
  2.4 0.5 collective-permute-start
  3.0 1.8 %cut_slices.3 = (bf16[64,1536]{1,0:T(8,128)(2,1)}, bf16[64,1536]{1,0:T(8,128)(2,1)}) custom-call(bf16[1,64,6144]{2,1,0:T(8,128)(2,1)} %src.3), custom_call_target="tpu_custom_call" | custom-call | tf_op jit(solution)/shard_map/cut_slices/pallas_call | solution.py:48
  4.8 2.6 %collective-permute-start.1 = (bf16[64,1536]{1,0:T(8,128)(2,1)}, bf16[64,1536]{1,0:T(8,128)(2,1)S(1)}, u32[]{:S(2)}, u32[]{:S(2)}) collective-permute-start(bf16[64,1536]{1,0:T(8,128)(2,1)} %get-tuple-element.13), channel_id=1, source_target_pairs={{0,2},{1,3},{2,0},{3,1},{4,6},{5,7},{6,4},{7,5},{8,10},{9,11},{10,... | collective-permute-start | bytes 589832 | tf_op jit(solution)/shard_map/ppermute | solution.py:23
  7.4 0.2 collective-permute-start.2
  7.7 0.9 %select_reduce_fusion = s32[256]{0:T(256)S(1)} fusion(s32[256]{0:T(256)S(1)} %and_select_fusion.1, s32[256]{0:T(256)} %param.13, s32[256]{0:T(256)S(1)} %add.52), kind=kLoop, calls=%fused_computation.8 | loop fusion | flops 196352 | bytes 4096 | tf_op jit(solution)/shard_map/reduce_sum | solution.py:191
  8.6 1.0 %fusion = f32[256,256]{1,0:T(8,128)S(1)} fusion(s32[256]{0:T(256)S(1)} %select_reduce_fusion, s32[1,2,2]{2,1,0:T(2,128)} %param.12, s32[2]{0:T(128)S(1)} %and_select_fusion), kind=kOutput, calls=%fused_computation.1 | convolution fusion | flops 396300 | bytes 263192 | tf_op jit(solution)/shard_map/dot_general | solution.py:200
  9.6 1.6 %copy-done.1 = bf16[1,512,2048]{2,1,0:T(8,128)(2,1)S(1)} copy-done((bf16[1,512,2048]{2,1,0:T(8,128)(2,1)S(1)}, bf16[1,512,2048]{2,1,0:T(8,128)(2,1)}, u32[]{:S(2)}) %copy-start.1) | copy-done | bytes 2097176
  11.2 0.9 %copy-done.2 = bf16[1,64,2048]{2,1,0:T(8,128)(2,1)S(1)} copy-done((bf16[1,64,2048]{2,1,0:T(8,128)(2,1)S(1)}, bf16[1,64,2048]{2,1,0:T(8,128)(2,1)}, u32[]{:S(2)}) %copy-start.2) | copy-done | bytes 262168
  12.2 5.7 %load_weights.1 = (bf16[1,64,2048]{2,1,0:T(8,128)(2,1)S(1)}, bf16[1,512,2048]{2,1,0:T(8,128)(2,1)S(1)}, bf16[1,2048,1536]{2,1,0:T(8,128)(2,1)}) custom-call(bf16[1,64,2048]{2,1,0:T(8,128)(2,1)S(1)} %copy-done.2, bf16[1,512,2048]{2,1,0:T(8,128)(2,1)S(1)} %copy-done.1, bf16[1,2048,1536]{2,1,0:T(8,128)(2,1)} %refs_2_.1), custom_call_target="tpu_custom_call" | custom-call | bytes 17301504 | tf_op jit(solution)/shard_map/load_weights/pallas_call | solution.py:74
  17.9 1.8 %attend_project.5 = bf16[64,2048]{1,0:T(8,128)(2,1)S(1)} custom-call(bf16[64,1536]{1,0:T(8,128)(2,1)S(1)} %copy-done, bf16[64,1536]{1,0:T(8,128)(2,1)S(1)} %collective-permute-done.refs_1_, bf16[64,1536]{1,0:T(8,128)(2,1)S(1)} %collective-permute-done.1.refs_2_, bf16[64,1536]{1,0:T(8,128)(2,1)S(1)} %collective-permute-done.2.refs_3_, ...), custom_call_target="tpu_custom_call" | custom-call | flops 167772160 | bytes 2097152 | tf_op jit(solution)/shard_map/attend_project/pallas_call | solution.py:117
  19.8 0.1 collective-permute-start.3
  19.9 1.8 %attend_project.4 = bf16[64,2048]{1,0:T(8,128)(2,1)S(1)} custom-call(bf16[64,1536]{1,0:T(8,128)(2,1)S(1)} %copy-done, bf16[64,1536]{1,0:T(8,128)(2,1)S(1)} %collective-permute-done.refs_1_, bf16[64,1536]{1,0:T(8,128)(2,1)S(1)} %collective-permute-done.1.refs_2_, bf16[64,1536]{1,0:T(8,128)(2,1)S(1)} %collective-permute-done.2.refs_3_, ...), custom_call_target="tpu_custom_call" | custom-call | flops 167772160 | bytes 2097152 | tf_op jit(solution)/shard_map/attend_project/pallas_call | solution.py:117
  21.8 2.0 %collective-permute-start.5 = (bf16[64,2048]{1,0:T(8,128)(2,1)S(1)}, bf16[64,2048]{1,0:T(8,128)(2,1)S(1)}, u32[]{:S(2)}, u32[]{:S(2)}) collective-permute-start(bf16[64,2048]{1,0:T(8,128)(2,1)S(1)} %add_convert_fusion), channel_id=1, source_target_pairs={{0,2},{1,3},{2,0},{3,1},{4,6},{5,7},{6,4},{7,5},{8,10},{9,11},{10,... | collective-permute-start | bytes 786440 | tf_op jit(solution)/shard_map/ppermute | solution.py:23
  23.8 1.8 %attend_project.7 = bf16[64,2048]{1,0:T(8,128)(2,1)S(1)} custom-call(bf16[64,1536]{1,0:T(8,128)(2,1)S(1)} %copy-done, bf16[64,1536]{1,0:T(8,128)(2,1)S(1)} %collective-permute-done.refs_1_, bf16[64,1536]{1,0:T(8,128)(2,1)S(1)} %collective-permute-done.1.refs_2_, bf16[64,1536]{1,0:T(8,128)(2,1)S(1)} %collective-permute-done.2.refs_3_, ...), custom_call_target="tpu_custom_call" | custom-call | flops 167772160 | bytes 2097152 | tf_op jit(solution)/shard_map/attend_project/pallas_call | solution.py:117
  25.7 1.8 %attend_project.6 = bf16[64,2048]{1,0:T(8,128)(2,1)S(1)} custom-call(bf16[64,1536]{1,0:T(8,128)(2,1)S(1)} %copy-done, bf16[64,1536]{1,0:T(8,128)(2,1)S(1)} %collective-permute-done.refs_1_, bf16[64,1536]{1,0:T(8,128)(2,1)S(1)} %collective-permute-done.1.refs_2_, bf16[64,1536]{1,0:T(8,128)(2,1)S(1)} %collective-permute-done.2.refs_3_, ...), custom_call_target="tpu_custom_call" | custom-call | flops 167772160 | bytes 2097152 | tf_op jit(solution)/shard_map/attend_project/pallas_call | solution.py:117
  27.5 3.0 %collective-permute-done.5 = bf16[64,2048]{1,0:T(8,128)(2,1)S(1)} collective-permute-done((bf16[64,2048]{1,0:T(8,128)(2,1)S(1)}, bf16[64,2048]{1,0:T(8,128)(2,1)S(1)}, u32[]{:S(2)}, u32[]{:S(2)}) %collective-permute-start.5) | collective-permute-done | bytes 262176 | tf_op jit(solution)/shard_map/ppermute | solution.py:23
  30.5 0.1 fusion.5
  30.7 1.7 %collective-permute-start.6 = (bf16[64,2048]{1,0:T(8,128)(2,1)S(1)}, bf16[64,2048]{1,0:T(8,128)(2,1)S(1)}, u32[]{:S(2)}, u32[]{:S(2)}) collective-permute-start(bf16[64,2048]{1,0:T(8,128)(2,1)S(1)} %fusion.5), channel_id=1, source_target_pairs={{0,4},{4,8},{8,12},{12,16},{16,20},{20,24},{24,28},{28,0},{1,5},{5... | collective-permute-start | bytes 786440 | tf_op jit(solution)/shard_map/ppermute | solution.py:28
  32.4 8.9 %collective-permute-done.6.refs_0_ = bf16[64,2048]{1,0:T(8,128)(2,1)S(1)} collective-permute-done((bf16[64,2048]{1,0:T(8,128)(2,1)S(1)}, bf16[64,2048]{1,0:T(8,128)(2,1)S(1)}, u32[]{:S(2)}, u32[]{:S(2)}) %collective-permute-start.6) | collective-permute-done | bytes 262176 | tf_op jit(solution)/shard_map/ppermute | solution.py:28
  41.3 1.5 %collective-permute-start.8 = (bf16[64,2048]{1,0:T(8,128)(2,1)S(1)}, bf16[64,2048]{1,0:T(8,128)(2,1)S(1)}, u32[]{:S(2)}, u32[]{:S(2)}) collective-permute-start(bf16[64,2048]{1,0:T(8,128)(2,1)S(1)} %collective-permute-done.6.refs_0_), channel_id=1, source_target_pairs={{0,2},{1,3},{2,0},{3,1},{4,6},{5,7},{6,4},{7,5},{8,10},{9,11},{10,... | collective-permute-start | bytes 786440 | tf_op jit(solution)/shard_map/ppermute | solution.py:23
  42.8 5.4 %collective-permute-done.8.refs_2_ = bf16[64,2048]{1,0:T(8,128)(2,1)S(1)} collective-permute-done((bf16[64,2048]{1,0:T(8,128)(2,1)S(1)}, bf16[64,2048]{1,0:T(8,128)(2,1)S(1)}, u32[]{:S(2)}, u32[]{:S(2)}) %collective-permute-start.8) | collective-permute-done | bytes 262176 | tf_op jit(solution)/shard_map/ppermute | solution.py:23
  48.2 1.5 %collective-permute-done.9.refs_3_ = bf16[64,2048]{1,0:T(8,128)(2,1)S(1)} collective-permute-done((bf16[64,2048]{1,0:T(8,128)(2,1)S(1)}, bf16[64,2048]{1,0:T(8,128)(2,1)S(1)}, u32[]{:S(2)}, u32[]{:S(2)}) %collective-permute-start.9) | collective-permute-done | bytes 262176 | tf_op jit(solution)/shard_map/ppermute | solution.py:23
  49.8 5.8 %norm_project.1 = (bf16[1,64,2048]{2,1,0:T(8,128)(2,1)}, bf16[1,256,1536]{2,1,0:T(8,128)(2,1)}) custom-call(bf16[64,2048]{1,0:T(8,128)(2,1)S(1)} %collective-permute-done.6.refs_0_, bf16[64,2048]{1,0:T(8,128)(2,1)S(1)} %collective-permute-done.7.refs_1_, bf16[64,2048]{1,0:T(8,128)(2,1)S(1)} %collective-permute-done.8.refs_2_, ...), custom_call_target="tpu_custom_call" | custom-call | flops 1610612736 | bytes 6291456 | tf_op jit(solution)/shard_map/norm_project/pallas_call | solution.py:158
  (24 shorter events, 0.4 us)
Async XLA Ops:
  2.4 15.5 %copy-start = (bf16[64,1536]{1,0:T(8,128)(2,1)S(1)}, bf16[64,1536]{1,0:T(8,128)(2,1)}, u32[]{:S(2)}) copy-start(bf16[64,1536]{1,0:T(8,128)(2,1)} %get-tuple-element.11.refs_0_) | copy-start | bytes 589828
  2.4 15.5 %collective-permute-start = (bf16[64,1536]{1,0:T(8,128)(2,1)}, bf16[64,1536]{1,0:T(8,128)(2,1)S(1)}, u32[]{:S(2)}, u32[]{:S(2)}) collective-permute-start(bf16[64,1536]{1,0:T(8,128)(2,1)} %get-tuple-element.12), channel_id=1, source_target_pairs={{0,1},{1,0},{2,3},{3,2},{4,5},{5,4},{6,7},{7,6},{8,9},{9,8},{10,11... | collective-permute-start | bytes 589832 | tf_op jit(solution)/shard_map/ppermute | solution.py:23
  4.8 13.2 %collective-permute-start.1 = (bf16[64,1536]{1,0:T(8,128)(2,1)}, bf16[64,1536]{1,0:T(8,128)(2,1)S(1)}, u32[]{:S(2)}, u32[]{:S(2)}) collective-permute-start(bf16[64,1536]{1,0:T(8,128)(2,1)} %get-tuple-element.13), channel_id=1, source_target_pairs={{0,2},{1,3},{2,0},{3,1},{4,6},{5,7},{6,4},{7,5},{8,10},{9,11},{10,... | collective-permute-start | bytes 589832 | tf_op jit(solution)/shard_map/ppermute | solution.py:23
  7.4 10.6 %collective-permute-start.2 = (bf16[64,1536]{1,0:T(8,128)(2,1)}, bf16[64,1536]{1,0:T(8,128)(2,1)S(1)}, u32[]{:S(2)}, u32[]{:S(2)}) collective-permute-start(bf16[64,1536]{1,0:T(8,128)(2,1)} %get-tuple-element.14), channel_id=1, source_target_pairs={{0,3},{1,2},{2,1},{3,0},{4,7},{5,6},{6,5},{7,4},{8,11},{9,10},{10,... | collective-permute-start | bytes 589832 | tf_op jit(solution)/shard_map/ppermute | solution.py:23
  9.6 1.6 %copy-start.1 = (bf16[1,512,2048]{2,1,0:T(8,128)(2,1)S(1)}, bf16[1,512,2048]{2,1,0:T(8,128)(2,1)}, u32[]{:S(2)}) copy-start(bf16[1,512,2048]{2,1,0:T(8,128)(2,1)} %refs_1_.1) | copy-start | bytes 6291460
  11.2 0.9 %copy-start.2 = (bf16[1,64,2048]{2,1,0:T(8,128)(2,1)S(1)}, bf16[1,64,2048]{2,1,0:T(8,128)(2,1)}, u32[]{:S(2)}) copy-start(bf16[1,64,2048]{2,1,0:T(8,128)(2,1)} %refs_0_.1) | copy-start | bytes 786436
  19.8 30.0 %copy-start.3 = (f32[1,2048]{1,0:T(1,128)S(1)}, f32[1,2048]{1,0:T(1,128)}, u32[]{:S(2)}) copy-start(f32[1,2048]{1,0:T(1,128)} %refs_4_.1) | copy-start | bytes 24580
  19.8 2.0 %collective-permute-start.3 = (bf16[64,2048]{1,0:T(8,128)(2,1)S(1)}, bf16[64,2048]{1,0:T(8,128)(2,1)S(1)}, u32[]{:S(2)}, u32[]{:S(2)}) collective-permute-start(bf16[64,2048]{1,0:T(8,128)(2,1)S(1)} %attend_project.5), channel_id=1, source_target_pairs={{0,1},{1,0},{2,3},{3,2},{4,5},{5,4},{6,7},{7,6},{8,9},{9,8},{10,11... | collective-permute-start | bytes 786440 | tf_op jit(solution)/shard_map/ppermute | solution.py:23
  21.8 8.7 %collective-permute-start.5 = (bf16[64,2048]{1,0:T(8,128)(2,1)S(1)}, bf16[64,2048]{1,0:T(8,128)(2,1)S(1)}, u32[]{:S(2)}, u32[]{:S(2)}) collective-permute-start(bf16[64,2048]{1,0:T(8,128)(2,1)S(1)} %add_convert_fusion), channel_id=1, source_target_pairs={{0,2},{1,3},{2,0},{3,1},{4,6},{5,7},{6,4},{7,5},{8,10},{9,11},{10,... | collective-permute-start | bytes 786440 | tf_op jit(solution)/shard_map/ppermute | solution.py:23
  25.6 4.9 %collective-permute-start.4 = (bf16[64,2048]{1,0:T(8,128)(2,1)S(1)}, bf16[64,2048]{1,0:T(8,128)(2,1)S(1)}, u32[]{:S(2)}, u32[]{:S(2)}) collective-permute-start(bf16[64,2048]{1,0:T(8,128)(2,1)S(1)} %attend_project.7), channel_id=1, source_target_pairs={{0,1},{1,0},{2,3},{3,2},{4,5},{5,4},{6,7},{7,6},{8,9},{9,8},{10,11... | collective-permute-start | bytes 786440 | tf_op jit(solution)/shard_map/ppermute | solution.py:23
  30.7 10.6 %collective-permute-start.6 = (bf16[64,2048]{1,0:T(8,128)(2,1)S(1)}, bf16[64,2048]{1,0:T(8,128)(2,1)S(1)}, u32[]{:S(2)}, u32[]{:S(2)}) collective-permute-start(bf16[64,2048]{1,0:T(8,128)(2,1)S(1)} %fusion.5), channel_id=1, source_target_pairs={{0,4},{4,8},{8,12},{12,16},{16,20},{20,24},{24,28},{28,0},{1,5},{5... | collective-permute-start | bytes 786440 | tf_op jit(solution)/shard_map/ppermute | solution.py:28
  41.3 7.0 %collective-permute-start.8 = (bf16[64,2048]{1,0:T(8,128)(2,1)S(1)}, bf16[64,2048]{1,0:T(8,128)(2,1)S(1)}, u32[]{:S(2)}, u32[]{:S(2)}) collective-permute-start(bf16[64,2048]{1,0:T(8,128)(2,1)S(1)} %collective-permute-done.6.refs_0_), channel_id=1, source_target_pairs={{0,2},{1,3},{2,0},{3,1},{4,6},{5,7},{6,4},{7,5},{8,10},{9,11},{10,... | collective-permute-start | bytes 786440 | tf_op jit(solution)/shard_map/ppermute | solution.py:23
  42.8 5.5 %collective-permute-start.7 = (bf16[64,2048]{1,0:T(8,128)(2,1)S(1)}, bf16[64,2048]{1,0:T(8,128)(2,1)S(1)}, u32[]{:S(2)}, u32[]{:S(2)}) collective-permute-start(bf16[64,2048]{1,0:T(8,128)(2,1)S(1)} %collective-permute-done.6.refs_0_), channel_id=1, source_target_pairs={{0,1},{1,0},{2,3},{3,2},{4,5},{5,4},{6,7},{7,6},{8,9},{9,8},{10,11... | collective-permute-start | bytes 786440 | tf_op jit(solution)/shard_map/ppermute | solution.py:23
  48.2 1.5 %collective-permute-start.9 = (bf16[64,2048]{1,0:T(8,128)(2,1)S(1)}, bf16[64,2048]{1,0:T(8,128)(2,1)S(1)}, u32[]{:S(2)}, u32[]{:S(2)}) collective-permute-start(bf16[64,2048]{1,0:T(8,128)(2,1)S(1)} %collective-permute-done.8.refs_2_), channel_id=1, source_target_pairs={{0,1},{1,0},{2,3},{3,2},{4,5},{5,4},{6,7},{7,6},{8,9},{9,8},{10,11... | collective-permute-start | bytes 786440 | tf_op jit(solution)/shard_map/ppermute | solution.py:23

commit v3 on v2

--- a/solution.py
+++ b/solution.py
@@ -12,7 +12,8 @@
 WIN = 256
 BLOCK = 128
 NEG = -1e30
-VMEM_LIMIT = 48 * 1024 * 1024
+VMEM_LIMIT = 16 * 1024 * 1024
+SMALL_LIMIT = 4 * 1024 * 1024
 
 VM = pl.BlockSpec(memory_space=pltpu.VMEM)
 ANY = pl.BlockSpec(memory_space=pltpu.HBM)
@@ -29,7 +30,7 @@
 
 
 def cut_kernel(js, src, *refs):
-    outs, sems = refs[: len(js)], refs[len(js)]
+    outs, sems = refs[-1 - len(js) : -1], refs[-1]
     width = outs[0].shape[1]
     me = lax.axis_index("seq")
     copies = []
@@ -42,22 +43,23 @@
         c.wait()
 
 
-def cut(projected, n, js):
+def cut(projected, n, js, after=()):
     _, rows, columns = projected.shape
     width = columns // n
     return pl.pallas_call(
         functools.partial(cut_kernel, js),
         out_shape=[jax.ShapeDtypeStruct((rows, width), projected.dtype)] * len(js),
-        in_specs=[ANY],
+        in_specs=[ANY] * (1 + len(after)),
         out_specs=[VM] * len(js),
         scratch_shapes=[pltpu.SemaphoreType.DMA((len(js),))],
+        compiler_params=pltpu.CompilerParams(vmem_limit_bytes=SMALL_LIMIT),
         name="cut_slices",
-    )(projected)
+    )(projected, *after)
 
 
 def load_kernel(pieces, *refs):
     count = len(pieces)
-    ins, outs, sems = refs[:count], refs[count : 2 * count], refs[2 * count]
+    ins, outs, sems = refs[:count], refs[-1 - count : -1], refs[-1]
     copies = []
     for i, many in enumerate(pieces):
         step = ins[i].shape[1] // many
@@ -70,19 +72,19 @@
         c.wait()
 
 
-def load(arrays, pieces):
+def load(arrays, pieces, after=()):
     return pl.pallas_call(
         functools.partial(load_kernel, pieces),
         out_shape=[jax.ShapeDtypeStruct(a.shape, a.dtype) for a in arrays],
-        in_specs=[ANY] * len(arrays),
+        in_specs=[ANY] * (len(arrays) + len(after)),
         out_specs=[VM] * len(arrays),
         scratch_shapes=[pltpu.SemaphoreType.DMA((sum(pieces),))],
-        compiler_params=pltpu.CompilerParams(vmem_limit_bytes=VMEM_LIMIT),
+        compiler_params=pltpu.CompilerParams(vmem_limit_bytes=SMALL_LIMIT),
         cost_estimate=pl.CostEstimate(
             flops=0, bytes_accessed=2 * sum(a.size * a.dtype.itemsize for a in arrays), transcendentals=0
         ),
         name="load_weights",
-    )(*arrays)
+    )(*arrays, *after)
 
 
 def attend_kernel(n, lo, hi, *refs):
@@ -107,8 +109,7 @@
         outs[j][...] = term[j * rows : (j + 1) * rows]
 
 
-def attend(blocks, bias, weight, lo):
-    hi = lo + 1
+def attend(blocks, bias, weight, lo, hi):
     n = len(blocks)
     rows, width = blocks[0].shape
     depth = weight.shape[2]
@@ -206,24 +207,23 @@
     rows = projected.shape[1]
     far_cut = cut(projected, n, tuple(range(2, n)))
     far = [swap(far_cut[j - 2], j) for j in range(2, n)]
-    near_cut = cut(projected, n, (0, 1))
+    near_cut = cut(projected, n, (0, 1), (far_cut[0],))
     blocks = [near_cut[0], swap(near_cut[1], 1)] + far
+    stream, out_weight = load((stream_before, out_weight), (1, 4))
     bias = mask_bias(block_mask, token_order, n, rows)
-    stream, out_weight, proj_weight = load((stream_before, out_weight, proj_weight), (1, 4, 8))
+    terms = attend(blocks, bias[2 * rows :], out_weight, 2, n)
     sums = []
-    for k in range(2, n, 2):
-        (crossing,) = attend(blocks, bias[(k + 1) * rows : (k + 2) * rows], out_weight, k + 1)
-        (staying,) = attend(blocks, bias[k * rows : (k + 1) * rows], out_weight, k)
-        joined = staying.astype(jnp.float32) + swap(crossing, 1).astype(jnp.float32)
+    for k in range(0, n - 2, 2):
+        joined = terms[k].astype(jnp.float32) + swap(terms[k + 1], 1).astype(jnp.float32)
         sums.append(joined.astype(jnp.bfloat16))
     arrived = [swap(x, 2 * k + 2) for k, x in enumerate(sums)]
-    sums, near_bias = lax.optimization_barrier((sums, bias[: 2 * rows]))
-    (crossing,) = attend(blocks, near_bias[rows:], out_weight, 1)
-    (staying,) = attend(blocks, near_bias[:rows], out_weight, 0)
+    staying, crossing = attend(blocks, bias[: 2 * rows], out_weight, 0, 2)
+    (proj_weight,) = load((proj_weight,), (8,), (staying,))
     total = stream[0].astype(jnp.float32) + staying.astype(jnp.float32) + swap(crossing, 1).astype(jnp.float32)
     for a in arrived:
         total = total + a.astype(jnp.float32)
-    incoming = onward(total.astype(jnp.bfloat16))
+    total, proj_weight = lax.optimization_barrier((total.astype(jnp.bfloat16), proj_weight))
+    incoming = onward(total)
     xs = [incoming, swap(incoming, 1)]
     for k in range(2, n, 2):
         other = swap(incoming, k)

time: 55.8 us -> 48.6 us (0.87)
  Pallas kernels: 22.3 us -> 7.13 us
  waiting for transfers between devices: 18.9 us -> 23.3 us
  local copies, waits for them, and re-layouts: 2.66 us -> 4.89 us
  starting transfers between devices: 8.67 us -> 9.44 us
  matrix products: 1.04 us -> 1.74 us
    pallas_call x1 -> x2, Pallas kernels: 5.73 us -> 0.72 us  [load(): pl.pallas_call(functools.partial(load_kernel, pieces), out_shape=[jax.Sha...]
    pallas_call x4 -> x2, Pallas kernels: 7.25 us -> 2.51 us  [attend(): pl.pallas_call(functools.partial(attend_kernel, n, lo, hi), out_shape=[ja...]
    ppermute x9, waiting for transfers between devices: 10 us -> 14.4 us  [swap(): return lax.ppermute(x, 'seq', [(i, i ^ by) for i in range(size)])]
    pallas_call x2, Pallas kernels: 3.59 us -> 0.84 us  [cut(): pl.pallas_call(functools.partial(cut_kernel, js), out_shape=[jax.ShapeDty...]
    pallas_call x1, Pallas kernels: 5.78 us -> 3.06 us  [project(): pl.pallas_call(functools.partial(project_whole, n, tile), out_shape=[jax....]
    unnamed x8 -> x10, local copies, waits for them, and re-layouts: 2.55 us -> 3.67 us
    slice x3 -> x1, local copies, waits for them, and re-layouts: 0.03 us -> 1.14 us  [local(): staying, crossing = attend(blocks, bias[:2 * rows], out_weight, 0, 2)]
    ppermute x9, starting transfers between devices: 6.98 us -> 7.73 us  [swap(): return lax.ppermute(x, 'seq', [(i, i ^ by) for i in range(size)])]
  transfers between devices with their start and end apart: 10 -> 10, of which waited for: 4 -> 5; matrix products, arithmetic and copies ran while one was open for 4% -> 8% of each run, Pallas kernels for 23% -> 6%
where the time goes in v3:
time: 48.6 us; the launch traced here: 48.3 us
  waiting for transfers between devices  23.3 us (48%)
  starting transfers between devices  9.44 us (19%)
  Pallas kernels  7.13 us (15%)
  local copies, waits for them, and re-layouts  4.89 us (10%)
  matrix products  1.74 us (4%)
  other arithmetic  1.14 us (2%)
  between operations  0.73 us (2%)
    ppermute x9, waiting for transfers between devices, swap(): return lax.ppermute(x, 'seq', [(i, i ^ by) for i in range(size)])  14.4 us
    ppermute x1, waiting for transfers between devices, onward(): lax.ppermute(x, 'segment', [(i, (i + 1) % size) for i in range(size)])  8.84 us
    ppermute x9, starting transfers between devices, swap(): return lax.ppermute(x, 'seq', [(i, i ^ by) for i in range(size)])  7.73 us
    unnamed x10, local copies, waits for them, and re-layouts  3.67 us
    pallas_call x1, Pallas kernels, project(): pl.pallas_call(functools.partial(project_whole, n, tile), out_shape=[jax....  3.06 us
    pallas_call x2, Pallas kernels, attend(): pl.pallas_call(functools.partial(attend_kernel, n, lo, hi), out_shape=[ja...  2.51 us
    dot_general x1, matrix products, mask_bias(): seen = hot @ full.astype(jnp.float32) @ hot.T  1.74 us
    ppermute x1, starting transfers between devices, onward(): lax.ppermute(x, 'segment', [(i, (i + 1) % size) for i in range(size)])  1.7 us
  transfers between devices with their start and end apart: 10, of which 5 were waited for; matrix products, arithmetic and copies ran while one was open for 8% of the time, Pallas kernels for 6%

profile of v3, /device:TPU:0, one launch (start us, length us, event | category | flops | bytes accessed | tf_op | source)
XLA Modules:
  0.0 48.3 jit_solution(664419953050939577)
XLA Ops:
  0.6 1.1 %copy-done.1 = bf16[1,64,6144]{2,1,0:T(8,128)(2,1)S(1)} copy-done((bf16[1,64,6144]{2,1,0:T(8,128)(2,1)S(1)}, bf16[1,64,6144]{2,1,0:T(8,128)(2,1)}, u32[]{:S(2)}) %copy-start.1) | copy-done | bytes 786456
  1.9 2.5 %collective-permute-start.2 = (bf16[64,1536]{1,0:T(8,128)(2,1)S(1)}, bf16[64,1536]{1,0:T(8,128)(2,1)S(1)}, u32[]{:S(2)}, u32[]{:S(2)}) collective-permute-start(bf16[64,1536]{1,0:T(8,128)(2,1)S(1)} %get-tuple-element.18), channel_id=1, source_target_pairs={{0,3},{1,2},{2,1},{3,0},{4,7},{5,6},{6,5},{7,4},{8,11},{9,10},{10,... | collective-permute-start | bytes 589832 | tf_op jit(solution)/shard_map/ppermute | solution.py:24
  4.3 0.6 %collective-permute-start.1 = (bf16[64,1536]{1,0:T(8,128)(2,1)S(1)}, bf16[64,1536]{1,0:T(8,128)(2,1)S(1)}, u32[]{:S(2)}, u32[]{:S(2)}) collective-permute-start(bf16[64,1536]{1,0:T(8,128)(2,1)S(1)} %get-tuple-element.15.refs_0_), channel_id=1, source_target_pairs={{0,2},{1,3},{2,0},{3,1},{4,6},{5,7},{6,4},{7,5},{8,10},{9,11},{10,... | collective-permute-start | bytes 589832 | tf_op jit(solution)/shard_map/ppermute | solution.py:24
  5.0 0.8 %cut_slices.3 = (bf16[64,1536]{1,0:T(8,128)(2,1)S(1)}, bf16[64,1536]{1,0:T(8,128)(2,1)}) custom-call(bf16[1,64,6144]{2,1,0:T(8,128)(2,1)S(1)} %copy-done.1, bf16[64,1536]{1,0:T(8,128)(2,1)S(1)} %get-tuple-element.15.refs_0_), custom_call_target="tpu_custom_call" | custom-call | tf_op jit(solution)/shard_map/cut_slices/pallas_call | solution.py:49
  6.0 1.6 %copy-done.2 = bf16[1,512,2048]{2,1,0:T(8,128)(2,1)S(1)} copy-done((bf16[1,512,2048]{2,1,0:T(8,128)(2,1)S(1)}, bf16[1,512,2048]{2,1,0:T(8,128)(2,1)}, u32[]{:S(2)}) %copy-start.2) | copy-done | bytes 2097176
  7.6 0.9 %copy-done.3 = bf16[1,64,2048]{2,1,0:T(8,128)(2,1)S(1)} copy-done((bf16[1,64,2048]{2,1,0:T(8,128)(2,1)S(1)}, bf16[1,64,2048]{2,1,0:T(8,128)(2,1)}, u32[]{:S(2)}) %copy-start.3) | copy-done | bytes 262168
  8.5 0.2 load_weights.2
  8.8 0.9 %select_reduce_fusion = s32[256]{0:T(256)S(1)} fusion(s32[256]{0:T(256)S(1)} %and_select_fusion.1, s32[256]{0:T(256)} %param.13, s32[256]{0:T(256)S(1)} %add.52), kind=kLoop, calls=%fused_computation.8 | loop fusion | flops 196352 | bytes 4096 | tf_op jit(solution)/shard_map/reduce_sum | solution.py:192
  9.6 1.7 %fusion = f32[256,256]{1,0:T(8,128)} fusion(s32[256]{0:T(256)S(1)} %select_reduce_fusion, s32[1,2,2]{2,1,0:T(2,128)} %param.12, s32[2]{0:T(128)S(1)} %and_select_fusion), kind=kOutput, calls=%fused_computation.1 | convolution fusion | flops 396300 | bytes 263192 | tf_op jit(solution)/shard_map/dot_general | solution.py:201
  11.4 1.1 %fusion.21 = (f32[128,256]{1,0:T(8,128)S(1)}, f32[128,256]{1,0:T(8,128)S(1)}) fusion(f32[256,256]{1,0:T(8,128)} %fusion), kind=kLoop, calls=%fused_computation.28 | loop fusion | bytes 524288 | tf_op jit(solution)/shard_map/slice | solution.py:220
  12.5 1.5 %collective-permute-done.1.refs_2_ = bf16[64,1536]{1,0:T(8,128)(2,1)S(1)} collective-permute-done((bf16[64,1536]{1,0:T(8,128)(2,1)S(1)}, bf16[64,1536]{1,0:T(8,128)(2,1)S(1)}, u32[]{:S(2)}, u32[]{:S(2)}) %collective-permute-start.1) | collective-permute-done | bytes 196640 | tf_op jit(solution)/shard_map/ppermute | solution.py:24
  14.0 1.3 %attend_project.3 = (bf16[64,2048]{1,0:T(8,128)(2,1)S(1)}, bf16[64,2048]{1,0:T(8,128)(2,1)S(1)}) custom-call(bf16[64,1536]{1,0:T(8,128)(2,1)S(1)} %get-tuple-element.16.refs_0_, bf16[64,1536]{1,0:T(8,128)(2,1)S(1)} %collective-permute-done.refs_1_, bf16[64,1536]{1,0:T(8,128)(2,1)S(1)} %collective-permute-done.1.refs_2_, ...), custom_call_target="tpu_custom_call" | custom-call | flops 335544320 | bytes 2097152 | tf_op jit(solution)/shard_map/attend_project/pallas_call | solution.py:118
  15.3 1.3 %attend_project.2 = (bf16[64,2048]{1,0:T(8,128)(2,1)S(1)}, bf16[64,2048]{1,0:T(8,128)(2,1)S(1)}) custom-call(bf16[64,1536]{1,0:T(8,128)(2,1)S(1)} %get-tuple-element.16.refs_0_, bf16[64,1536]{1,0:T(8,128)(2,1)S(1)} %collective-permute-done.refs_1_, bf16[64,1536]{1,0:T(8,128)(2,1)S(1)} %collective-permute-done.1.refs_2_, ...), custom_call_target="tpu_custom_call" | custom-call | flops 335544320 | bytes 2097152 | tf_op jit(solution)/shard_map/attend_project/pallas_call | solution.py:118
  16.6 0.6 %collective-permute-start.3 = (bf16[64,2048]{1,0:T(8,128)(2,1)S(1)}, bf16[64,2048]{1,0:T(8,128)(2,1)S(1)}, u32[]{:S(2)}, u32[]{:S(2)}) collective-permute-start(bf16[64,2048]{1,0:T(8,128)(2,1)S(1)} %get-tuple-element.21), channel_id=1, source_target_pairs={{0,1},{1,0},{2,3},{3,2},{4,5},{5,4},{6,7},{7,6},{8,9},{9,8},{10,11... | collective-permute-start | bytes 786440 | tf_op jit(solution)/shard_map/ppermute | solution.py:24
  17.2 2.4 %collective-permute-start.5 = (bf16[64,2048]{1,0:T(8,128)(2,1)S(1)}, bf16[64,2048]{1,0:T(8,128)(2,1)S(1)}, u32[]{:S(2)}, u32[]{:S(2)}) collective-permute-start(bf16[64,2048]{1,0:T(8,128)(2,1)S(1)} %add_convert_fusion), channel_id=1, source_target_pairs={{0,2},{1,3},{2,0},{3,1},{4,6},{5,7},{6,4},{7,5},{8,10},{9,11},{10,... | collective-permute-start | bytes 786440 | tf_op jit(solution)/shard_map/ppermute | solution.py:24
  19.6 0.5 %load_weights.3.refs_5_ = bf16[1,2048,1536]{2,1,0:T(8,128)(2,1)S(1)} custom-call(bf16[1,2048,1536]{2,1,0:T(8,128)(2,1)S(1)} %copy-done, bf16[64,2048]{1,0:T(8,128)(2,1)S(1)} %get-tuple-element.20.refs_1_), custom_call_target="tpu_custom_call" | custom-call | bytes 12582912 | tf_op jit(solution)/shard_map/load_weights/pallas_call | solution.py:76
  20.1 6.0 %collective-permute-done.5 = bf16[64,2048]{1,0:T(8,128)(2,1)S(1)} collective-permute-done((bf16[64,2048]{1,0:T(8,128)(2,1)S(1)}, bf16[64,2048]{1,0:T(8,128)(2,1)S(1)}, u32[]{:S(2)}, u32[]{:S(2)}) %collective-permute-start.5) | collective-permute-done | bytes 262176 | tf_op jit(solution)/shard_map/ppermute | solution.py:24
  26.2 0.1 fusion.5
  26.3 1.7 %collective-permute-start.6 = (bf16[64,2048]{1,0:T(8,128)(2,1)S(1)}, bf16[64,2048]{1,0:T(8,128)(2,1)S(1)}, u32[]{:S(2)}, u32[]{:S(2)}) collective-permute-start(bf16[64,2048]{1,0:T(8,128)(2,1)S(1)} %fusion.5), channel_id=1, source_target_pairs={{0,4},{4,8},{8,12},{12,16},{16,20},{20,24},{24,28},{28,0},{1,5},{5... | collective-permute-start | bytes 786440 | tf_op jit(solution)/shard_map/ppermute | solution.py:29
  28.0 8.8 %collective-permute-done.6.refs_0_ = bf16[64,2048]{1,0:T(8,128)(2,1)S(1)} collective-permute-done((bf16[64,2048]{1,0:T(8,128)(2,1)S(1)}, bf16[64,2048]{1,0:T(8,128)(2,1)S(1)}, u32[]{:S(2)}, u32[]{:S(2)}) %collective-permute-start.6) | collective-permute-done | bytes 262176 | tf_op jit(solution)/shard_map/ppermute | solution.py:29
  36.9 1.5 %collective-permute-start.8 = (bf16[64,2048]{1,0:T(8,128)(2,1)S(1)}, bf16[64,2048]{1,0:T(8,128)(2,1)S(1)}, u32[]{:S(2)}, u32[]{:S(2)}) collective-permute-start(bf16[64,2048]{1,0:T(8,128)(2,1)S(1)} %collective-permute-done.6.refs_0_), channel_id=1, source_target_pairs={{0,2},{1,3},{2,0},{3,1},{4,6},{5,7},{6,4},{7,5},{8,10},{9,11},{10,... | collective-permute-start | bytes 786440 | tf_op jit(solution)/shard_map/ppermute | solution.py:24
  38.4 5.4 %collective-permute-done.8.refs_2_ = bf16[64,2048]{1,0:T(8,128)(2,1)S(1)} collective-permute-done((bf16[64,2048]{1,0:T(8,128)(2,1)S(1)}, bf16[64,2048]{1,0:T(8,128)(2,1)S(1)}, u32[]{:S(2)}, u32[]{:S(2)}) %collective-permute-start.8) | collective-permute-done | bytes 262176 | tf_op jit(solution)/shard_map/ppermute | solution.py:24
  43.8 1.5 %collective-permute-done.9.refs_3_ = bf16[64,2048]{1,0:T(8,128)(2,1)S(1)} collective-permute-done((bf16[64,2048]{1,0:T(8,128)(2,1)S(1)}, bf16[64,2048]{1,0:T(8,128)(2,1)S(1)}, u32[]{:S(2)}, u32[]{:S(2)}) %collective-permute-start.9) | collective-permute-done | bytes 262176 | tf_op jit(solution)/shard_map/ppermute | solution.py:24
  45.3 3.1 %norm_project.1 = (bf16[1,64,2048]{2,1,0:T(8,128)(2,1)}, bf16[1,256,1536]{2,1,0:T(8,128)(2,1)}) custom-call(bf16[64,2048]{1,0:T(8,128)(2,1)S(1)} %collective-permute-done.6.refs_0_, bf16[64,2048]{1,0:T(8,128)(2,1)S(1)} %collective-permute-done.7.refs_1_, bf16[64,2048]{1,0:T(8,128)(2,1)S(1)} %collective-permute-done.8.refs_2_, ...), custom_call_target="tpu_custom_call" | custom-call | flops 1610612736 | bytes 6291456 | tf_op jit(solution)/shard_map/norm_project/pallas_call | solution.py:159
  (23 shorter events, 0.5 us)
Async XLA Ops:
  0.6 1.1 %copy-start.1 = (bf16[1,64,6144]{2,1,0:T(8,128)(2,1)S(1)}, bf16[1,64,6144]{2,1,0:T(8,128)(2,1)}, u32[]{:S(2)}) copy-start(bf16[1,64,6144]{2,1,0:T(8,128)(2,1)} %src.3) | copy-start | bytes 2359300
  1.9 10.7 %collective-permute-start.2 = (bf16[64,1536]{1,0:T(8,128)(2,1)S(1)}, bf16[64,1536]{1,0:T(8,128)(2,1)S(1)}, u32[]{:S(2)}, u32[]{:S(2)}) collective-permute-start(bf16[64,1536]{1,0:T(8,128)(2,1)S(1)} %get-tuple-element.18), channel_id=1, source_target_pairs={{0,3},{1,2},{2,1},{3,0},{4,7},{5,6},{6,5},{7,4},{8,11},{9,10},{10,... | collective-permute-start | bytes 589832 | tf_op jit(solution)/shard_map/ppermute | solution.py:24
  4.3 9.7 %collective-permute-start.1 = (bf16[64,1536]{1,0:T(8,128)(2,1)S(1)}, bf16[64,1536]{1,0:T(8,128)(2,1)S(1)}, u32[]{:S(2)}, u32[]{:S(2)}) collective-permute-start(bf16[64,1536]{1,0:T(8,128)(2,1)S(1)} %get-tuple-element.15.refs_0_), channel_id=1, source_target_pairs={{0,2},{1,3},{2,0},{3,1},{4,6},{5,7},{6,4},{7,5},{8,10},{9,11},{10,... | collective-permute-start | bytes 589832 | tf_op jit(solution)/shard_map/ppermute | solution.py:24
  5.7 8.3 %collective-permute-start = (bf16[64,1536]{1,0:T(8,128)(2,1)}, bf16[64,1536]{1,0:T(8,128)(2,1)S(1)}, u32[]{:S(2)}, u32[]{:S(2)}) collective-permute-start(bf16[64,1536]{1,0:T(8,128)(2,1)} %get-tuple-element.17), channel_id=1, source_target_pairs={{0,1},{1,0},{2,3},{3,2},{4,5},{5,4},{6,7},{7,6},{8,9},{9,8},{10,11... | collective-permute-start | bytes 589832 | tf_op jit(solution)/shard_map/ppermute | solution.py:24
  6.0 1.6 %copy-start.2 = (bf16[1,512,2048]{2,1,0:T(8,128)(2,1)S(1)}, bf16[1,512,2048]{2,1,0:T(8,128)(2,1)}, u32[]{:S(2)}) copy-start(bf16[1,512,2048]{2,1,0:T(8,128)(2,1)} %refs_1_.1) | copy-start | bytes 6291460
  7.6 0.9 %copy-start.3 = (bf16[1,64,2048]{2,1,0:T(8,128)(2,1)S(1)}, bf16[1,64,2048]{2,1,0:T(8,128)(2,1)}, u32[]{:S(2)}) copy-start(bf16[1,64,2048]{2,1,0:T(8,128)(2,1)} %refs_0_.2) | copy-start | bytes 786436
  11.4 8.2 %copy-start = (bf16[1,2048,1536]{2,1,0:T(8,128)(2,1)S(1)}, bf16[1,2048,1536]{2,1,0:T(8,128)(2,1)}, u32[]{:S(2)}) copy-start(bf16[1,2048,1536]{2,1,0:T(8,128)(2,1)} %refs_0_.3) | copy-start | bytes 18874372
  15.3 1.9 %collective-permute-start.4 = (bf16[64,2048]{1,0:T(8,128)(2,1)S(1)}, bf16[64,2048]{1,0:T(8,128)(2,1)S(1)}, u32[]{:S(2)}, u32[]{:S(2)}) collective-permute-start(bf16[64,2048]{1,0:T(8,128)(2,1)S(1)} %get-tuple-element.23), channel_id=1, source_target_pairs={{0,1},{1,0},{2,3},{3,2},{4,5},{5,4},{6,7},{7,6},{8,9},{9,8},{10,11... | collective-permute-start | bytes 786440 | tf_op jit(solution)/shard_map/ppermute | solution.py:24
  16.6 3.5 %collective-permute-start.3 = (bf16[64,2048]{1,0:T(8,128)(2,1)S(1)}, bf16[64,2048]{1,0:T(8,128)(2,1)S(1)}, u32[]{:S(2)}, u32[]{:S(2)}) collective-permute-start(bf16[64,2048]{1,0:T(8,128)(2,1)S(1)} %get-tuple-element.21), channel_id=1, source_target_pairs={{0,1},{1,0},{2,3},{3,2},{4,5},{5,4},{6,7},{7,6},{8,9},{9,8},{10,11... | collective-permute-start | bytes 786440 | tf_op jit(solution)/shard_map/ppermute | solution.py:24
  17.2 8.9 %collective-permute-start.5 = (bf16[64,2048]{1,0:T(8,128)(2,1)S(1)}, bf16[64,2048]{1,0:T(8,128)(2,1)S(1)}, u32[]{:S(2)}, u32[]{:S(2)}) collective-permute-start(bf16[64,2048]{1,0:T(8,128)(2,1)S(1)} %add_convert_fusion), channel_id=1, source_target_pairs={{0,2},{1,3},{2,0},{3,1},{4,6},{5,7},{6,4},{7,5},{8,10},{9,11},{10,... | collective-permute-start | bytes 786440 | tf_op jit(solution)/shard_map/ppermute | solution.py:24
  19.6 25.7 %copy-start.4 = (f32[1,2048]{1,0:T(1,128)S(1)}, f32[1,2048]{1,0:T(1,128)}, u32[]{:S(2)}) copy-start(f32[1,2048]{1,0:T(1,128)} %refs_4_.1) | copy-start | bytes 24580
  26.3 10.5 %collective-permute-start.6 = (bf16[64,2048]{1,0:T(8,128)(2,1)S(1)}, bf16[64,2048]{1,0:T(8,128)(2,1)S(1)}, u32[]{:S(2)}, u32[]{:S(2)}) collective-permute-start(bf16[64,2048]{1,0:T(8,128)(2,1)S(1)} %fusion.5), channel_id=1, source_target_pairs={{0,4},{4,8},{8,12},{12,16},{16,20},{20,24},{24,28},{28,0},{1,5},{5... | collective-permute-start | bytes 786440 | tf_op jit(solution)/shard_map/ppermute | solution.py:29
  36.9 6.9 %collective-permute-start.8 = (bf16[64,2048]{1,0:T(8,128)(2,1)S(1)}, bf16[64,2048]{1,0:T(8,128)(2,1)S(1)}, u32[]{:S(2)}, u32[]{:S(2)}) collective-permute-start(bf16[64,2048]{1,0:T(8,128)(2,1)S(1)} %collective-permute-done.6.refs_0_), channel_id=1, source_target_pairs={{0,2},{1,3},{2,0},{3,1},{4,6},{5,7},{6,4},{7,5},{8,10},{9,11},{10,... | collective-permute-start | bytes 786440 | tf_op jit(solution)/shard_map/ppermute | solution.py:24
  38.4 5.4 %collective-permute-start.7 = (bf16[64,2048]{1,0:T(8,128)(2,1)S(1)}, bf16[64,2048]{1,0:T(8,128)(2,1)S(1)}, u32[]{:S(2)}, u32[]{:S(2)}) collective-permute-start(bf16[64,2048]{1,0:T(8,128)(2,1)S(1)} %collective-permute-done.6.refs_0_), channel_id=1, source_target_pairs={{0,1},{1,0},{2,3},{3,2},{4,5},{5,4},{6,7},{7,6},{8,9},{9,8},{10,11... | collective-permute-start | bytes 786440 | tf_op jit(solution)/shard_map/ppermute | solution.py:24
  43.7 1.5 %collective-permute-start.9 = (bf16[64,2048]{1,0:T(8,128)(2,1)S(1)}, bf16[64,2048]{1,0:T(8,128)(2,1)S(1)}, u32[]{:S(2)}, u32[]{:S(2)}) collective-permute-start(bf16[64,2048]{1,0:T(8,128)(2,1)S(1)} %collective-permute-done.8.refs_2_), channel_id=1, source_target_pairs={{0,1},{1,0},{2,3},{3,2},{4,5},{5,4},{6,7},{7,6},{8,9},{9,8},{10,11... | collective-permute-start | bytes 786440 | tf_op jit(solution)/shard_map/ppermute | solution.py:24

commit v4 on v3

--- a/solution.py
+++ b/solution.py
@@ -24,9 +24,12 @@
     return lax.ppermute(x, "seq", [(i, i ^ by) for i in range(size)])
 
 
-def onward(x):
-    size = lax.axis_size("segment")
-    return lax.ppermute(x, "segment", [(i, (i + 1) % size) for i in range(size)])
+def onward(x, by):
+    sections, size = lax.axis_size("segment"), lax.axis_size("seq")
+    pairs = [
+        (s * size + t, (s + 1) % sections * size + (t ^ by)) for s in range(sections) for t in range(size)
+    ]
+    return lax.ppermute(x, ("segment", "seq"), pairs)
 
 
 def cut_kernel(js, src, *refs):
@@ -87,61 +90,131 @@
     )(*arrays, *after)
 
 
-def attend_kernel(n, lo, hi, *refs):
-    blocks, bias, weight, outs = refs[:n], refs[n], refs[n + 1], refs[n + 2 :]
+def attend_kernel(n, js, *refs):
+    blocks, bias, weight, out = refs[:n], refs[n], refs[n + 1], refs[n + 2]
     rows, width = blocks[0].shape
     heads = width // (3 * DH)
+    seen = jnp.concatenate([bias[j * rows : (j + 1) * rows] for j in js], axis=0)
     attended = []
     for h in range(heads):
         c = h * 3 * DH
-        q = jnp.concatenate([blocks[j][:, c : c + DH] for j in range(lo, hi)], axis=0)
+        q = jnp.concatenate([blocks[j][:, c : c + DH] for j in js], axis=0)
         k = jnp.concatenate([b[:, c + DH : c + 2 * DH] for b in blocks], axis=0)
         v = jnp.concatenate([b[:, c + 2 * DH : c + 3 * DH] for b in blocks], axis=0)
         s = lax.dot_general(q, k, (((1,), (1,)), ((), ())), preferred_element_type=jnp.float32)
-        s = s * DH ** (-0.5) + bias[...]
+        s = s * DH ** (-0.5) + seen
         m = jnp.max(s, axis=-1, keepdims=True)
         e = jnp.exp(s - m)
         p = (e / jnp.sum(e, axis=-1, keepdims=True)).astype(jnp.bfloat16)
         attended.append(jnp.dot(p, v, preferred_element_type=jnp.float32).astype(jnp.bfloat16))
     attended = jnp.concatenate(attended, axis=1)
-    term = jnp.dot(attended, weight[0], preferred_element_type=jnp.float32).astype(jnp.bfloat16)
-    for j in range(hi - lo):
-        outs[j][...] = term[j * rows : (j + 1) * rows]
-
-
-def attend(blocks, bias, weight, lo, hi):
+    out[...] = jnp.dot(attended, weight[0], preferred_element_type=jnp.float32).astype(jnp.bfloat16)
+
+
+def attend(blocks, bias, weight, js):
     n = len(blocks)
     rows, width = blocks[0].shape
     depth = weight.shape[2]
     heads = width // (3 * DH)
     tokens = n * rows
     return pl.pallas_call(
-        functools.partial(attend_kernel, n, lo, hi),
-        out_shape=[jax.ShapeDtypeStruct((rows, depth), jnp.bfloat16)] * (hi - lo),
+        functools.partial(attend_kernel, n, js),
+        out_shape=jax.ShapeDtypeStruct((len(js) * rows, depth), jnp.bfloat16),
         in_specs=[VM] * (n + 2),
-        out_specs=[VM] * (hi - lo),
+        out_specs=VM,
         compiler_params=pltpu.CompilerParams(vmem_limit_bytes=VMEM_LIMIT),
         cost_estimate=pl.CostEstimate(
-            flops=2 * (hi - lo) * rows * heads * DH * (2 * tokens + depth),
+            flops=2 * len(js) * rows * heads * DH * (2 * tokens + depth),
             bytes_accessed=2 * heads * DH * depth,
-            transcendentals=(hi - lo) * rows * tokens * heads,
+            transcendentals=len(js) * rows * tokens * heads,
         ),
         name="attend_project",
     )(*blocks, bias, weight)
 
 
-def project_kernel(n, tile, xs, gain, weight, kept, out, normed, made, sems):
-    rows = xs[0].shape[0]
+def chip_sum_kernel(rows, cols, mine, theirs, stream, partial, own, *others):
+    for i in range(mine.shape[0] // rows):
+        part = slice(i * rows, (i + 1) * rows)
+        total = mine[part, :].astype(jnp.float32) + theirs[part, :].astype(jnp.float32)
+        if i == 0:
+            total = total + stream[0].astype(jnp.float32)
+            own[...] = total[:, cols:]
+        else:
+            others[i - 1][...] = total[:, cols:].astype(jnp.bfloat16)
+        partial[part, :] = total[:, :cols].astype(jnp.bfloat16)
+
+
+def chip_sum(mine, theirs, stream, cols):
+    rows = stream.shape[1]
+    count, depth = mine.shape
+    rest = (rows, depth - cols)
+    return pl.pallas_call(
+        functools.partial(chip_sum_kernel, rows, cols),
+        out_shape=[
+            jax.ShapeDtypeStruct((count, cols), jnp.bfloat16),
+            jax.ShapeDtypeStruct(rest, jnp.float32),
+        ]
+        + [jax.ShapeDtypeStruct(rest, jnp.bfloat16)] * (count // rows - 1),
+        in_specs=[VM] * 3,
+        out_specs=[VM] * (count // rows + 1),
+        compiler_params=pltpu.CompilerParams(vmem_limit_bytes=SMALL_LIMIT),
+        name="chip_sum",
+    )(mine, theirs, stream)
+
+
+def settle_kernel(x, after, out):
+    out[...] = x[...]
+
+
+def settle(x, after):
+    return pl.pallas_call(
+        settle_kernel,
+        out_shape=jax.ShapeDtypeStruct(x.shape, x.dtype),
+        in_specs=[VM, ANY],
+        out_specs=VM,
+        compiler_params=pltpu.CompilerParams(vmem_limit_bytes=SMALL_LIMIT),
+        name="settle",
+    )(x, after)
+
+
+def join_kernel(rows, mine, *refs):
+    others, out = refs[:-1], refs[-1]
+    for i in range(mine.shape[0] // rows):
+        total = mine[i * rows : (i + 1) * rows, :].astype(jnp.float32)
+        for k, other in enumerate(others):
+            at = i ^ (k + 1)
+            total = total + other[at * rows : (at + 1) * rows, :].astype(jnp.float32)
+        out[i * rows : (i + 1) * rows, :] = total.astype(jnp.bfloat16)
+
+
+def join(rows, mine, others):
+    return pl.pallas_call(
+        functools.partial(join_kernel, rows),
+        out_shape=jax.ShapeDtypeStruct(mine.shape, mine.dtype),
+        in_specs=[VM] * (1 + len(others)),
+        out_specs=VM,
+        compiler_params=pltpu.CompilerParams(vmem_limit_bytes=SMALL_LIMIT),
+        name="join_chips",
+    )(mine, *others)
+
+
+def project_kernel(n, tile, even, odd, *refs):
+    rest, gain, weight, kept, out, normed, made, hold, sems = refs[:n], *refs[n:]
+    rows, cols = rest[0].shape[0], even.shape[1]
     width = weight.shape[2]
     me = lax.axis_index("seq")
-    keep = pltpu.make_async_copy(xs[0], kept.at[0], sems.at[0])
-    keep.start()
+    hold[:, :cols] = even[:rows, :]
+    hold[:, cols:] = rest[0][...]
+    copies = [pltpu.make_async_copy(hold, kept.at[0], sems.at[0])]
+    copies[0].start()
     for j in range(n):
-        x = xs[j][...].astype(jnp.float32)
-        scale = lax.rsqrt(jnp.mean(x * x, axis=-1, keepdims=True) + 1e-06)
+        first = (odd if j % 2 else even)[j // 2 * rows : (j // 2 + 1) * rows, :].astype(jnp.float32)
+        second = rest[j][...].astype(jnp.float32)
+        squares = jnp.sum(first * first, axis=-1, keepdims=True) + jnp.sum(second * second, axis=-1, keepdims=True)
+        scale = lax.rsqrt(squares / normed.shape[1] + 1e-06)
         at = pl.multiple_of((me ^ j) * rows, rows)
-        normed[pl.ds(at, rows), :] = (x * scale * gain[...]).astype(jnp.bfloat16)
-    copies = [keep]
+        normed[pl.ds(at, rows), :cols] = (first * scale * gain[:, :cols]).astype(jnp.bfloat16)
+        normed[pl.ds(at, rows), cols:] = (second * scale * gain[:, cols:]).astype(jnp.bfloat16)
     for i in range(width // tile):
         part = pl.ds(i * tile, tile)
         made[:, part] = jnp.dot(normed[...], weight[0, :, part], preferred_element_type=jnp.float32).astype(jnp.bfloat16)
@@ -151,22 +224,23 @@
         c.wait()
 
 
-def project(xs, gain, weight):
-    n = len(xs)
-    rows, depth = xs[0].shape
-    width = weight.shape[2]
+def project(even, odd, rest, gain, weight):
+    n = len(rest)
+    rows = rest[0].shape[0]
+    _, depth, width = weight.shape
     tile = 256 if width % 256 == 0 else 128
     return pl.pallas_call(
-        functools.partial(project_whole, n, tile),
+        functools.partial(project_kernel, n, tile),
         out_shape=[
             jax.ShapeDtypeStruct((1, rows, depth), jnp.bfloat16),
             jax.ShapeDtypeStruct((1, n * rows, width), jnp.bfloat16),
         ],
-        in_specs=[VM] * (n + 2),
+        in_specs=[VM] * (n + 4),
         out_specs=[ANY, ANY],
         scratch_shapes=[
             pltpu.VMEM((n * rows, depth), jnp.bfloat16),
             pltpu.VMEM((n * rows, width), jnp.bfloat16),
+            pltpu.VMEM((rows, depth), jnp.bfloat16),
             pltpu.SemaphoreType.DMA((1 + width // tile,)),
         ],
         compiler_params=pltpu.CompilerParams(vmem_limit_bytes=VMEM_LIMIT),
@@ -174,11 +248,7 @@
             flops=2 * n * rows * depth * width, bytes_accessed=2 * depth * width, transcendentals=0
         ),
         name="norm_project",
-    )(*xs, gain, weight)
-
-
-def project_whole(n, tile, *refs):
-    project_kernel(n, tile, refs[:n], *refs[n:])
+    )(even, odd, *rest, gain, weight)
 
 
 def mask_bias(block_mask, token_order, n, rows):
@@ -211,24 +281,25 @@
     blocks = [near_cut[0], swap(near_cut[1], 1)] + far
     stream, out_weight = load((stream_before, out_weight), (1, 4))
     bias = mask_bias(block_mask, token_order, n, rows)
-    terms = attend(blocks, bias[2 * rows :], out_weight, 2, n)
-    sums = []
-    for k in range(0, n - 2, 2):
-        joined = terms[k].astype(jnp.float32) + swap(terms[k + 1], 1).astype(jnp.float32)
-        sums.append(joined.astype(jnp.bfloat16))
-    arrived = [swap(x, 2 * k + 2) for k, x in enumerate(sums)]
-    staying, crossing = attend(blocks, bias[: 2 * rows], out_weight, 0, 2)
-    (proj_weight,) = load((proj_weight,), (8,), (staying,))
-    total = stream[0].astype(jnp.float32) + staying.astype(jnp.float32) + swap(crossing, 1).astype(jnp.float32)
-    for a in arrived:
-        total = total + a.astype(jnp.float32)
-    total, proj_weight = lax.optimization_barrier((total.astype(jnp.bfloat16), proj_weight))
-    incoming = onward(total)
-    xs = [incoming, swap(incoming, 1)]
-    for k in range(2, n, 2):
-        other = swap(incoming, k)
-        xs += [other, swap(other, 1)]
-    kept, following = project(xs, norm_gain, proj_weight)
+    crossing = attend(blocks, bias, out_weight, tuple(range(1, n, 2)))
+    staying = attend(blocks, bias, out_weight, tuple(range(0, n, 2)))
+    cols = crossing.shape[1] // 2
+    partial, own, *others = chip_sum(staying, swap(crossing, 1), stream, cols)
+    partial = onward(partial, 0)
+    total = own
+    for k, x in enumerate(others):
+        total = total + swap(x, 2 * k + 2).astype(jnp.float32)
+    total = total.astype(jnp.bfloat16)
+    rest = [onward(total, j) for j in range(0, n, 2)]
+    partial = settle(partial, total)
+    swapped = [swap(partial, j) for j in range(2, n, 2)]
+    (proj_weight,) = load((proj_weight,), (8,), (partial,))
+    rest, proj_weight = lax.optimization_barrier((rest, proj_weight))
+    rest = [r for x in rest for r in (x, swap(x, 1))]
+    swapped, rest = lax.optimization_barrier((swapped, rest))
+    even = join(rows, partial, swapped)
+    odd = swap(even, 1)
+    kept, following = project(even, odd, rest, norm_gain, proj_weight)
     return (kept, following)
 
 

time: 48.6 us -> 44.9 us (0.924)
  waiting for transfers between devices: 23.3 us -> 14.9 us
  starting transfers between devices: 9.44 us -> 12.4 us
  local copies, waits for them, and re-layouts: 4.89 us -> 6.54 us
  Pallas kernels: 7.13 us -> 8.04 us
  matrix products: 1.74 us -> 1.04 us
    ppermute x9, waiting for transfers between devices: 14.4 us -> 10.2 us  [swap(): return lax.ppermute(x, 'seq', [(i, i ^ by) for i in range(size)])]
    ppermute x1 -> x3, waiting for transfers between devices: 8.84 us -> 4.68 us  [onward(): return lax.ppermute(x, ('segment', 'seq'), pairs)]
    ppermute x1 -> x3, starting transfers between devices: 1.7 us -> 5.76 us  [onward(): return lax.ppermute(x, ('segment', 'seq'), pairs)]
    unnamed x10, local copies, waits for them, and re-layouts: 3.67 us -> 6.45 us
    slice x1 -> x0, local copies, waits for them, and re-layouts: 1.14 us -> none  [local(): staying, crossing = attend(blocks, bias[:2 * rows], out_weight, 0, 2)]
    ppermute x9, starting transfers between devices: 7.73 us -> 6.61 us  [swap(): return lax.ppermute(x, 'seq', [(i, i ^ by) for i in range(size)])]
    pallas_call x2, Pallas kernels: 0.84 us -> 1.59 us  [cut(): pl.pallas_call(functools.partial(cut_kernel, js), out_shape=[jax.ShapeDty...]
    dot_general x1, matrix products: 1.74 us -> 1.04 us  [mask_bias(): seen = hot @ full.astype(jnp.float32) @ hot.T]
  transfers between devices with their start and end apart: 10 -> 12, of which waited for: 5 -> 9; matrix products, arithmetic and copies ran while one was open for 8% -> 5% of each run, Pallas kernels for 6% -> 6%
where the time goes in v4:
time: 44.9 us; the launch traced here: 44.6 us
  waiting for transfers between devices  14.9 us (33%)
  starting transfers between devices  12.4 us (28%)
  Pallas kernels  8.04 us (18%)
  local copies, waits for them, and re-layouts  6.54 us (15%)
  matrix products  1.04 us (2%)
  other arithmetic  0.97 us (2%)
  between operations  0.74 us (2%)
    ppermute x9, waiting for transfers between devices, swap(): return lax.ppermute(x, 'seq', [(i, i ^ by) for i in range(size)])  10.2 us
    ppermute x9, starting transfers between devices, swap(): return lax.ppermute(x, 'seq', [(i, i ^ by) for i in range(size)])  6.61 us
    unnamed x10, local copies, waits for them, and re-layouts  6.45 us
    ppermute x3, starting transfers between devices, onward(): return lax.ppermute(x, ('segment', 'seq'), pairs)  5.76 us
    ppermute x3, waiting for transfers between devices, onward(): return lax.ppermute(x, ('segment', 'seq'), pairs)  4.68 us
    pallas_call x1, Pallas kernels, project(): pl.pallas_call(functools.partial(project_kernel, n, tile), out_shape=[jax...  2.98 us
    pallas_call x2, Pallas kernels, attend(): pl.pallas_call(functools.partial(attend_kernel, n, js), out_shape=jax.Sha...  2.51 us
    pallas_call x2, Pallas kernels, cut(): pl.pallas_call(functools.partial(cut_kernel, js), out_shape=[jax.ShapeDty...  1.59 us
  transfers between devices with their start and end apart: 12, of which 9 were waited for; matrix products, arithmetic and copies ran while one was open for 5% of the time, Pallas kernels for 6%

profile of v4, /device:TPU:0, one launch (start us, length us, event | category | flops | bytes accessed | tf_op | source)
XLA Modules:
  0.0 44.6 jit_solution(7793181706647905734)
XLA Ops:
  0.6 1.1 %copy-done.1 = bf16[1,64,6144]{2,1,0:T(8,128)(2,1)S(1)} copy-done((bf16[1,64,6144]{2,1,0:T(8,128)(2,1)S(1)}, bf16[1,64,6144]{2,1,0:T(8,128)(2,1)}, u32[]{:S(2)}) %copy-start.1) | copy-done | bytes 786456
  1.8 0.8 %cut_slices.2 = (bf16[64,1536]{1,0:T(8,128)(2,1)}, bf16[64,1536]{1,0:T(8,128)(2,1)}) custom-call(bf16[1,64,6144]{2,1,0:T(8,128)(2,1)S(1)} %copy-done.1), custom_call_target="tpu_custom_call" | custom-call | tf_op jit(solution)/shard_map/cut_slices/pallas_call | solution.py:52
  2.6 2.5 %collective-permute-start.2 = (bf16[64,1536]{1,0:T(8,128)(2,1)}, bf16[64,1536]{1,0:T(8,128)(2,1)S(1)}, u32[]{:S(2)}, u32[]{:S(2)}) collective-permute-start(bf16[64,1536]{1,0:T(8,128)(2,1)} %get-tuple-element.22), channel_id=1, source_target_pairs={{0,3},{1,2},{2,1},{3,0},{4,7},{5,6},{6,5},{7,4},{8,11},{9,10},{10,... | collective-permute-start | bytes 589832 | tf_op jit(solution)/shard_map/ppermute | solution.py:24
  5.1 0.6 %collective-permute-start.1 = (bf16[64,1536]{1,0:T(8,128)(2,1)}, bf16[64,1536]{1,0:T(8,128)(2,1)S(1)}, u32[]{:S(2)}, u32[]{:S(2)}) collective-permute-start(bf16[64,1536]{1,0:T(8,128)(2,1)} %get-tuple-element.19.refs_0_), channel_id=1, source_target_pairs={{0,2},{1,3},{2,0},{3,1},{4,6},{5,7},{6,4},{7,5},{8,10},{9,11},{10,... | collective-permute-start | bytes 589832 | tf_op jit(solution)/shard_map/ppermute | solution.py:24
  5.7 0.8 %cut_slices.3 = (bf16[64,1536]{1,0:T(8,128)(2,1)S(1)}, bf16[64,1536]{1,0:T(8,128)(2,1)}) custom-call(bf16[1,64,6144]{2,1,0:T(8,128)(2,1)S(1)} %copy-done.1, bf16[64,1536]{1,0:T(8,128)(2,1)} %get-tuple-element.19.refs_0_), custom_call_target="tpu_custom_call" | custom-call | tf_op jit(solution)/shard_map/cut_slices/pallas_call | solution.py:52
  6.8 1.6 %copy-done.2 = bf16[1,512,2048]{2,1,0:T(8,128)(2,1)S(1)} copy-done((bf16[1,512,2048]{2,1,0:T(8,128)(2,1)S(1)}, bf16[1,512,2048]{2,1,0:T(8,128)(2,1)}, u32[]{:S(2)}) %copy-start.2) | copy-done | bytes 2097176
  8.4 0.9 %copy-done.3 = bf16[1,64,2048]{2,1,0:T(8,128)(2,1)S(1)} copy-done((bf16[1,64,2048]{2,1,0:T(8,128)(2,1)S(1)}, bf16[1,64,2048]{2,1,0:T(8,128)(2,1)}, u32[]{:S(2)}) %copy-start.3) | copy-done | bytes 262168
  9.5 0.9 %select_reduce_fusion = s32[256]{0:T(256)S(1)} fusion(s32[256]{0:T(256)S(1)} %and_select_fusion.1, s32[256]{0:T(256)} %param.13, s32[256]{0:T(256)S(1)} %add.43), kind=kLoop, calls=%fused_computation.4 | loop fusion | flops 196352 | bytes 4096 | tf_op jit(solution)/shard_map/reduce_sum | solution.py:262
  10.4 1.0 %fusion.refs_4_ = f32[256,256]{1,0:T(8,128)S(1)} fusion(s32[256]{0:T(256)S(1)} %select_reduce_fusion, s32[1,2,2]{2,1,0:T(2,128)} %param.12, s32[2]{0:T(128)S(1)} %and_select_fusion), kind=kOutput, calls=%fused_computation.1 | convolution fusion | flops 396300 | bytes 263192 | tf_op jit(solution)/shard_map/dot_general | solution.py:271
  11.4 3.5 %collective-permute-done.1.refs_2_ = bf16[64,1536]{1,0:T(8,128)(2,1)S(1)} collective-permute-done((bf16[64,1536]{1,0:T(8,128)(2,1)}, bf16[64,1536]{1,0:T(8,128)(2,1)S(1)}, u32[]{:S(2)}, u32[]{:S(2)}) %collective-permute-start.1) | collective-permute-done | bytes 196640 | tf_op jit(solution)/shard_map/ppermute | solution.py:24
  15.0 1.3 %attend_project.3 = bf16[128,2048]{1,0:T(8,128)(2,1)S(1)} custom-call(bf16[64,1536]{1,0:T(8,128)(2,1)S(1)} %get-tuple-element.20.refs_0_, bf16[64,1536]{1,0:T(8,128)(2,1)S(1)} %collective-permute-done.refs_1_, bf16[64,1536]{1,0:T(8,128)(2,1)S(1)} %collective-permute-done.1.refs_2_, bf16[64,1536]{1,0:T(8,128)(2,1)S(1)} %collective-permute-done.2.refs_3_, ...), custom_call_target="tpu_custom_call" | custom-call | flops 335544320 | bytes 2097152 | tf_op jit(solution)/shard_map/attend_project/pallas_call | solution.py:120
  16.3 1.3 %attend_project.2.mine = bf16[128,2048]{1,0:T(8,128)(2,1)S(1)} custom-call(bf16[64,1536]{1,0:T(8,128)(2,1)S(1)} %get-tuple-element.20.refs_0_, bf16[64,1536]{1,0:T(8,128)(2,1)S(1)} %collective-permute-done.refs_1_, bf16[64,1536]{1,0:T(8,128)(2,1)S(1)} %collective-permute-done.1.refs_2_, bf16[64,1536]{1,0:T(8,128)(2,1)S(1)} %collective-permute-done.2.refs_3_, ...), custom_call_target="tpu_custom_call" | custom-call | flops 335544320 | bytes 2097152 | tf_op jit(solution)/shard_map/attend_project/pallas_call | solution.py:120
  18.3 2.4 %collective-permute-start.5 = (bf16[64,1024]{1,0:T(8,128)(2,1)S(1)}, bf16[64,1024]{1,0:T(8,128)(2,1)S(1)}, u32[]{:S(2)}, u32[]{:S(2)}) collective-permute-start(bf16[64,1024]{1,0:T(8,128)(2,1)S(1)} %get-tuple-element.27), channel_id=1, source_target_pairs={{0,2},{1,3},{2,0},{3,1},{4,6},{5,7},{6,4},{7,5},{8,10},{9,11},{10,... | collective-permute-start | bytes 393224 | tf_op jit(solution)/shard_map/ppermute | solution.py:24
  20.7 1.5 %collective-permute-start.4 = (bf16[128,1024]{1,0:T(8,128)(2,1)S(1)}, bf16[128,1024]{1,0:T(8,128)(2,1)S(1)}, u32[]{:S(2)}, u32[]{:S(2)}) collective-permute-start(bf16[128,1024]{1,0:T(8,128)(2,1)S(1)} %get-tuple-element.25), channel_id=1, source_target_pairs={{0,4},{1,5},{2,6},{3,7},{4,8},{5,9},{6,10},{7,11},{8,12},{9,13},{1... | collective-permute-start | bytes 786440 | tf_op jit(solution)/shard_map/ppermute | solution.py:32
  22.2 2.3 %collective-permute-done.5 = bf16[64,1024]{1,0:T(8,128)(2,1)S(1)} collective-permute-done((bf16[64,1024]{1,0:T(8,128)(2,1)S(1)}, bf16[64,1024]{1,0:T(8,128)(2,1)S(1)}, u32[]{:S(2)}, u32[]{:S(2)}) %collective-permute-start.5) | collective-permute-done | bytes 131104 | tf_op jit(solution)/shard_map/ppermute | solution.py:24
  24.5 2.7 %collective-permute-start.8 = (bf16[64,1024]{1,0:T(8,128)(2,1)S(1)}, bf16[64,1024]{1,0:T(8,128)(2,1)S(1)}, u32[]{:S(2)}, u32[]{:S(2)}) collective-permute-start(bf16[64,1024]{1,0:T(8,128)(2,1)S(1)} %add_convert_fusion.after), channel_id=1, source_target_pairs={{0,6},{1,7},{2,4},{3,5},{4,10},{5,11},{6,8},{7,9},{8,14},{9,15},{1... | collective-permute-start | bytes 393224 | tf_op jit(solution)/shard_map/ppermute | solution.py:32
  27.3 1.5 %collective-permute-start.7 = (bf16[64,1024]{1,0:T(8,128)(2,1)S(1)}, bf16[64,1024]{1,0:T(8,128)(2,1)S(1)}, u32[]{:S(2)}, u32[]{:S(2)}) collective-permute-start(bf16[64,1024]{1,0:T(8,128)(2,1)S(1)} %add_convert_fusion.after), channel_id=1, source_target_pairs={{0,4},{1,5},{2,6},{3,7},{4,8},{5,9},{6,10},{7,11},{8,12},{9,13},{1... | collective-permute-start | bytes 393224 | tf_op jit(solution)/shard_map/ppermute | solution.py:32
  28.8 3.8 %collective-permute-done.4.x = bf16[128,1024]{1,0:T(8,128)(2,1)S(1)} collective-permute-done((bf16[128,1024]{1,0:T(8,128)(2,1)S(1)}, bf16[128,1024]{1,0:T(8,128)(2,1)S(1)}, u32[]{:S(2)}, u32[]{:S(2)}) %collective-permute-start.4) | collective-permute-done | bytes 262176 | tf_op jit(solution)/shard_map/ppermute | solution.py:32
  33.0 2.8 %copy-done = bf16[1,2048,1536]{2,1,0:T(8,128)(2,1)S(1)} copy-done((bf16[1,2048,1536]{2,1,0:T(8,128)(2,1)S(1)}, bf16[1,2048,1536]{2,1,0:T(8,128)(2,1)}, u32[]{:S(2)}) %copy-start) | copy-done | bytes 6291480
  36.3 0.9 %collective-permute-done.7.refs_0_ = bf16[64,1024]{1,0:T(8,128)(2,1)S(1)} collective-permute-done((bf16[64,1024]{1,0:T(8,128)(2,1)S(1)}, bf16[64,1024]{1,0:T(8,128)(2,1)S(1)}, u32[]{:S(2)}, u32[]{:S(2)}) %collective-permute-start.7) | collective-permute-done | bytes 131104 | tf_op jit(solution)/shard_map/ppermute | solution.py:32
  37.7 0.8 %collective-permute-done.9.refs_1_ = bf16[64,1024]{1,0:T(8,128)(2,1)S(1)} collective-permute-done((bf16[64,1024]{1,0:T(8,128)(2,1)S(1)}, bf16[64,1024]{1,0:T(8,128)(2,1)S(1)}, u32[]{:S(2)}, u32[]{:S(2)}) %collective-permute-start.9) | collective-permute-done | bytes 131104 | tf_op jit(solution)/shard_map/ppermute | solution.py:24
  38.7 1.2 %collective-permute-done.6.refs_0_ = bf16[128,1024]{1,0:T(8,128)(2,1)S(1)} collective-permute-done((bf16[128,1024]{1,0:T(8,128)(2,1)S(1)}, bf16[128,1024]{1,0:T(8,128)(2,1)S(1)}, u32[]{:S(2)}, u32[]{:S(2)}) %collective-permute-start.6) | collective-permute-done | bytes 262176 | tf_op jit(solution)/shard_map/ppermute | solution.py:24
  40.1 1.5 %collective-permute-done.11.odd = bf16[128,1024]{1,0:T(8,128)(2,1)S(1)} collective-permute-done((bf16[128,1024]{1,0:T(8,128)(2,1)S(1)}, bf16[128,1024]{1,0:T(8,128)(2,1)S(1)}, u32[]{:S(2)}, u32[]{:S(2)}) %collective-permute-start.11) | collective-permute-done | bytes 262176 | tf_op jit(solution)/shard_map/ppermute | solution.py:24
  41.6 3.0 %norm_project.1 = (bf16[1,64,2048]{2,1,0:T(8,128)(2,1)}, bf16[1,256,1536]{2,1,0:T(8,128)(2,1)}) custom-call(bf16[128,1024]{1,0:T(8,128)(2,1)S(1)} %join_chips.1.even, bf16[128,1024]{1,0:T(8,128)(2,1)S(1)} %collective-permute-done.11.odd, bf16[64,1024]{1,0:T(8,128)(2,1)S(1)} %collective-permute-done.7.refs_0_, ...), custom_call_target="tpu_custom_call" | custom-call | flops 1610612736 | bytes 6291456 | tf_op jit(solution)/shard_map/norm_project/pallas_call | solution.py:232
  (28 shorter events, 3.1 us)
Async XLA Ops:
  0.6 1.1 %copy-start.1 = (bf16[1,64,6144]{2,1,0:T(8,128)(2,1)S(1)}, bf16[1,64,6144]{2,1,0:T(8,128)(2,1)}, u32[]{:S(2)}) copy-start(bf16[1,64,6144]{2,1,0:T(8,128)(2,1)} %src.3) | copy-start | bytes 2359300
  2.6 8.8 %collective-permute-start.2 = (bf16[64,1536]{1,0:T(8,128)(2,1)}, bf16[64,1536]{1,0:T(8,128)(2,1)S(1)}, u32[]{:S(2)}, u32[]{:S(2)}) collective-permute-start(bf16[64,1536]{1,0:T(8,128)(2,1)} %get-tuple-element.22), channel_id=1, source_target_pairs={{0,3},{1,2},{2,1},{3,0},{4,7},{5,6},{6,5},{7,4},{8,11},{9,10},{10,... | collective-permute-start | bytes 589832 | tf_op jit(solution)/shard_map/ppermute | solution.py:24
  5.1 9.9 %collective-permute-start.1 = (bf16[64,1536]{1,0:T(8,128)(2,1)}, bf16[64,1536]{1,0:T(8,128)(2,1)S(1)}, u32[]{:S(2)}, u32[]{:S(2)}) collective-permute-start(bf16[64,1536]{1,0:T(8,128)(2,1)} %get-tuple-element.19.refs_0_), channel_id=1, source_target_pairs={{0,2},{1,3},{2,0},{3,1},{4,6},{5,7},{6,4},{7,5},{8,10},{9,11},{10,... | collective-permute-start | bytes 589832 | tf_op jit(solution)/shard_map/ppermute | solution.py:24
  6.5 8.5 %collective-permute-start = (bf16[64,1536]{1,0:T(8,128)(2,1)}, bf16[64,1536]{1,0:T(8,128)(2,1)S(1)}, u32[]{:S(2)}, u32[]{:S(2)}) collective-permute-start(bf16[64,1536]{1,0:T(8,128)(2,1)} %get-tuple-element.21), channel_id=1, source_target_pairs={{0,1},{1,0},{2,3},{3,2},{4,5},{5,4},{6,7},{7,6},{8,9},{9,8},{10,11... | collective-permute-start | bytes 589832 | tf_op jit(solution)/shard_map/ppermute | solution.py:24
  6.8 1.6 %copy-start.2 = (bf16[1,512,2048]{2,1,0:T(8,128)(2,1)S(1)}, bf16[1,512,2048]{2,1,0:T(8,128)(2,1)}, u32[]{:S(2)}) copy-start(bf16[1,512,2048]{2,1,0:T(8,128)(2,1)} %refs_1_.1) | copy-start | bytes 6291460
  8.4 0.9 %copy-start.3 = (bf16[1,64,2048]{2,1,0:T(8,128)(2,1)S(1)}, bf16[1,64,2048]{2,1,0:T(8,128)(2,1)}, u32[]{:S(2)}) copy-start(bf16[1,64,2048]{2,1,0:T(8,128)(2,1)} %refs_0_.2) | copy-start | bytes 786436
  16.2 2.0 %collective-permute-start.3 = (bf16[128,2048]{1,0:T(8,128)(2,1)S(1)}, bf16[128,2048]{1,0:T(8,128)(2,1)S(1)}, u32[]{:S(2)}, u32[]{:S(2)}) collective-permute-start(bf16[128,2048]{1,0:T(8,128)(2,1)S(1)} %attend_project.3), channel_id=1, source_target_pairs={{0,1},{1,0},{2,3},{3,2},{4,5},{5,4},{6,7},{7,6},{8,9},{9,8},{10,11... | collective-permute-start | bytes 1572872 | tf_op jit(solution)/shard_map/ppermute | solution.py:24
  18.3 6.2 %collective-permute-start.5 = (bf16[64,1024]{1,0:T(8,128)(2,1)S(1)}, bf16[64,1024]{1,0:T(8,128)(2,1)S(1)}, u32[]{:S(2)}, u32[]{:S(2)}) collective-permute-start(bf16[64,1024]{1,0:T(8,128)(2,1)S(1)} %get-tuple-element.27), channel_id=1, source_target_pairs={{0,2},{1,3},{2,0},{3,1},{4,6},{5,7},{6,4},{7,5},{8,10},{9,11},{10,... | collective-permute-start | bytes 393224 | tf_op jit(solution)/shard_map/ppermute | solution.py:24
  20.7 11.9 %collective-permute-start.4 = (bf16[128,1024]{1,0:T(8,128)(2,1)S(1)}, bf16[128,1024]{1,0:T(8,128)(2,1)S(1)}, u32[]{:S(2)}, u32[]{:S(2)}) collective-permute-start(bf16[128,1024]{1,0:T(8,128)(2,1)S(1)} %get-tuple-element.25), channel_id=1, source_target_pairs={{0,4},{1,5},{2,6},{3,7},{4,8},{5,9},{6,10},{7,11},{8,12},{9,13},{1... | collective-permute-start | bytes 786440 | tf_op jit(solution)/shard_map/ppermute | solution.py:32
  24.5 11.7 %collective-permute-start.8 = (bf16[64,1024]{1,0:T(8,128)(2,1)S(1)}, bf16[64,1024]{1,0:T(8,128)(2,1)S(1)}, u32[]{:S(2)}, u32[]{:S(2)}) collective-permute-start(bf16[64,1024]{1,0:T(8,128)(2,1)S(1)} %add_convert_fusion.after), channel_id=1, source_target_pairs={{0,6},{1,7},{2,4},{3,5},{4,10},{5,11},{6,8},{7,9},{8,14},{9,15},{1... | collective-permute-start | bytes 393224 | tf_op jit(solution)/shard_map/ppermute | solution.py:32
  27.3 9.9 %collective-permute-start.7 = (bf16[64,1024]{1,0:T(8,128)(2,1)S(1)}, bf16[64,1024]{1,0:T(8,128)(2,1)S(1)}, u32[]{:S(2)}, u32[]{:S(2)}) collective-permute-start(bf16[64,1024]{1,0:T(8,128)(2,1)S(1)} %add_convert_fusion.after), channel_id=1, source_target_pairs={{0,4},{1,5},{2,6},{3,7},{4,8},{5,9},{6,10},{7,11},{8,12},{9,13},{1... | collective-permute-start | bytes 393224 | tf_op jit(solution)/shard_map/ppermute | solution.py:32
  32.6 7.3 %collective-permute-start.6 = (bf16[128,1024]{1,0:T(8,128)(2,1)S(1)}, bf16[128,1024]{1,0:T(8,128)(2,1)S(1)}, u32[]{:S(2)}, u32[]{:S(2)}) collective-permute-start(bf16[128,1024]{1,0:T(8,128)(2,1)S(1)} %settle.1.refs_1_.mine), channel_id=1, source_target_pairs={{0,2},{1,3},{2,0},{3,1},{4,6},{5,7},{6,4},{7,5},{8,10},{9,11},{10,... | collective-permute-start | bytes 786440 | tf_op jit(solution)/shard_map/ppermute | solution.py:24
  33.0 2.8 %copy-start = (bf16[1,2048,1536]{2,1,0:T(8,128)(2,1)S(1)}, bf16[1,2048,1536]{2,1,0:T(8,128)(2,1)}, u32[]{:S(2)}) copy-start(bf16[1,2048,1536]{2,1,0:T(8,128)(2,1)} %refs_0_.3) | copy-start | bytes 18874372
  35.7 5.9 %copy-start.4 = (f32[1,2048]{1,0:T(1,128)S(1)}, f32[1,2048]{1,0:T(1,128)}, u32[]{:S(2)}) copy-start(f32[1,2048]{1,0:T(1,128)} %refs_4_.1) | copy-start | bytes 24580
  37.2 1.3 %collective-permute-start.9 = (bf16[64,1024]{1,0:T(8,128)(2,1)S(1)}, bf16[64,1024]{1,0:T(8,128)(2,1)S(1)}, u32[]{:S(2)}, u32[]{:S(2)}) collective-permute-start(bf16[64,1024]{1,0:T(8,128)(2,1)S(1)} %collective-permute-done.7.refs_0_), channel_id=1, source_target_pairs={{0,1},{1,0},{2,3},{3,2},{4,5},{5,4},{6,7},{7,6},{8,9},{9,8},{10,11... | collective-permute-start | bytes 393224 | tf_op jit(solution)/shard_map/ppermute | solution.py:24
  37.2 1.5 %collective-permute-start.10 = (bf16[64,1024]{1,0:T(8,128)(2,1)S(1)}, bf16[64,1024]{1,0:T(8,128)(2,1)S(1)}, u32[]{:S(2)}, u32[]{:S(2)}) collective-permute-start(bf16[64,1024]{1,0:T(8,128)(2,1)S(1)} %collective-permute-done.8.refs_2_), channel_id=1, source_target_pairs={{0,1},{1,0},{2,3},{3,2},{4,5},{5,4},{6,7},{7,6},{8,9},{9,8},{10,11... | collective-permute-start | bytes 393224 | tf_op jit(solution)/shard_map/ppermute | solution.py:24
  40.0 1.6 %collective-permute-start.11 = (bf16[128,1024]{1,0:T(8,128)(2,1)S(1)}, bf16[128,1024]{1,0:T(8,128)(2,1)S(1)}, u32[]{:S(2)}, u32[]{:S(2)}) collective-permute-start(bf16[128,1024]{1,0:T(8,128)(2,1)S(1)} %join_chips.1.even), channel_id=1, source_target_pairs={{0,1},{1,0},{2,3},{3,2},{4,5},{5,4},{6,7},{7,6},{8,9},{9,8},{10,11... | collective-permute-start | bytes 786440 | tf_op jit(solution)/shard_map/ppermute | solution.py:24

commit v5 on v4

v5 whole, which is shorter than its diff:
```python
import functools
import math

import jax
import jax.numpy as jnp
from jax import lax
from jax.experimental import pallas as pl
from jax.experimental.pallas import tpu as pltpu
from jax.sharding import PartitionSpec as P

HEADS = 16
DH = 128
WIN = 256
BLOCK = 128
NEG = -1e30
VMEM_LIMIT = 16 * 1024 * 1024
SMALL_LIMIT = 4 * 1024 * 1024

VM = pl.BlockSpec(memory_space=pltpu.VMEM)
ANY = pl.BlockSpec(memory_space=pltpu.HBM)


def swap(x, by):
    size = lax.axis_size("seq")
    return lax.ppermute(x, "seq", [(i, i ^ by) for i in range(size)])


def onward(x, by):
    sections, size = lax.axis_size("segment"), lax.axis_size("seq")
    pairs = [
        (s * size + t, (s + 1) % sections * size + (t ^ by)) for s in range(sections) for t in range(size)
    ]
    return lax.ppermute(x, ("segment", "seq"), pairs)


def cut_kernel(js, src, *refs):
    outs, sems = refs[-1 - len(js) : -1], refs[-1]
    width = outs[0].shape[1]
    me = lax.axis_index("seq")
    copies = []
    for at, j in enumerate(js):
        first = pl.multiple_of((me ^ j) * width, 128)
        copies.append(pltpu.make_async_copy(src.at[0, :, pl.ds(first, width)], outs[at], sems.at[at]))
    for c in copies:
        c.start()
    for c in copies:
        c.wait()


def cut(projected, n, js, after=()):
    _, rows, columns = projected.shape
    width = columns // n
    return pl.pallas_call(
        functools.partial(cut_kernel, js),
        out_shape=[pltpu.VMEM((rows, width), projected.dtype)] * len(js),
        in_specs=[ANY] * (1 + len(after)),
        out_specs=[VM] * len(js),
        scratch_shapes=[pltpu.SemaphoreType.DMA((len(js),))],
        compiler_params=pltpu.CompilerParams(vmem_limit_bytes=SMALL_LIMIT),
        name="cut_slices",
    )(pltpu.with_memory_space_constraint(projected, pltpu.HBM), *after)


def load_kernel(pieces, *refs):
    count = len(pieces)
    ins, outs, sems = refs[:count], refs[-1 - count : -1], refs[-1]
    copies = []
    for i, many in enumerate(pieces):
        step = ins[i].shape[1] // many
        for p in range(many):
            part = (slice(None), pl.ds(p * step, step))
            copies.append(pltpu.make_async_copy(ins[i].at[part], outs[i].at[part], sems.at[len(copies)]))
    for c in copies:
        c.start()
    for c in copies:
        c.wait()


def load(arrays, pieces, after=(), cost=0):
    return pl.pallas_call(
        functools.partial(load_kernel, pieces),
        out_shape=[pltpu.VMEM(a.shape, a.dtype) for a in arrays],
        in_specs=[ANY] * (len(arrays) + len(after)),
        out_specs=[VM] * len(arrays),
        scratch_shapes=[pltpu.SemaphoreType.DMA((sum(pieces),))],
        compiler_params=pltpu.CompilerParams(vmem_limit_bytes=SMALL_LIMIT),
        cost_estimate=pl.CostEstimate(
            flops=0, bytes_accessed=cost, transcendentals=0
        ),
        name="load_weights",
    )(*[pltpu.with_memory_space_constraint(a, pltpu.HBM) for a in arrays], *after)


def attention(blocks, bias, js):
    rows, width = blocks[0].shape
    seen = jnp.concatenate([bias[j * rows : (j + 1) * rows] for j in js], axis=0)
    attended = []
    for h in range(width // (3 * DH)):
        c = h * 3 * DH
        q = jnp.concatenate([blocks[j][:, c : c + DH] for j in js], axis=0)
        k = jnp.concatenate([b[:, c + DH : c + 2 * DH] for b in blocks], axis=0)
        v = jnp.concatenate([b[:, c + 2 * DH : c + 3 * DH] for b in blocks], axis=0)
        s = lax.dot_general(q, k, (((1,), (1,)), ((), ())), preferred_element_type=jnp.float32) + seen
        e = jnp.exp2((s - jnp.max(s, axis=-1, keepdims=True)) * (DH ** (-0.5) * math.log2(math.e)))
        mixed = jnp.dot(e.astype(jnp.bfloat16), v, preferred_element_type=jnp.float32)
        attended.append((mixed * (1.0 / jnp.sum(e, axis=-1, keepdims=True))).astype(jnp.bfloat16))
    return jnp.concatenate(attended, axis=1)


def attend_kernel(n, js, *refs):
    blocks, bias, out = refs[:2] + refs[2:n][::-1], refs[n], refs[n + 1]
    out[...] = attention(blocks, bias, js)


def attend_project_kernel(n, js, *refs):
    blocks, bias, weight, out = refs[:2] + refs[2:n][::-1], refs[n], refs[n + 1], refs[n + 2]
    out[...] = jnp.dot(attention(blocks, bias, js), weight[0], preferred_element_type=jnp.float32)


def attend(blocks, bias, js, weight=None):
    n = len(blocks)
    rows, width = blocks[0].shape
    depth = width // 3
    queries = len(js) * rows
    made = (attend_kernel, depth, jnp.bfloat16) if weight is None else (attend_project_kernel, weight.shape[2], jnp.float32)
    return pl.pallas_call(
        functools.partial(made[0], n, js),
        out_shape=jax.ShapeDtypeStruct((queries, made[1]), made[2]),
        in_specs=[VM] * (n + 1 + (weight is not None)),
        out_specs=VM,
        compiler_params=pltpu.CompilerParams(vmem_limit_bytes=VMEM_LIMIT),
        cost_estimate=pl.CostEstimate(
            flops=4 * queries * depth * n * rows + (0 if weight is None else 2 * queries * depth * weight.shape[2]),
            bytes_accessed=2 * n * rows * width,
            transcendentals=queries * n * rows * depth // DH,
        ),
        name="attend" if weight is None else "attend_project",
    )(*blocks[:2], *blocks[2:][::-1], bias, *(() if weight is None else (weight,)))


def chip_sum_kernel(rows, cols, mine, theirs, weight, stream, partial, own, *others):
    total = mine[...] + jnp.dot(theirs[...], weight[0], preferred_element_type=jnp.float32)
    for i in range(mine.shape[0] // rows):
        part = slice(i * rows, (i + 1) * rows)
        here = total[part]
        if i == 0:
            here = here + stream[0].astype(jnp.float32)
            own[...] = here[:, cols:]
        else:
            others[i - 1][...] = here[:, cols:].astype(jnp.bfloat16)
        partial[part, :] = here[:, :cols].astype(jnp.bfloat16)


def chip_sum(mine, theirs, weight, stream, cols):
    rows = stream.shape[1]
    count, depth = mine.shape
    rest = (rows, depth - cols)
    return pl.pallas_call(
        functools.partial(chip_sum_kernel, rows, cols),
        out_shape=[
            jax.ShapeDtypeStruct((count, cols), jnp.bfloat16),
            jax.ShapeDtypeStruct(rest, jnp.float32),
        ]
        + [jax.ShapeDtypeStruct(rest, jnp.bfloat16)] * (count // rows - 1),
        in_specs=[VM] * 4,
        out_specs=[VM] * (count // rows + 1),
        compiler_params=pltpu.CompilerParams(vmem_limit_bytes=VMEM_LIMIT),
        name="chip_sum",
    )(mine, theirs, weight, stream)


def join_kernel(rows, mine, *refs):
    others, out = refs[:-1], refs[-1]
    for i in range(mine.shape[0] // rows):
        total = mine[i * rows : (i + 1) * rows, :].astype(jnp.float32)
        for k, other in enumerate(others):
            at = i ^ (k + 1)
            total = total + other[at * rows : (at + 1) * rows, :].astype(jnp.float32)
        out[i * rows : (i + 1) * rows, :] = total.astype(jnp.bfloat16)


def join(rows, mine, others):
    return pl.pallas_call(
        functools.partial(join_kernel, rows),
        out_shape=jax.ShapeDtypeStruct(mine.shape, mine.dtype),
        in_specs=[VM] * (1 + len(others)),
        out_specs=VM,
        compiler_params=pltpu.CompilerParams(vmem_limit_bytes=SMALL_LIMIT),
        name="join_chips",
    )(mine, *others)


def settle_kernel(x, after, out):
    out[...] = x[...]


def settle(x, after):
    return pl.pallas_call(
        settle_kernel,
        out_shape=jax.ShapeDtypeStruct(x.shape, x.dtype),
        in_specs=[VM, ANY],
        out_specs=VM,
        compiler_params=pltpu.CompilerParams(vmem_limit_bytes=SMALL_LIMIT),
        name="settle",
    )(x, after)


def project_first_kernel(n, *refs):
    rest, gain, weight, total, squares, scaled = refs[:n], *refs[n:]
    rows, count = rest[0].shape
    cols = weight.shape[1] - count
    me = lax.axis_index("seq")
    for j in range(n):
        x = rest[j][...].astype(jnp.float32)
        here = pl.ds(pl.multiple_of((me ^ j) * rows, rows), rows)
        squares[here, :] = jnp.sum(x * x, axis=-1, keepdims=True)
        scaled[here, :] = (x * gain[:, cols:]).astype(jnp.bfloat16)
    total[...] = jnp.dot(scaled[...], weight[0, cols:, :], preferred_element_type=jnp.float32)


def project_first(rest, gain, weight):
    n = len(rest)
    rows, count = rest[0].shape
    width = weight.shape[2]
    tokens = n * rows
    return pl.pallas_call(
        functools.partial(project_first_kernel, n),
        out_shape=[
            jax.ShapeDtypeStruct((tokens, width), jnp.float32),
            jax.ShapeDtypeStruct((tokens, 1), jnp.float32),
        ],
        in_specs=[VM] * (n + 2),
        out_specs=[VM, VM],
        scratch_shapes=[pltpu.VMEM((tokens, count), jnp.bfloat16)],
        compiler_params=pltpu.CompilerParams(vmem_limit_bytes=VMEM_LIMIT),
        cost_estimate=pl.CostEstimate(
            flops=2 * tokens * count * width, bytes_accessed=2 * count * width, transcendentals=0
        ),
        name="project_first",
    )(*rest, gain, weight)


def project_second_kernel(n, tile, even, odd, rest, gain, weight, total, squares, kept, out, scaled, sums, made, sems):
    rows, cols = rest.shape[0], even.shape[1]
    depth, width = weight.shape[1:]
    me = lax.axis_index("seq")
    copies = [
        pltpu.make_async_copy(even.at[:rows], kept.at[0, :, pl.ds(0, cols)], sems.at[0]),
        pltpu.make_async_copy(rest, kept.at[0, :, pl.ds(cols, depth - cols)], sems.at[1]),
    ]
    for c in copies:
        c.start()
    for j in range(n):
        x = (odd if j % 2 else even)[j // 2 * rows : (j // 2 + 1) * rows, :].astype(jnp.float32)
        here = pl.ds(pl.multiple_of((me ^ j) * rows, rows), rows)
        sums[here, :] = squares[here, :] + jnp.sum(x * x, axis=-1, keepdims=True)
        scaled[here, :] = (x * gain[:, :cols]).astype(jnp.bfloat16)
    scale = lax.rsqrt(sums[...] / depth + 1e-06)
    for i in range(width // tile):
        part = pl.ds(i * tile, tile)
        mine = jnp.dot(scaled[...], weight[0, :cols, part], preferred_element_type=jnp.float32)
        made[:, part] = ((total[:, part] + mine) * scale).astype(jnp.bfloat16)
        copies.append(pltpu.make_async_copy(made.at[:, part], out.at[0, :, part], sems.at[2 + i]))
        copies[-1].start()
    for c in copies:
        c.wait()


def project_second(n, even, odd, rest, gain, weight, total, squares):
    rows = rest.shape[0]
    cols = even.shape[1]
    _, depth, width = weight.shape
    tile = 256 if width % 256 == 0 else 128
    return pl.pallas_call(
        functools.partial(project_second_kernel, n, tile),
        out_shape=[
            jax.ShapeDtypeStruct((1, rows, depth), jnp.bfloat16),
            jax.ShapeDtypeStruct((1, n * rows, width), jnp.bfloat16),
        ],
        in_specs=[VM] * 7,
        out_specs=[ANY, ANY],
        scratch_shapes=[
            pltpu.VMEM((n * rows, cols), jnp.bfloat16),
            pltpu.VMEM((n * rows, 1), jnp.float32),
            pltpu.VMEM((n * rows, width), jnp.bfloat16),
            pltpu.SemaphoreType.DMA((2 + width // tile,)),
        ],
        compiler_params=pltpu.CompilerParams(vmem_limit_bytes=VMEM_LIMIT),
        cost_estimate=pl.CostEstimate(
            flops=2 * n * rows * cols * width, bytes_accessed=2 * cols * width, transcendentals=0
        ),
        name="project_second",
    )(even, odd, rest, gain, weight, total, squares)


def mask_kernel(rows, mask, order, out):
    tokens = out.shape[0]
    windows, per, _ = mask.shape
    lanes = max(windows * per, 128)
    me = lax.axis_index("seq")
    row = lax.broadcasted_iota(jnp.int32, (tokens, tokens), 0)
    token = ((row // rows) ^ me) * rows + row % rows
    at = (order[...].reshape(1, tokens) == token).astype(jnp.bfloat16)
    position = lax.broadcasted_iota(jnp.int32, (tokens, lanes), 0)
    lane = lax.broadcasted_iota(jnp.int32, (tokens, lanes), 1)
    block = jnp.dot(
        at, (position // BLOCK == lane).astype(jnp.bfloat16), preferred_element_type=jnp.float32
    ).astype(jnp.bfloat16)
    first = lax.broadcasted_iota(jnp.int32, (lanes, lanes), 0)
    second = lax.broadcasted_iota(jnp.int32, (lanes, lanes), 1)
    visible = jnp.zeros((lanes, lanes), jnp.int32)
    for w in range(windows):
        for i in range(per):
            for j in range(per):
                here = (first == w * per + i) & (second == w * per + j)
                visible = jnp.where(here, mask[w, i, j], visible)
    visible = (visible > 0).astype(jnp.bfloat16)
    reach = jnp.dot(block, visible, preferred_element_type=jnp.float32).astype(jnp.bfloat16)
    seen = lax.dot_general(reach, block, (((1,), (1,)), ((), ())), preferred_element_type=jnp.float32)
    out[...] = jnp.where(seen > 0.5, 0.0, NEG)


def mask_bias(block_mask, token_order, n, rows):
    tokens = n * rows
    return pl.pallas_call(
        functools.partial(mask_kernel, rows),
        out_shape=jax.ShapeDtypeStruct((tokens, tokens), jnp.float32),
        in_specs=[pl.BlockSpec(memory_space=pltpu.SMEM), VM],
        out_specs=VM,
        compiler_params=pltpu.CompilerParams(vmem_limit_bytes=SMALL_LIMIT + 24 * tokens * tokens),
        name="mask_bias",
    )(block_mask, token_order)


def local(projected, stream_before, out_weight, proj_weight, norm_gain, block_mask, token_order):
    n = lax.axis_size("seq")
    rows = projected.shape[1]
    far_cut = cut(projected, n, tuple(range(2, n)))
    far = [swap(far_cut[j - 2], j) for j in range(2, n)]
    near_cut = cut(projected, n, (0, 1), (far_cut[0],))
    blocks = [near_cut[0], swap(near_cut[1], 1)] + far
    beside_weight = swap(out_weight, 1)
    stream, out_weight = load((stream_before, out_weight), (1, 4), (near_cut[0],))
    bias = mask_bias(block_mask, token_order, n, rows)
    bias, out_weight = lax.optimization_barrier((bias, out_weight))
    crossing = attend(blocks, bias, tuple(range(1, n, 2)))
    staying = attend(blocks, bias, tuple(range(0, n, 2)), out_weight)
    cols = out_weight.shape[2] * 7 // 16
    partial, own, *others = chip_sum(staying, swap(crossing, 1), beside_weight, stream, cols)
    partial = onward(partial, 0)
    total = own
    for k, x in enumerate(others):
        total = total + swap(x, 2 * k + 2).astype(jnp.float32)
    total = total.astype(jnp.bfloat16)
    rest = [onward(total, j) for j in range(0, n, 2)]
    partial = settle(partial, total)
    swapped = [swap(partial, j) for j in range(2, n, 2)]
    (proj_weight,) = load((proj_weight,), (8,), (partial,), 2 * proj_weight.size)
    rest, proj_weight = lax.optimization_barrier((rest, proj_weight))
    rest = [r for x in rest for r in (x, swap(x, 1))]
    swapped, rest = lax.optimization_barrier((swapped, rest))
    even = join(rows, partial, swapped)
    odd = swap(even, 1)
    total, squares = project_first(rest, norm_gain, proj_weight)
    kept, following = project_second(n, even, odd, rest[0], norm_gain, proj_weight, total, squares)
    return (kept, following)


def solution(mesh):
    placed = (
        P("segment", "seq", None),
        P("segment", "seq", None),
        P("segment", "seq", None),
        P("segment", None, "seq"),
        P("segment", None),
        P(),
        P(),
    )
    return jax.shard_map(
        local,
        mesh=mesh,
        in_specs=placed,
        out_specs=(P("segment", "seq", None), P("segment", None, "seq")),
        check_vma=False,
    )
```

time: 44.9 us -> 41.1 us (0.915)
  local copies, waits for them, and re-layouts: 6.54 us -> 1.36 us
  Pallas kernels: 8.04 us -> 13.1 us
  waiting for transfers between devices: 14.9 us -> 13.5 us
  matrix products: 1.04 us -> 0 us
  other arithmetic: 0.97 us -> 0.03 us
    unnamed x10 -> x6, local copies, waits for them, and re-layouts: 6.45 us -> 1.36 us
    pallas_call x7 -> x9, Pallas kernels: 7.81 us -> 12.6 us  [the longest x2 4.5 us: load(): pl.pallas_call(functools.partial(load_kernel, pieces), out_shape=[pltpu.V...]
    ppermute x9 -> x10, waiting for transfers between devices: 10.2 us -> 8.91 us  [swap(): return lax.ppermute(x, 'seq', [(i, i ^ by) for i in range(size)])]
    dot_general x1 -> x0, matrix products: 1.04 us -> none  [mask_bias(): seen = hot @ full.astype(jnp.float32) @ hot.T]
    reduce_sum x1 -> x0, other arithmetic: 0.86 us -> none  [mask_bias(): jnp.sum(jnp.where(token_order[None, :] == token[:, None], block[None, :],...]
    ppermute x9 -> x10, starting transfers between devices: 6.61 us -> 6.46 us  [swap(): return lax.ppermute(x, 'seq', [(i, i ^ by) for i in range(size)])]
  transfers between devices with their start and end apart: 12 -> 13, of which waited for: 9 -> 10; matrix products, arithmetic and copies ran while one was open for 5% -> 0% of each run, Pallas kernels for 6% -> 26%
where the time goes in v5:
time: 41.1 us; the launch traced here: 40.8 us
  waiting for transfers between devices  13.5 us (33%)
  Pallas kernels  13.1 us (32%)
  starting transfers between devices  12.1 us (29%)
  local copies, waits for them, and re-layouts  1.36 us (3%)
  between operations  0.74 us (2%)
    ppermute x10, waiting for transfers between devices, swap(): return lax.ppermute(x, 'seq', [(i, i ^ by) for i in range(size)])  8.91 us
    ppermute x10, starting transfers between devices, swap(): return lax.ppermute(x, 'seq', [(i, i ^ by) for i in range(size)])  6.46 us
    ppermute x3, starting transfers between devices, onward(): return lax.ppermute(x, ('segment', 'seq'), pairs)  5.67 us
    ppermute x3, waiting for transfers between devices, onward(): return lax.ppermute(x, ('segment', 'seq'), pairs)  4.55 us
    pallas_call x2, Pallas kernels, load(): pl.pallas_call(functools.partial(load_kernel, pieces), out_shape=[pltpu.V...  4.5 us
    pallas_call x2, Pallas kernels, cut(): pl.pallas_call(functools.partial(cut_kernel, js), out_shape=[pltpu.VMEM((...  2.08 us
    pallas_call x1, Pallas kernels, project_second(): pl.pallas_call(functools.partial(project_second_kernel, n, tile), out_sha...  1.93 us
    pallas_call x2, Pallas kernels, attend(): pl.pallas_call(functools.partial(made[0], n, js), out_shape=jax.ShapeDtyp...  1.76 us
  transfers between devices with their start and end apart: 13, of which 10 were waited for; matrix products, arithmetic and copies ran while one was open for 0% of the time, Pallas kernels for 26%

profile of v5, /device:TPU:0, one launch (start us, length us, event | category | flops | bytes accessed | tf_op | source)
XLA Modules:
  0.0 40.8 jit_solution(18421221465598644920)
XLA Ops:
  0.6 0.5 %collective-permute-start.4 = (bf16[1,512,2048]{2,1,0:T(8,128)(2,1)}, bf16[1,512,2048]{2,1,0:T(8,128)(2,1)S(1)}, u32[]{:S(2)}, u32[]{:S(2)}) collective-permute-start(bf16[1,512,2048]{2,1,0:T(8,128)(2,1)} %refs_1_.1), channel_id=1, source_target_pairs={{0,1},{1,0},{2,3},{3,2},{4,5},{5,4},{6,7},{7,6},{8,9},{9,8},{10,11... | collective-permute-start | bytes 6291464 | tf_op jit(solution)/shard_map/ppermute | solution.py:25
  1.1 1.0 %cut_slices.2 = (bf16[64,1536]{1,0:T(8,128)(2,1)S(1)}, bf16[64,1536]{1,0:T(8,128)(2,1)S(1)}) custom-call(bf16[1,64,6144]{2,1,0:T(8,128)(2,1)} %src.3), custom_call_target="tpu_custom_call" | custom-call | tf_op jit(solution)/shard_map/cut_slices/pallas_call | solution.py:53
  2.2 2.7 %collective-permute-start.1 = (bf16[64,1536]{1,0:T(8,128)(2,1)S(1)}, bf16[64,1536]{1,0:T(8,128)(2,1)S(1)}, u32[]{:S(2)}, u32[]{:S(2)}) collective-permute-start(bf16[64,1536]{1,0:T(8,128)(2,1)S(1)} %get-tuple-element.26), channel_id=1, source_target_pairs={{0,3},{1,2},{2,1},{3,0},{4,7},{5,6},{6,5},{7,4},{8,11},{9,10},{10,... | collective-permute-start | bytes 589832 | tf_op jit(solution)/shard_map/ppermute | solution.py:25
  4.9 1.0 %cut_slices.3 = (bf16[64,1536]{1,0:T(8,128)(2,1)S(1)}, bf16[64,1536]{1,0:T(8,128)(2,1)S(1)}) custom-call(bf16[1,64,6144]{2,1,0:T(8,128)(2,1)} %src.3, bf16[64,1536]{1,0:T(8,128)(2,1)S(1)} %get-tuple-element.23.refs_0_), custom_call_target="tpu_custom_call" | custom-call | tf_op jit(solution)/shard_map/cut_slices/pallas_call | solution.py:53
  6.2 0.7 %copy-done.1 = s32[1,2,2]{2,1,0:T(2,128)S(1)} copy-done((s32[1,2,2]{2,1,0:T(2,128)S(1)}, s32[1,2,2]{2,1,0:T(2,128)}, u32[]{:S(2)}) %copy-start.1) | copy-done | bytes 40
  6.9 0.7 %copy-done.2 = s32[256]{0:T(256)S(1)} copy-done((s32[256]{0:T(256)S(1)}, s32[256]{0:T(256)}, u32[]{:S(2)}) %copy-start.2) | copy-done | bytes 1048
  7.6 1.0 %mask_bias.1.refs_4_ = f32[256,256]{1,0:T(8,128)S(1)} custom-call(s32[1,2,2]{2,1,0:T(2,128)S(1)} %copy-done.1, s32[256]{0:T(256)S(1)} %copy-done.2), custom_call_target="tpu_custom_call" | custom-call | tf_op jit(solution)/shard_map/mask_bias/pallas_call | solution.py:325
  8.5 1.6 %load_weights.2 = (bf16[1,64,2048]{2,1,0:T(8,128)(2,1)S(1)}, bf16[1,512,2048]{2,1,0:T(8,128)(2,1)S(1)}) custom-call(bf16[1,64,2048]{2,1,0:T(8,128)(2,1)} %refs_0_.2, bf16[1,512,2048]{2,1,0:T(8,128)(2,1)} %refs_1_.1, bf16[64,1536]{1,0:T(8,128)(2,1)S(1)} %get-tuple-element.24.refs_2_.refs_0_), custom_call_target="tpu_custom_call" | custom-call | tf_op jit(solution)/shard_map/load_weights/pallas_call | solution.py:80
  10.2 4.3 %collective-permute-done.2.refs_3_ = bf16[64,1536]{1,0:T(8,128)(2,1)S(1)} collective-permute-done((bf16[64,1536]{1,0:T(8,128)(2,1)S(1)}, bf16[64,1536]{1,0:T(8,128)(2,1)S(1)}, u32[]{:S(2)}, u32[]{:S(2)}) %collective-permute-start.2) | collective-permute-done | bytes 196640 | tf_op jit(solution)/shard_map/ppermute | solution.py:25
  14.6 0.7 %attend.1 = bf16[128,512]{1,0:T(8,128)(2,1)S(1)} custom-call(bf16[64,1536]{1,0:T(8,128)(2,1)S(1)} %get-tuple-element.24.refs_2_.refs_0_, bf16[64,1536]{1,0:T(8,128)(2,1)S(1)} %collective-permute-done.refs_1_, bf16[64,1536]{1,0:T(8,128)(2,1)S(1)} %collective-permute-done.1.refs_2_, bf16[64,1536]{1,0:T(8,128)(2,1)S(1)} %collective-permute-done.2.refs_3_, ...), custom_call_target="tpu_custom_call" | custom-call | flops 67108864 | bytes 786432 | tf_op jit(solution)/shard_map/attend/pallas_call | solution.py:126
  15.3 1.1 %attend_project.1.mine = f32[128,2048]{1,0:T(8,128)S(1)} custom-call(bf16[64,1536]{1,0:T(8,128)(2,1)S(1)} %get-tuple-element.24.refs_2_.refs_0_, bf16[64,1536]{1,0:T(8,128)(2,1)S(1)} %collective-permute-done.refs_1_, bf16[64,1536]{1,0:T(8,128)(2,1)S(1)} %collective-permute-done.1.refs_2_, bf16[64,1536]{1,0:T(8,128)(2,1)S(1)} %collective-permute-done.2.refs_3_, ...), custom_call_target="tpu_custom_call" | custom-call | flops 335544320 | bytes 786432 | tf_op jit(solution)/shard_map/attend_project/pallas_call | solution.py:126
  17.1 1.7 %collective-permute-start.6 = (bf16[64,1152]{1,0:T(8,128)(2,1)S(1)}, bf16[64,1152]{1,0:T(8,128)(2,1)S(1)}, u32[]{:S(2)}, u32[]{:S(2)}) collective-permute-start(bf16[64,1152]{1,0:T(8,128)(2,1)S(1)} %get-tuple-element.33), channel_id=1, source_target_pairs={{0,2},{1,3},{2,0},{3,1},{4,6},{5,7},{6,4},{7,5},{8,10},{9,11},{10,... | collective-permute-start | bytes 442376 | tf_op jit(solution)/shard_map/ppermute | solution.py:25
  18.9 1.5 %collective-permute-start.5 = (bf16[128,896]{1,0:T(8,128)(2,1)S(1)}, bf16[128,896]{1,0:T(8,128)(2,1)S(1)}, u32[]{:S(2)}, u32[]{:S(2)}) collective-permute-start(bf16[128,896]{1,0:T(8,128)(2,1)S(1)} %get-tuple-element.31), channel_id=1, source_target_pairs={{0,4},{1,5},{2,6},{3,7},{4,8},{5,9},{6,10},{7,11},{8,12},{9,13},{1... | collective-permute-start | bytes 688136 | tf_op jit(solution)/shard_map/ppermute | solution.py:33
  20.4 2.9 %collective-permute-done.6 = bf16[64,1152]{1,0:T(8,128)(2,1)S(1)} collective-permute-done((bf16[64,1152]{1,0:T(8,128)(2,1)S(1)}, bf16[64,1152]{1,0:T(8,128)(2,1)S(1)}, u32[]{:S(2)}, u32[]{:S(2)}) %collective-permute-start.6) | collective-permute-done | bytes 147488 | tf_op jit(solution)/shard_map/ppermute | solution.py:25
  23.2 2.6 %collective-permute-start.9 = (bf16[64,1152]{1,0:T(8,128)(2,1)S(1)}, bf16[64,1152]{1,0:T(8,128)(2,1)S(1)}, u32[]{:S(2)}, u32[]{:S(2)}) collective-permute-start(bf16[64,1152]{1,0:T(8,128)(2,1)S(1)} %add_convert_fusion.after), channel_id=1, source_target_pairs={{0,6},{1,7},{2,4},{3,5},{4,10},{5,11},{6,8},{7,9},{8,14},{9,15},{1... | collective-permute-start | bytes 442376 | tf_op jit(solution)/shard_map/ppermute | solution.py:33
  25.9 1.6 %collective-permute-start.8 = (bf16[64,1152]{1,0:T(8,128)(2,1)S(1)}, bf16[64,1152]{1,0:T(8,128)(2,1)S(1)}, u32[]{:S(2)}, u32[]{:S(2)}) collective-permute-start(bf16[64,1152]{1,0:T(8,128)(2,1)S(1)} %add_convert_fusion.after), channel_id=1, source_target_pairs={{0,4},{1,5},{2,6},{3,7},{4,8},{5,9},{6,10},{7,11},{8,12},{9,13},{1... | collective-permute-start | bytes 442376 | tf_op jit(solution)/shard_map/ppermute | solution.py:33
  27.4 1.7 %collective-permute-done.5.x = bf16[128,896]{1,0:T(8,128)(2,1)S(1)} collective-permute-done((bf16[128,896]{1,0:T(8,128)(2,1)S(1)}, bf16[128,896]{1,0:T(8,128)(2,1)S(1)}, u32[]{:S(2)}, u32[]{:S(2)}) %collective-permute-start.5) | collective-permute-done | bytes 229408 | tf_op jit(solution)/shard_map/ppermute | solution.py:33
  29.2 0.6 %collective-permute-start.7 = (bf16[128,896]{1,0:T(8,128)(2,1)S(1)}, bf16[128,896]{1,0:T(8,128)(2,1)S(1)}, u32[]{:S(2)}, u32[]{:S(2)}) collective-permute-start(bf16[128,896]{1,0:T(8,128)(2,1)S(1)} %settle.1.refs_1_.mine), channel_id=1, source_target_pairs={{0,2},{1,3},{2,0},{3,1},{4,6},{5,7},{6,4},{7,5},{8,10},{9,11},{10,... | collective-permute-start | bytes 688136 | tf_op jit(solution)/shard_map/ppermute | solution.py:25
  29.7 2.9 %load_weights.3.refs_5_.weight = bf16[1,2048,1536]{2,1,0:T(8,128)(2,1)S(1)} custom-call(bf16[1,2048,1536]{2,1,0:T(8,128)(2,1)} %refs_0_.3, bf16[128,896]{1,0:T(8,128)(2,1)S(1)} %settle.1.refs_1_.mine), custom_call_target="tpu_custom_call" | custom-call | bytes 6291456 | tf_op jit(solution)/shard_map/load_weights/pallas_call | solution.py:80
  32.6 1.0 %collective-permute-done.9.refs_2_ = bf16[64,1152]{1,0:T(8,128)(2,1)S(1)} collective-permute-done((bf16[64,1152]{1,0:T(8,128)(2,1)S(1)}, bf16[64,1152]{1,0:T(8,128)(2,1)S(1)}, u32[]{:S(2)}, u32[]{:S(2)}) %collective-permute-start.9) | collective-permute-done | bytes 147488 | tf_op jit(solution)/shard_map/ppermute | solution.py:33
  33.6 1.8 %collective-permute-done.8.refs_0_.rest = bf16[64,1152]{1,0:T(8,128)(2,1)S(1)} collective-permute-done((bf16[64,1152]{1,0:T(8,128)(2,1)S(1)}, bf16[64,1152]{1,0:T(8,128)(2,1)S(1)}, u32[]{:S(2)}, u32[]{:S(2)}) %collective-permute-start.8) | collective-permute-done | bytes 147488 | tf_op jit(solution)/shard_map/ppermute | solution.py:33
  36.0 0.9 %collective-permute-done.10.refs_1_ = bf16[64,1152]{1,0:T(8,128)(2,1)S(1)} collective-permute-done((bf16[64,1152]{1,0:T(8,128)(2,1)S(1)}, bf16[64,1152]{1,0:T(8,128)(2,1)S(1)}, u32[]{:S(2)}, u32[]{:S(2)}) %collective-permute-start.10) | collective-permute-done | bytes 147488 | tf_op jit(solution)/shard_map/ppermute | solution.py:25
  37.5 1.3 %project_first.1 = (f32[256,1536]{1,0:T(8,128)S(1)}, f32[256,1]{1,0:T(8,128)S(1)}) custom-call(bf16[64,1152]{1,0:T(8,128)(2,1)S(1)} %collective-permute-done.8.refs_0_.rest, bf16[64,1152]{1,0:T(8,128)(2,1)S(1)} %collective-permute-done.10.refs_1_, bf16[64,1152]{1,0:T(8,128)(2,1)S(1)} %collective-permute-done.9.refs_2_, ...), custom_call_target="tpu_custom_call" | custom-call | flops 905969664 | bytes 3538944 | tf_op jit(solution)/shard_map/project_first/pallas_call | solution.py:226
  38.9 1.9 %project_second.1 = (bf16[1,64,2048]{2,1,0:T(8,128)(2,1)}, bf16[1,256,1536]{2,1,0:T(8,128)(2,1)}) custom-call(bf16[128,896]{1,0:T(8,128)(2,1)S(1)} %join_chips.1.even, bf16[128,896]{1,0:T(8,128)(2,1)S(1)} %collective-permute-done.12.odd, bf16[64,1152]{1,0:T(8,128)(2,1)S(1)} %collective-permute-done.8.refs_0_.rest, f32[1,2048]{1,0:T(1,128)S(1)} %copy-done, ...), custom_call_target="tpu_custom_call" | custom-call | flops 704643072 | bytes 2752512 | tf_op jit(solution)/shard_map/project_second/pallas_call | solution.py:274
  (21 shorter events, 2.3 us)
Async XLA Ops:
  0.6 16.1 %collective-permute-start.4 = (bf16[1,512,2048]{2,1,0:T(8,128)(2,1)}, bf16[1,512,2048]{2,1,0:T(8,128)(2,1)S(1)}, u32[]{:S(2)}, u32[]{:S(2)}) collective-permute-start(bf16[1,512,2048]{2,1,0:T(8,128)(2,1)} %refs_1_.1), channel_id=1, source_target_pairs={{0,1},{1,0},{2,3},{3,2},{4,5},{5,4},{6,7},{7,6},{8,9},{9,8},{10,11... | collective-permute-start | bytes 6291464 | tf_op jit(solution)/shard_map/ppermute | solution.py:25
  2.2 8.0 %collective-permute-start.1 = (bf16[64,1536]{1,0:T(8,128)(2,1)S(1)}, bf16[64,1536]{1,0:T(8,128)(2,1)S(1)}, u32[]{:S(2)}, u32[]{:S(2)}) collective-permute-start(bf16[64,1536]{1,0:T(8,128)(2,1)S(1)} %get-tuple-element.26), channel_id=1, source_target_pairs={{0,3},{1,2},{2,1},{3,0},{4,7},{5,6},{6,5},{7,4},{8,11},{9,10},{10,... | collective-permute-start | bytes 589832 | tf_op jit(solution)/shard_map/ppermute | solution.py:25
  4.9 9.7 %collective-permute-start.2 = (bf16[64,1536]{1,0:T(8,128)(2,1)S(1)}, bf16[64,1536]{1,0:T(8,128)(2,1)S(1)}, u32[]{:S(2)}, u32[]{:S(2)}) collective-permute-start(bf16[64,1536]{1,0:T(8,128)(2,1)S(1)} %get-tuple-element.23.refs_0_), channel_id=1, source_target_pairs={{0,2},{1,3},{2,0},{3,1},{4,6},{5,7},{6,4},{7,5},{8,10},{9,11},{10,... | collective-permute-start | bytes 589832 | tf_op jit(solution)/shard_map/ppermute | solution.py:25
  6.0 8.6 %collective-permute-start = (bf16[64,1536]{1,0:T(8,128)(2,1)S(1)}, bf16[64,1536]{1,0:T(8,128)(2,1)S(1)}, u32[]{:S(2)}, u32[]{:S(2)}) collective-permute-start(bf16[64,1536]{1,0:T(8,128)(2,1)S(1)} %get-tuple-element.25), channel_id=1, source_target_pairs={{0,1},{1,0},{2,3},{3,2},{4,5},{5,4},{6,7},{7,6},{8,9},{9,8},{10,11... | collective-permute-start | bytes 589832 | tf_op jit(solution)/shard_map/ppermute | solution.py:25
  6.2 0.7 %copy-start.1 = (s32[1,2,2]{2,1,0:T(2,128)S(1)}, s32[1,2,2]{2,1,0:T(2,128)}, u32[]{:S(2)}) copy-start(s32[1,2,2]{2,1,0:T(2,128)} %mask.1) | copy-start | bytes 52
  6.9 0.7 %copy-start.2 = (s32[256]{0:T(256)S(1)}, s32[256]{0:T(256)}, u32[]{:S(2)}) copy-start(s32[256]{0:T(256)} %order.1) | copy-start | bytes 3076
  15.3 1.4 %collective-permute-start.3 = (bf16[128,512]{1,0:T(8,128)(2,1)S(1)}, bf16[128,512]{1,0:T(8,128)(2,1)S(1)}, u32[]{:S(2)}, u32[]{:S(2)}) collective-permute-start(bf16[128,512]{1,0:T(8,128)(2,1)S(1)} %attend.1), channel_id=1, source_target_pairs={{0,1},{1,0},{2,3},{3,2},{4,5},{5,4},{6,7},{7,6},{8,9},{9,8},{10,11... | collective-permute-start | bytes 393224 | tf_op jit(solution)/shard_map/ppermute | solution.py:25
  17.1 6.1 %collective-permute-start.6 = (bf16[64,1152]{1,0:T(8,128)(2,1)S(1)}, bf16[64,1152]{1,0:T(8,128)(2,1)S(1)}, u32[]{:S(2)}, u32[]{:S(2)}) collective-permute-start(bf16[64,1152]{1,0:T(8,128)(2,1)S(1)} %get-tuple-element.33), channel_id=1, source_target_pairs={{0,2},{1,3},{2,0},{3,1},{4,6},{5,7},{6,4},{7,5},{8,10},{9,11},{10,... | collective-permute-start | bytes 442376 | tf_op jit(solution)/shard_map/ppermute | solution.py:25
  18.9 10.3 %collective-permute-start.5 = (bf16[128,896]{1,0:T(8,128)(2,1)S(1)}, bf16[128,896]{1,0:T(8,128)(2,1)S(1)}, u32[]{:S(2)}, u32[]{:S(2)}) collective-permute-start(bf16[128,896]{1,0:T(8,128)(2,1)S(1)} %get-tuple-element.31), channel_id=1, source_target_pairs={{0,4},{1,5},{2,6},{3,7},{4,8},{5,9},{6,10},{7,11},{8,12},{9,13},{1... | collective-permute-start | bytes 688136 | tf_op jit(solution)/shard_map/ppermute | solution.py:33
  23.2 10.4 %collective-permute-start.9 = (bf16[64,1152]{1,0:T(8,128)(2,1)S(1)}, bf16[64,1152]{1,0:T(8,128)(2,1)S(1)}, u32[]{:S(2)}, u32[]{:S(2)}) collective-permute-start(bf16[64,1152]{1,0:T(8,128)(2,1)S(1)} %add_convert_fusion.after), channel_id=1, source_target_pairs={{0,6},{1,7},{2,4},{3,5},{4,10},{5,11},{6,8},{7,9},{8,14},{9,15},{1... | collective-permute-start | bytes 442376 | tf_op jit(solution)/shard_map/ppermute | solution.py:33
  25.9 9.6 %collective-permute-start.8 = (bf16[64,1152]{1,0:T(8,128)(2,1)S(1)}, bf16[64,1152]{1,0:T(8,128)(2,1)S(1)}, u32[]{:S(2)}, u32[]{:S(2)}) collective-permute-start(bf16[64,1152]{1,0:T(8,128)(2,1)S(1)} %add_convert_fusion.after), channel_id=1, source_target_pairs={{0,4},{1,5},{2,6},{3,7},{4,8},{5,9},{6,10},{7,11},{8,12},{9,13},{1... | collective-permute-start | bytes 442376 | tf_op jit(solution)/shard_map/ppermute | solution.py:33
  29.2 8.3 %copy-start = (f32[1,2048]{1,0:T(1,128)S(1)}, f32[1,2048]{1,0:T(1,128)}, u32[]{:S(2)}) copy-start(f32[1,2048]{1,0:T(1,128)} %gain.1) | copy-start | bytes 24580
  29.2 8.1 %collective-permute-start.7 = (bf16[128,896]{1,0:T(8,128)(2,1)S(1)}, bf16[128,896]{1,0:T(8,128)(2,1)S(1)}, u32[]{:S(2)}, u32[]{:S(2)}) collective-permute-start(bf16[128,896]{1,0:T(8,128)(2,1)S(1)} %settle.1.refs_1_.mine), channel_id=1, source_target_pairs={{0,2},{1,3},{2,0},{3,1},{4,6},{5,7},{6,4},{7,5},{8,10},{9,11},{10,... | collective-permute-start | bytes 688136 | tf_op jit(solution)/shard_map/ppermute | solution.py:25
  35.5 1.4 %collective-permute-start.10 = (bf16[64,1152]{1,0:T(8,128)(2,1)S(1)}, bf16[64,1152]{1,0:T(8,128)(2,1)S(1)}, u32[]{:S(2)}, u32[]{:S(2)}) collective-permute-start(bf16[64,1152]{1,0:T(8,128)(2,1)S(1)} %collective-permute-done.8.refs_0_.rest), channel_id=1, source_target_pairs={{0,1},{1,0},{2,3},{3,2},{4,5},{5,4},{6,7},{7,6},{8,9},{9,8},{10,11... | collective-permute-start | bytes 442376 | tf_op jit(solution)/shard_map/ppermute | solution.py:25
  35.5 1.6 %collective-permute-start.11 = (bf16[64,1152]{1,0:T(8,128)(2,1)S(1)}, bf16[64,1152]{1,0:T(8,128)(2,1)S(1)}, u32[]{:S(2)}, u32[]{:S(2)}) collective-permute-start(bf16[64,1152]{1,0:T(8,128)(2,1)S(1)} %collective-permute-done.9.refs_2_), channel_id=1, source_target_pairs={{0,1},{1,0},{2,3},{3,2},{4,5},{5,4},{6,7},{7,6},{8,9},{9,8},{10,11... | collective-permute-start | bytes 442376 | tf_op jit(solution)/shard_map/ppermute | solution.py:25
  37.3 1.6 %collective-permute-start.12 = (bf16[128,896]{1,0:T(8,128)(2,1)S(1)}, bf16[128,896]{1,0:T(8,128)(2,1)S(1)}, u32[]{:S(2)}, u32[]{:S(2)}) collective-permute-start(bf16[128,896]{1,0:T(8,128)(2,1)S(1)} %join_chips.1.even), channel_id=1, source_target_pairs={{0,1},{1,0},{2,3},{3,2},{4,5},{5,4},{6,7},{7,6},{8,9},{9,8},{10,11... | collective-permute-start | bytes 688136 | tf_op jit(solution)/shard_map/ppermute | solution.py:25

commit v6 on v5

--- a/solution.py
+++ b/solution.py
@@ -76,7 +76,7 @@
         c.wait()
 
 
-def load(arrays, pieces, after=(), cost=0):
+def load(arrays, pieces, after=()):
     return pl.pallas_call(
         functools.partial(load_kernel, pieces),
         out_shape=[pltpu.VMEM(a.shape, a.dtype) for a in arrays],
@@ -85,7 +85,7 @@
         scratch_shapes=[pltpu.SemaphoreType.DMA((sum(pieces),))],
         compiler_params=pltpu.CompilerParams(vmem_limit_bytes=SMALL_LIMIT),
         cost_estimate=pl.CostEstimate(
-            flops=0, bytes_accessed=cost, transcendentals=0
+            flops=0, bytes_accessed=2 * sum(a.size * a.dtype.itemsize for a in arrays), transcendentals=0
         ),
         name="load_weights",
     )(*[pltpu.with_memory_space_constraint(a, pltpu.HBM) for a in arrays], *after)
@@ -108,13 +108,15 @@
 
 
 def attend_kernel(n, js, *refs):
-    blocks, bias, out = refs[:2] + refs[2:n][::-1], refs[n], refs[n + 1]
+    blocks, bias, out = refs[:n], refs[n], refs[n + 1]
     out[...] = attention(blocks, bias, js)
 
 
 def attend_project_kernel(n, js, *refs):
-    blocks, bias, weight, out = refs[:2] + refs[2:n][::-1], refs[n], refs[n + 1], refs[n + 2]
-    out[...] = jnp.dot(attention(blocks, bias, js), weight[0], preferred_element_type=jnp.float32)
+    blocks, bias, weight, out = refs[:n], refs[n], refs[n + 1], refs[n + 2]
+    out[...] = jnp.dot(
+        attention(blocks, bias, js), weight[0], preferred_element_type=jnp.float32
+    ).astype(jnp.bfloat16)
 
 
 def attend(blocks, bias, js, weight=None):
@@ -122,7 +124,7 @@
     rows, width = blocks[0].shape
     depth = width // 3
     queries = len(js) * rows
-    made = (attend_kernel, depth, jnp.bfloat16) if weight is None else (attend_project_kernel, weight.shape[2], jnp.float32)
+    made = (attend_kernel, depth, jnp.bfloat16) if weight is None else (attend_project_kernel, weight.shape[2], jnp.bfloat16)
     return pl.pallas_call(
         functools.partial(made[0], n, js),
         out_shape=jax.ShapeDtypeStruct((queries, made[1]), made[2]),
@@ -135,23 +137,22 @@
             transcendentals=queries * n * rows * depth // DH,
         ),
         name="attend" if weight is None else "attend_project",
-    )(*blocks[:2], *blocks[2:][::-1], bias, *(() if weight is None else (weight,)))
-
-
-def chip_sum_kernel(rows, cols, mine, theirs, weight, stream, partial, own, *others):
-    total = mine[...] + jnp.dot(theirs[...], weight[0], preferred_element_type=jnp.float32)
+    )(*blocks, bias, *(() if weight is None else (weight,)))
+
+
+def chip_sum_kernel(rows, cols, mine, theirs, stream, partial, own, *others):
     for i in range(mine.shape[0] // rows):
         part = slice(i * rows, (i + 1) * rows)
-        here = total[part]
+        total = mine[part, :].astype(jnp.float32) + theirs[part, :].astype(jnp.float32)
         if i == 0:
-            here = here + stream[0].astype(jnp.float32)
-            own[...] = here[:, cols:]
+            total = total + stream[0].astype(jnp.float32)
+            own[...] = total[:, cols:]
         else:
-            others[i - 1][...] = here[:, cols:].astype(jnp.bfloat16)
-        partial[part, :] = here[:, :cols].astype(jnp.bfloat16)
-
-
-def chip_sum(mine, theirs, weight, stream, cols):
+            others[i - 1][...] = total[:, cols:].astype(jnp.bfloat16)
+        partial[part, :] = total[:, :cols].astype(jnp.bfloat16)
+
+
+def chip_sum(mine, theirs, stream, cols):
     rows = stream.shape[1]
     count, depth = mine.shape
     rest = (rows, depth - cols)
@@ -162,11 +163,26 @@
             jax.ShapeDtypeStruct(rest, jnp.float32),
         ]
         + [jax.ShapeDtypeStruct(rest, jnp.bfloat16)] * (count // rows - 1),
-        in_specs=[VM] * 4,
+        in_specs=[VM] * 3,
         out_specs=[VM] * (count // rows + 1),
-        compiler_params=pltpu.CompilerParams(vmem_limit_bytes=VMEM_LIMIT),
+        compiler_params=pltpu.CompilerParams(vmem_limit_bytes=SMALL_LIMIT),
         name="chip_sum",
-    )(mine, theirs, weight, stream)
+    )(mine, theirs, stream)
+
+
+def settle_kernel(x, after, out):
+    out[...] = x[...]
+
+
+def settle(x, after):
+    return pl.pallas_call(
+        settle_kernel,
+        out_shape=jax.ShapeDtypeStruct(x.shape, x.dtype),
+        in_specs=[VM, ANY],
+        out_specs=VM,
+        compiler_params=pltpu.CompilerParams(vmem_limit_bytes=SMALL_LIMIT),
+        name="settle",
+    )(x, after)
 
 
 def join_kernel(rows, mine, *refs):
@@ -188,21 +204,6 @@
         compiler_params=pltpu.CompilerParams(vmem_limit_bytes=SMALL_LIMIT),
         name="join_chips",
     )(mine, *others)
-
-
-def settle_kernel(x, after, out):
-    out[...] = x[...]
-
-
-def settle(x, after):
-    return pl.pallas_call(
-        settle_kernel,
-        out_shape=jax.ShapeDtypeStruct(x.shape, x.dtype),
-        in_specs=[VM, ANY],
-        out_specs=VM,
-        compiler_params=pltpu.CompilerParams(vmem_limit_bytes=SMALL_LIMIT),
-        name="settle",
-    )(x, after)
 
 
 def project_first_kernel(n, *refs):
@@ -337,16 +338,14 @@
     rows = projected.shape[1]
     far_cut = cut(projected, n, tuple(range(2, n)))
     far = [swap(far_cut[j - 2], j) for j in range(2, n)]
-    near_cut = cut(projected, n, (0, 1), (far_cut[0],))
+    near_cut = cut(projected, n, (0, 1), (far_cut[-1],))
     blocks = [near_cut[0], swap(near_cut[1], 1)] + far
-    beside_weight = swap(out_weight, 1)
-    stream, out_weight = load((stream_before, out_weight), (1, 4), (near_cut[0],))
+    stream, out_weight = load((stream_before, out_weight), (1, 4))
     bias = mask_bias(block_mask, token_order, n, rows)
-    bias, out_weight = lax.optimization_barrier((bias, out_weight))
-    crossing = attend(blocks, bias, tuple(range(1, n, 2)))
+    crossing = attend(blocks, bias, tuple(range(1, n, 2)), out_weight)
     staying = attend(blocks, bias, tuple(range(0, n, 2)), out_weight)
-    cols = out_weight.shape[2] * 7 // 16
-    partial, own, *others = chip_sum(staying, swap(crossing, 1), beside_weight, stream, cols)
+    cols = crossing.shape[1] * 7 // 16
+    partial, own, *others = chip_sum(staying, swap(crossing, 1), stream, cols)
     partial = onward(partial, 0)
     total = own
     for k, x in enumerate(others):
@@ -355,7 +354,7 @@
     rest = [onward(total, j) for j in range(0, n, 2)]
     partial = settle(partial, total)
     swapped = [swap(partial, j) for j in range(2, n, 2)]
-    (proj_weight,) = load((proj_weight,), (8,), (partial,), 2 * proj_weight.size)
+    (proj_weight,) = load((proj_weight,), (8,), (partial,))
     rest, proj_weight = lax.optimization_barrier((rest, proj_weight))
     rest = [r for x in rest for r in (x, swap(x, 1))]
     swapped, rest = lax.optimization_barrier((swapped, rest))

time: 41.1 us -> 40.7 us (level)
  waiting for transfers between devices: 13.5 us -> 12.5 us
  starting transfers between devices: 12.1 us -> 12.7 us
    ppermute x10 -> x9, waiting for transfers between devices: 8.91 us -> 7.85 us  [swap(): return lax.ppermute(x, 'seq', [(i, i ^ by) for i in range(size)])]
    ppermute x10 -> x9, starting transfers between devices: 6.46 us -> 6.93 us  [swap(): return lax.ppermute(x, 'seq', [(i, i ^ by) for i in range(size)])]
  transfers between devices with their start and end apart: 13 -> 12, of which waited for: 10 -> 11; matrix products, arithmetic and copies ran while one was open for 0% -> 0% of each run, Pallas kernels for 26% -> 22%
where the time goes in v6:
time: 40.7 us; the launch traced here: 40.5 us
  Pallas kernels  13.2 us (32%)
  starting transfers between devices  12.7 us (31%)
  waiting for transfers between devices  12.5 us (31%)
  local copies, waits for them, and re-layouts  1.36 us (3%)
  between operations  0.72 us (2%)
    ppermute x9, waiting for transfers between devices, swap(): return lax.ppermute(x, 'seq', [(i, i ^ by) for i in range(size)])  7.85 us
    ppermute x9, starting transfers between devices, swap(): return lax.ppermute(x, 'seq', [(i, i ^ by) for i in range(size)])  6.93 us
    ppermute x3, starting transfers between devices, onward(): return lax.ppermute(x, ('segment', 'seq'), pairs)  5.76 us
    ppermute x3, waiting for transfers between devices, onward(): return lax.ppermute(x, ('segment', 'seq'), pairs)  4.66 us
    pallas_call x2, Pallas kernels, load(): pl.pallas_call(functools.partial(load_kernel, pieces), out_shape=[pltpu.V...  4.5 us
    pallas_call x2, Pallas kernels, attend(): pl.pallas_call(functools.partial(made[0], n, js), out_shape=jax.ShapeDtyp...  2.14 us
    pallas_call x2, Pallas kernels, cut(): pl.pallas_call(functools.partial(cut_kernel, js), out_shape=[pltpu.VMEM((...  2.09 us
    pallas_call x1, Pallas kernels, project_second(): pl.pallas_call(functools.partial(project_second_kernel, n, tile), out_sha...  1.93 us
  transfers between devices with their start and end apart: 12, of which 11 were waited for; matrix products, arithmetic and copies ran while one was open for 0% of the time, Pallas kernels for 22%

profile of v6, /device:TPU:0, one launch (start us, length us, event | category | flops | bytes accessed | tf_op | source)
XLA Modules:
  0.0 40.5 jit_solution(8386222877357858623)
XLA Ops:
  0.6 1.0 %cut_slices.2 = (bf16[64,1536]{1,0:T(8,128)(2,1)S(1)}, bf16[64,1536]{1,0:T(8,128)(2,1)S(1)}) custom-call(bf16[1,64,6144]{2,1,0:T(8,128)(2,1)} %src.3), custom_call_target="tpu_custom_call" | custom-call | tf_op jit(solution)/shard_map/cut_slices/pallas_call | solution.py:53
  1.7 3.0 %collective-permute-start.1 = (bf16[64,1536]{1,0:T(8,128)(2,1)S(1)}, bf16[64,1536]{1,0:T(8,128)(2,1)S(1)}, u32[]{:S(2)}, u32[]{:S(2)}) collective-permute-start(bf16[64,1536]{1,0:T(8,128)(2,1)S(1)} %get-tuple-element.24), channel_id=1, source_target_pairs={{0,2},{1,3},{2,0},{3,1},{4,6},{5,7},{6,4},{7,5},{8,10},{9,11},{10,... | collective-permute-start | bytes 589832 | tf_op jit(solution)/shard_map/ppermute | solution.py:25
  4.7 1.0 %cut_slices.3 = (bf16[64,1536]{1,0:T(8,128)(2,1)S(1)}, bf16[64,1536]{1,0:T(8,128)(2,1)S(1)}) custom-call(bf16[1,64,6144]{2,1,0:T(8,128)(2,1)} %src.3, bf16[64,1536]{1,0:T(8,128)(2,1)S(1)} %get-tuple-element.21.refs_0_), custom_call_target="tpu_custom_call" | custom-call | tf_op jit(solution)/shard_map/cut_slices/pallas_call | solution.py:53
  6.0 0.7 %copy-done.1 = s32[1,2,2]{2,1,0:T(2,128)S(1)} copy-done((s32[1,2,2]{2,1,0:T(2,128)S(1)}, s32[1,2,2]{2,1,0:T(2,128)}, u32[]{:S(2)}) %copy-start.1) | copy-done | bytes 40
  6.7 0.7 %copy-done.2 = s32[256]{0:T(256)S(1)} copy-done((s32[256]{0:T(256)S(1)}, s32[256]{0:T(256)}, u32[]{:S(2)}) %copy-start.2) | copy-done | bytes 1048
  7.4 1.0 %mask_bias.1.refs_4_ = f32[256,256]{1,0:T(8,128)S(1)} custom-call(s32[1,2,2]{2,1,0:T(2,128)S(1)} %copy-done.1, s32[256]{0:T(256)S(1)} %copy-done.2), custom_call_target="tpu_custom_call" | custom-call | tf_op jit(solution)/shard_map/mask_bias/pallas_call | solution.py:326
  8.4 1.6 %load_weights.2 = (bf16[1,64,2048]{2,1,0:T(8,128)(2,1)S(1)}, bf16[1,512,2048]{2,1,0:T(8,128)(2,1)S(1)}) custom-call(bf16[1,64,2048]{2,1,0:T(8,128)(2,1)} %refs_0_.2, bf16[1,512,2048]{2,1,0:T(8,128)(2,1)} %refs_1_.1), custom_call_target="tpu_custom_call" | custom-call | bytes 4718592 | tf_op jit(solution)/shard_map/load_weights/pallas_call | solution.py:80
  10.4 2.6 %collective-permute-done.2.refs_3_ = bf16[64,1536]{1,0:T(8,128)(2,1)S(1)} collective-permute-done((bf16[64,1536]{1,0:T(8,128)(2,1)S(1)}, bf16[64,1536]{1,0:T(8,128)(2,1)S(1)}, u32[]{:S(2)}, u32[]{:S(2)}) %collective-permute-start.2) | collective-permute-done | bytes 196640 | tf_op jit(solution)/shard_map/ppermute | solution.py:25
  13.1 1.1 %attend_project.3 = bf16[128,2048]{1,0:T(8,128)(2,1)S(1)} custom-call(bf16[64,1536]{1,0:T(8,128)(2,1)S(1)} %get-tuple-element.22.refs_0_, bf16[64,1536]{1,0:T(8,128)(2,1)S(1)} %collective-permute-done.refs_1_, bf16[64,1536]{1,0:T(8,128)(2,1)S(1)} %collective-permute-done.1.refs_2_, bf16[64,1536]{1,0:T(8,128)(2,1)S(1)} %collective-permute-done.2.refs_3_, ...), custom_call_target="tpu_custom_call" | custom-call | flops 335544320 | bytes 786432 | tf_op jit(solution)/shard_map/attend_project/pallas_call | solution.py:128
  14.2 0.6 %collective-permute-start.3 = (bf16[128,2048]{1,0:T(8,128)(2,1)S(1)}, bf16[128,2048]{1,0:T(8,128)(2,1)S(1)}, u32[]{:S(2)}, u32[]{:S(2)}) collective-permute-start(bf16[128,2048]{1,0:T(8,128)(2,1)S(1)} %attend_project.3), channel_id=1, source_target_pairs={{0,1},{1,0},{2,3},{3,2},{4,5},{5,4},{6,7},{7,6},{8,9},{9,8},{10,11... | collective-permute-start | bytes 1572872 | tf_op jit(solution)/shard_map/ppermute | solution.py:25
  14.8 1.1 %attend_project.2.mine = bf16[128,2048]{1,0:T(8,128)(2,1)S(1)} custom-call(bf16[64,1536]{1,0:T(8,128)(2,1)S(1)} %get-tuple-element.22.refs_0_, bf16[64,1536]{1,0:T(8,128)(2,1)S(1)} %collective-permute-done.refs_1_, bf16[64,1536]{1,0:T(8,128)(2,1)S(1)} %collective-permute-done.1.refs_2_, bf16[64,1536]{1,0:T(8,128)(2,1)S(1)} %collective-permute-done.2.refs_3_, ...), custom_call_target="tpu_custom_call" | custom-call | flops 335544320 | bytes 786432 | tf_op jit(solution)/shard_map/attend_project/pallas_call | solution.py:128
  16.5 1.8 %collective-permute-start.5 = (bf16[64,1152]{1,0:T(8,128)(2,1)S(1)}, bf16[64,1152]{1,0:T(8,128)(2,1)S(1)}, u32[]{:S(2)}, u32[]{:S(2)}) collective-permute-start(bf16[64,1152]{1,0:T(8,128)(2,1)S(1)} %get-tuple-element.29), channel_id=1, source_target_pairs={{0,2},{1,3},{2,0},{3,1},{4,6},{5,7},{6,4},{7,5},{8,10},{9,11},{10,... | collective-permute-start | bytes 442376 | tf_op jit(solution)/shard_map/ppermute | solution.py:25
  18.3 1.5 %collective-permute-start.4 = (bf16[128,896]{1,0:T(8,128)(2,1)S(1)}, bf16[128,896]{1,0:T(8,128)(2,1)S(1)}, u32[]{:S(2)}, u32[]{:S(2)}) collective-permute-start(bf16[128,896]{1,0:T(8,128)(2,1)S(1)} %get-tuple-element.27), channel_id=1, source_target_pairs={{0,4},{1,5},{2,6},{3,7},{4,8},{5,9},{6,10},{7,11},{8,12},{9,13},{1... | collective-permute-start | bytes 688136 | tf_op jit(solution)/shard_map/ppermute | solution.py:33
  19.8 2.9 %collective-permute-done.5 = bf16[64,1152]{1,0:T(8,128)(2,1)S(1)} collective-permute-done((bf16[64,1152]{1,0:T(8,128)(2,1)S(1)}, bf16[64,1152]{1,0:T(8,128)(2,1)S(1)}, u32[]{:S(2)}, u32[]{:S(2)}) %collective-permute-start.5) | collective-permute-done | bytes 147488 | tf_op jit(solution)/shard_map/ppermute | solution.py:25
  22.7 2.7 %collective-permute-start.8 = (bf16[64,1152]{1,0:T(8,128)(2,1)S(1)}, bf16[64,1152]{1,0:T(8,128)(2,1)S(1)}, u32[]{:S(2)}, u32[]{:S(2)}) collective-permute-start(bf16[64,1152]{1,0:T(8,128)(2,1)S(1)} %add_convert_fusion.after), channel_id=1, source_target_pairs={{0,6},{1,7},{2,4},{3,5},{4,10},{5,11},{6,8},{7,9},{8,14},{9,15},{1... | collective-permute-start | bytes 442376 | tf_op jit(solution)/shard_map/ppermute | solution.py:33
  25.4 1.5 %collective-permute-start.7 = (bf16[64,1152]{1,0:T(8,128)(2,1)S(1)}, bf16[64,1152]{1,0:T(8,128)(2,1)S(1)}, u32[]{:S(2)}, u32[]{:S(2)}) collective-permute-start(bf16[64,1152]{1,0:T(8,128)(2,1)S(1)} %add_convert_fusion.after), channel_id=1, source_target_pairs={{0,4},{1,5},{2,6},{3,7},{4,8},{5,9},{6,10},{7,11},{8,12},{9,13},{1... | collective-permute-start | bytes 442376 | tf_op jit(solution)/shard_map/ppermute | solution.py:33
  27.0 1.7 %collective-permute-done.4.x = bf16[128,896]{1,0:T(8,128)(2,1)S(1)} collective-permute-done((bf16[128,896]{1,0:T(8,128)(2,1)S(1)}, bf16[128,896]{1,0:T(8,128)(2,1)S(1)}, u32[]{:S(2)}, u32[]{:S(2)}) %collective-permute-start.4) | collective-permute-done | bytes 229408 | tf_op jit(solution)/shard_map/ppermute | solution.py:33
  28.7 0.6 %collective-permute-start.6 = (bf16[128,896]{1,0:T(8,128)(2,1)S(1)}, bf16[128,896]{1,0:T(8,128)(2,1)S(1)}, u32[]{:S(2)}, u32[]{:S(2)}) collective-permute-start(bf16[128,896]{1,0:T(8,128)(2,1)S(1)} %settle.1.refs_1_.mine), channel_id=1, source_target_pairs={{0,2},{1,3},{2,0},{3,1},{4,6},{5,7},{6,4},{7,5},{8,10},{9,11},{10,... | collective-permute-start | bytes 688136 | tf_op jit(solution)/shard_map/ppermute | solution.py:25
  29.3 2.9 %load_weights.3.refs_5_.weight = bf16[1,2048,1536]{2,1,0:T(8,128)(2,1)S(1)} custom-call(bf16[1,2048,1536]{2,1,0:T(8,128)(2,1)} %refs_0_.3, bf16[128,896]{1,0:T(8,128)(2,1)S(1)} %settle.1.refs_1_.mine), custom_call_target="tpu_custom_call" | custom-call | bytes 12582912 | tf_op jit(solution)/shard_map/load_weights/pallas_call | solution.py:80
  32.2 1.0 %collective-permute-done.8.refs_2_ = bf16[64,1152]{1,0:T(8,128)(2,1)S(1)} collective-permute-done((bf16[64,1152]{1,0:T(8,128)(2,1)S(1)}, bf16[64,1152]{1,0:T(8,128)(2,1)S(1)}, u32[]{:S(2)}, u32[]{:S(2)}) %collective-permute-start.8) | collective-permute-done | bytes 147488 | tf_op jit(solution)/shard_map/ppermute | solution.py:33
  33.2 1.9 %collective-permute-done.7.refs_0_.rest = bf16[64,1152]{1,0:T(8,128)(2,1)S(1)} collective-permute-done((bf16[64,1152]{1,0:T(8,128)(2,1)S(1)}, bf16[64,1152]{1,0:T(8,128)(2,1)S(1)}, u32[]{:S(2)}, u32[]{:S(2)}) %collective-permute-start.7) | collective-permute-done | bytes 147488 | tf_op jit(solution)/shard_map/ppermute | solution.py:33
  35.6 0.9 %collective-permute-done.9.refs_1_ = bf16[64,1152]{1,0:T(8,128)(2,1)S(1)} collective-permute-done((bf16[64,1152]{1,0:T(8,128)(2,1)S(1)}, bf16[64,1152]{1,0:T(8,128)(2,1)S(1)}, u32[]{:S(2)}, u32[]{:S(2)}) %collective-permute-start.9) | collective-permute-done | bytes 147488 | tf_op jit(solution)/shard_map/ppermute | solution.py:25
  37.1 1.3 %project_first.1 = (f32[256,1536]{1,0:T(8,128)S(1)}, f32[256,1]{1,0:T(8,128)S(1)}) custom-call(bf16[64,1152]{1,0:T(8,128)(2,1)S(1)} %collective-permute-done.7.refs_0_.rest, bf16[64,1152]{1,0:T(8,128)(2,1)S(1)} %collective-permute-done.9.refs_1_, bf16[64,1152]{1,0:T(8,128)(2,1)S(1)} %collective-permute-done.8.refs_2_, ...), custom_call_target="tpu_custom_call" | custom-call | flops 905969664 | bytes 3538944 | tf_op jit(solution)/shard_map/project_first/pallas_call | solution.py:227
  38.6 1.9 %project_second.1 = (bf16[1,64,2048]{2,1,0:T(8,128)(2,1)}, bf16[1,256,1536]{2,1,0:T(8,128)(2,1)}) custom-call(bf16[128,896]{1,0:T(8,128)(2,1)S(1)} %join_chips.1.even, bf16[128,896]{1,0:T(8,128)(2,1)S(1)} %collective-permute-done.11.odd, bf16[64,1152]{1,0:T(8,128)(2,1)S(1)} %collective-permute-done.7.refs_0_.rest, f32[1,2048]{1,0:T(1,128)S(1)} %copy-done, ...), custom_call_target="tpu_custom_call" | custom-call | flops 704643072 | bytes 2752512 | tf_op jit(solution)/shard_map/project_second/pallas_call | solution.py:275
  (19 shorter events, 2.6 us)
Async XLA Ops:
  1.7 8.8 %collective-permute-start.1 = (bf16[64,1536]{1,0:T(8,128)(2,1)S(1)}, bf16[64,1536]{1,0:T(8,128)(2,1)S(1)}, u32[]{:S(2)}, u32[]{:S(2)}) collective-permute-start(bf16[64,1536]{1,0:T(8,128)(2,1)S(1)} %get-tuple-element.24), channel_id=1, source_target_pairs={{0,2},{1,3},{2,0},{3,1},{4,6},{5,7},{6,4},{7,5},{8,10},{9,11},{10,... | collective-permute-start | bytes 589832 | tf_op jit(solution)/shard_map/ppermute | solution.py:25
  4.7 8.4 %collective-permute-start.2 = (bf16[64,1536]{1,0:T(8,128)(2,1)S(1)}, bf16[64,1536]{1,0:T(8,128)(2,1)S(1)}, u32[]{:S(2)}, u32[]{:S(2)}) collective-permute-start(bf16[64,1536]{1,0:T(8,128)(2,1)S(1)} %get-tuple-element.21.refs_0_), channel_id=1, source_target_pairs={{0,3},{1,2},{2,1},{3,0},{4,7},{5,6},{6,5},{7,4},{8,11},{9,10},{10,... | collective-permute-start | bytes 589832 | tf_op jit(solution)/shard_map/ppermute | solution.py:25
  5.8 7.3 %collective-permute-start = (bf16[64,1536]{1,0:T(8,128)(2,1)S(1)}, bf16[64,1536]{1,0:T(8,128)(2,1)S(1)}, u32[]{:S(2)}, u32[]{:S(2)}) collective-permute-start(bf16[64,1536]{1,0:T(8,128)(2,1)S(1)} %get-tuple-element.23), channel_id=1, source_target_pairs={{0,1},{1,0},{2,3},{3,2},{4,5},{5,4},{6,7},{7,6},{8,9},{9,8},{10,11... | collective-permute-start | bytes 589832 | tf_op jit(solution)/shard_map/ppermute | solution.py:25
  6.0 0.7 %copy-start.1 = (s32[1,2,2]{2,1,0:T(2,128)S(1)}, s32[1,2,2]{2,1,0:T(2,128)}, u32[]{:S(2)}) copy-start(s32[1,2,2]{2,1,0:T(2,128)} %mask.1) | copy-start | bytes 52
  6.7 0.7 %copy-start.2 = (s32[256]{0:T(256)S(1)}, s32[256]{0:T(256)}, u32[]{:S(2)}) copy-start(s32[256]{0:T(256)} %order.1) | copy-start | bytes 3076
  14.2 2.2 %collective-permute-start.3 = (bf16[128,2048]{1,0:T(8,128)(2,1)S(1)}, bf16[128,2048]{1,0:T(8,128)(2,1)S(1)}, u32[]{:S(2)}, u32[]{:S(2)}) collective-permute-start(bf16[128,2048]{1,0:T(8,128)(2,1)S(1)} %attend_project.3), channel_id=1, source_target_pairs={{0,1},{1,0},{2,3},{3,2},{4,5},{5,4},{6,7},{7,6},{8,9},{9,8},{10,11... | collective-permute-start | bytes 1572872 | tf_op jit(solution)/shard_map/ppermute | solution.py:25
  16.5 6.2 %collective-permute-start.5 = (bf16[64,1152]{1,0:T(8,128)(2,1)S(1)}, bf16[64,1152]{1,0:T(8,128)(2,1)S(1)}, u32[]{:S(2)}, u32[]{:S(2)}) collective-permute-start(bf16[64,1152]{1,0:T(8,128)(2,1)S(1)} %get-tuple-element.29), channel_id=1, source_target_pairs={{0,2},{1,3},{2,0},{3,1},{4,6},{5,7},{6,4},{7,5},{8,10},{9,11},{10,... | collective-permute-start | bytes 442376 | tf_op jit(solution)/shard_map/ppermute | solution.py:25
  18.3 10.4 %collective-permute-start.4 = (bf16[128,896]{1,0:T(8,128)(2,1)S(1)}, bf16[128,896]{1,0:T(8,128)(2,1)S(1)}, u32[]{:S(2)}, u32[]{:S(2)}) collective-permute-start(bf16[128,896]{1,0:T(8,128)(2,1)S(1)} %get-tuple-element.27), channel_id=1, source_target_pairs={{0,4},{1,5},{2,6},{3,7},{4,8},{5,9},{6,10},{7,11},{8,12},{9,13},{1... | collective-permute-start | bytes 688136 | tf_op jit(solution)/shard_map/ppermute | solution.py:33
  22.7 10.5 %collective-permute-start.8 = (bf16[64,1152]{1,0:T(8,128)(2,1)S(1)}, bf16[64,1152]{1,0:T(8,128)(2,1)S(1)}, u32[]{:S(2)}, u32[]{:S(2)}) collective-permute-start(bf16[64,1152]{1,0:T(8,128)(2,1)S(1)} %add_convert_fusion.after), channel_id=1, source_target_pairs={{0,6},{1,7},{2,4},{3,5},{4,10},{5,11},{6,8},{7,9},{8,14},{9,15},{1... | collective-permute-start | bytes 442376 | tf_op jit(solution)/shard_map/ppermute | solution.py:33
  25.4 9.7 %collective-permute-start.7 = (bf16[64,1152]{1,0:T(8,128)(2,1)S(1)}, bf16[64,1152]{1,0:T(8,128)(2,1)S(1)}, u32[]{:S(2)}, u32[]{:S(2)}) collective-permute-start(bf16[64,1152]{1,0:T(8,128)(2,1)S(1)} %add_convert_fusion.after), channel_id=1, source_target_pairs={{0,4},{1,5},{2,6},{3,7},{4,8},{5,9},{6,10},{7,11},{8,12},{9,13},{1... | collective-permute-start | bytes 442376 | tf_op jit(solution)/shard_map/ppermute | solution.py:33
  28.7 8.4 %copy-start = (f32[1,2048]{1,0:T(1,128)S(1)}, f32[1,2048]{1,0:T(1,128)}, u32[]{:S(2)}) copy-start(f32[1,2048]{1,0:T(1,128)} %gain.1) | copy-start | bytes 24580
  28.7 8.2 %collective-permute-start.6 = (bf16[128,896]{1,0:T(8,128)(2,1)S(1)}, bf16[128,896]{1,0:T(8,128)(2,1)S(1)}, u32[]{:S(2)}, u32[]{:S(2)}) collective-permute-start(bf16[128,896]{1,0:T(8,128)(2,1)S(1)} %settle.1.refs_1_.mine), channel_id=1, source_target_pairs={{0,2},{1,3},{2,0},{3,1},{4,6},{5,7},{6,4},{7,5},{8,10},{9,11},{10,... | collective-permute-start | bytes 688136 | tf_op jit(solution)/shard_map/ppermute | solution.py:25
  35.1 1.4 %collective-permute-start.9 = (bf16[64,1152]{1,0:T(8,128)(2,1)S(1)}, bf16[64,1152]{1,0:T(8,128)(2,1)S(1)}, u32[]{:S(2)}, u32[]{:S(2)}) collective-permute-start(bf16[64,1152]{1,0:T(8,128)(2,1)S(1)} %collective-permute-done.7.refs_0_.rest), channel_id=1, source_target_pairs={{0,1},{1,0},{2,3},{3,2},{4,5},{5,4},{6,7},{7,6},{8,9},{9,8},{10,11... | collective-permute-start | bytes 442376 | tf_op jit(solution)/shard_map/ppermute | solution.py:25
  35.1 1.6 %collective-permute-start.10 = (bf16[64,1152]{1,0:T(8,128)(2,1)S(1)}, bf16[64,1152]{1,0:T(8,128)(2,1)S(1)}, u32[]{:S(2)}, u32[]{:S(2)}) collective-permute-start(bf16[64,1152]{1,0:T(8,128)(2,1)S(1)} %collective-permute-done.8.refs_2_), channel_id=1, source_target_pairs={{0,1},{1,0},{2,3},{3,2},{4,5},{5,4},{6,7},{7,6},{8,9},{9,8},{10,11... | collective-permute-start | bytes 442376 | tf_op jit(solution)/shard_map/ppermute | solution.py:25
  37.0 1.6 %collective-permute-start.11 = (bf16[128,896]{1,0:T(8,128)(2,1)S(1)}, bf16[128,896]{1,0:T(8,128)(2,1)S(1)}, u32[]{:S(2)}, u32[]{:S(2)}) collective-permute-start(bf16[128,896]{1,0:T(8,128)(2,1)S(1)} %join_chips.1.even), channel_id=1, source_target_pairs={{0,1},{1,0},{2,3},{3,2},{4,5},{5,4},{6,7},{7,6},{8,9},{9,8},{10,11... | collective-permute-start | bytes 688136 | tf_op jit(solution)/shard_map/ppermute | solution.py:25

commit v7 on v6

--- a/solution.py
+++ b/solution.py
@@ -107,67 +107,79 @@
     return jnp.concatenate(attended, axis=1)
 
 
-def attend_kernel(n, js, *refs):
-    blocks, bias, out = refs[:n], refs[n], refs[n + 1]
-    out[...] = attention(blocks, bias, js)
-
-
 def attend_project_kernel(n, js, *refs):
-    blocks, bias, weight, out = refs[:n], refs[n], refs[n + 1], refs[n + 2]
-    out[...] = jnp.dot(
-        attention(blocks, bias, js), weight[0], preferred_element_type=jnp.float32
-    ).astype(jnp.bfloat16)
-
-
-def attend(blocks, bias, js, weight=None):
+    blocks, bias, weight, near, far = refs[:n], refs[n], refs[n + 1], refs[n + 2], refs[n + 3]
+    term = jnp.dot(attention(blocks, bias, js), weight[0], preferred_element_type=jnp.float32).astype(jnp.bfloat16)
+    rows = near.shape[0]
+    near[...] = term[:rows]
+    far[...] = term[rows:]
+
+
+def attend(blocks, bias, js, weight):
     n = len(blocks)
     rows, width = blocks[0].shape
-    depth = width // 3
+    depth = weight.shape[2]
     queries = len(js) * rows
-    made = (attend_kernel, depth, jnp.bfloat16) if weight is None else (attend_project_kernel, weight.shape[2], jnp.bfloat16)
-    return pl.pallas_call(
-        functools.partial(made[0], n, js),
-        out_shape=jax.ShapeDtypeStruct((queries, made[1]), made[2]),
-        in_specs=[VM] * (n + 1 + (weight is not None)),
-        out_specs=VM,
+    return pl.pallas_call(
+        functools.partial(attend_project_kernel, n, js),
+        out_shape=[
+            jax.ShapeDtypeStruct((rows, depth), jnp.bfloat16),
+            jax.ShapeDtypeStruct((queries - rows, depth), jnp.bfloat16),
+        ],
+        in_specs=[VM] * (n + 2),
+        out_specs=[VM, VM],
         compiler_params=pltpu.CompilerParams(vmem_limit_bytes=VMEM_LIMIT),
         cost_estimate=pl.CostEstimate(
-            flops=4 * queries * depth * n * rows + (0 if weight is None else 2 * queries * depth * weight.shape[2]),
+            flops=2 * queries * width // 3 * (2 * n * rows + depth),
             bytes_accessed=2 * n * rows * width,
-            transcendentals=queries * n * rows * depth // DH,
+            transcendentals=queries * n * rows * width // (3 * DH),
         ),
-        name="attend" if weight is None else "attend_project",
-    )(*blocks, bias, *(() if weight is None else (weight,)))
-
-
-def chip_sum_kernel(rows, cols, mine, theirs, stream, partial, own, *others):
-    for i in range(mine.shape[0] // rows):
-        part = slice(i * rows, (i + 1) * rows)
-        total = mine[part, :].astype(jnp.float32) + theirs[part, :].astype(jnp.float32)
-        if i == 0:
-            total = total + stream[0].astype(jnp.float32)
-            own[...] = total[:, cols:]
-        else:
-            others[i - 1][...] = total[:, cols:].astype(jnp.bfloat16)
-        partial[part, :] = total[:, :cols].astype(jnp.bfloat16)
-
-
-def chip_sum(mine, theirs, stream, cols):
-    rows = stream.shape[1]
+        name="attend_project",
+    )(*blocks, bias, weight)
+
+
+def far_sum_kernel(rows, cols, mine, theirs, partial, *others):
+    total = mine[...].astype(jnp.float32) + theirs[...].astype(jnp.float32)
+    partial[...] = total[:, :cols].astype(jnp.bfloat16)
+    for i, other in enumerate(others):
+        other[...] = total[i * rows : (i + 1) * rows, cols:].astype(jnp.bfloat16)
+
+
+def far_sum(mine, theirs, rows, cols):
     count, depth = mine.shape
-    rest = (rows, depth - cols)
-    return pl.pallas_call(
-        functools.partial(chip_sum_kernel, rows, cols),
+    return pl.pallas_call(
+        functools.partial(far_sum_kernel, rows, cols),
+        out_shape=[jax.ShapeDtypeStruct((count, cols), jnp.bfloat16)]
+        + [jax.ShapeDtypeStruct((rows, depth - cols), jnp.bfloat16)] * (count // rows),
+        in_specs=[VM] * 2,
+        out_specs=[VM] * (count // rows + 1),
+        compiler_params=pltpu.CompilerParams(vmem_limit_bytes=VMEM_LIMIT),
+        name="far_sum",
+    )(mine, theirs)
+
+
+def near_sum_kernel(mine, theirs, stream, far, partial, own):
+    rows, cols = mine.shape[0], partial.shape[1]
+    total = mine[...].astype(jnp.float32) + theirs[...].astype(jnp.float32) + stream[0].astype(jnp.float32)
+    partial[:rows, :] = total[:, :cols].astype(jnp.bfloat16)
+    partial[rows:, :] = far[...]
+    own[...] = total[:, cols:]
+
+
+def near_sum(mine, theirs, stream, far):
+    rows, depth = mine.shape
+    count, cols = far.shape
+    return pl.pallas_call(
+        near_sum_kernel,
         out_shape=[
-            jax.ShapeDtypeStruct((count, cols), jnp.bfloat16),
-            jax.ShapeDtypeStruct(rest, jnp.float32),
-        ]
-        + [jax.ShapeDtypeStruct(rest, jnp.bfloat16)] * (count // rows - 1),
-        in_specs=[VM] * 3,
-        out_specs=[VM] * (count // rows + 1),
-        compiler_params=pltpu.CompilerParams(vmem_limit_bytes=SMALL_LIMIT),
-        name="chip_sum",
-    )(mine, theirs, stream)
+            jax.ShapeDtypeStruct((rows + count, cols), jnp.bfloat16),
+            jax.ShapeDtypeStruct((rows, depth - cols), jnp.float32),
+        ],
+        in_specs=[VM] * 4,
+        out_specs=[VM] * 2,
+        compiler_params=pltpu.CompilerParams(vmem_limit_bytes=SMALL_LIMIT),
+        name="near_sum",
+    )(mine, theirs, stream, far)
 
 
 def settle_kernel(x, after, out):
@@ -342,20 +354,20 @@
     blocks = [near_cut[0], swap(near_cut[1], 1)] + far
     stream, out_weight = load((stream_before, out_weight), (1, 4))
     bias = mask_bias(block_mask, token_order, n, rows)
-    crossing = attend(blocks, bias, tuple(range(1, n, 2)), out_weight)
-    staying = attend(blocks, bias, tuple(range(0, n, 2)), out_weight)
-    cols = crossing.shape[1] * 7 // 16
-    partial, own, *others = chip_sum(staying, swap(crossing, 1), stream, cols)
+    near_out, far_out = attend(blocks, bias, tuple(range(1, n, 2)), out_weight)
+    near_own, far_own = attend(blocks, bias, tuple(range(0, n, 2)), out_weight)
+    cols = out_weight.shape[2] * 7 // 16
+    far_partial, *others = far_sum(far_own, swap(far_out, 1), rows, cols)
+    partial, own = near_sum(near_own, swap(near_out, 1), stream, far_partial)
     partial = onward(partial, 0)
-    total = own
+    (proj_weight,) = load((proj_weight,), (8,), (own,))
+    total, proj_weight = lax.optimization_barrier((own, proj_weight))
     for k, x in enumerate(others):
         total = total + swap(x, 2 * k + 2).astype(jnp.float32)
     total = total.astype(jnp.bfloat16)
     rest = [onward(total, j) for j in range(0, n, 2)]
     partial = settle(partial, total)
     swapped = [swap(partial, j) for j in range(2, n, 2)]
-    (proj_weight,) = load((proj_weight,), (8,), (partial,))
-    rest, proj_weight = lax.optimization_barrier((rest, proj_weight))
     rest = [r for x in rest for r in (x, swap(x, 1))]
     swapped, rest = lax.optimization_barrier((swapped, rest))
     even = join(rows, partial, swapped)

time: 40.7 us -> 40.4 us (level)
  starting transfers between devices: 12.7 us -> 12.2 us
    ppermute x3, waiting for transfers between devices: 4.66 us -> 7.63 us  [onward(): return lax.ppermute(x, ('segment', 'seq'), pairs)]
    ppermute x9 -> x10, waiting for transfers between devices: 7.85 us -> 5.05 us  [swap(): return lax.ppermute(x, 'seq', [(i, i ^ by) for i in range(size)])]
    ppermute x9 -> x10, starting transfers between devices: 6.93 us -> 6.45 us  [swap(): return lax.ppermute(x, 'seq', [(i, i ^ by) for i in range(size)])]
    pallas_call x3 -> x4, Pallas kernels: 2.29 us -> 2.29 us  [the longest x2 2.14 us: attend(): pl.pallas_call(functools.partial(attend_project_kernel, n, js), out_shape...]
  transfers between devices with their start and end apart: 12 -> 13, of which waited for: 11 -> 8; matrix products, arithmetic and copies ran while one was open for 0% -> 0% of each run, Pallas kernels for 22% -> 23%
where the time goes in v7:
time: 40.4 us; the launch traced here: 40.2 us
  Pallas kernels  13.2 us (33%)
  waiting for transfers between devices  12.7 us (31%)
  starting transfers between devices  12.2 us (30%)
  local copies, waits for them, and re-layouts  1.36 us (3%)
  between operations  0.74 us (2%)
    ppermute x3, waiting for transfers between devices, onward(): return lax.ppermute(x, ('segment', 'seq'), pairs)  7.63 us
    ppermute x10, starting transfers between devices, swap(): return lax.ppermute(x, 'seq', [(i, i ^ by) for i in range(size)])  6.45 us
    ppermute x3, starting transfers between devices, onward(): return lax.ppermute(x, ('segment', 'seq'), pairs)  5.74 us
    ppermute x10, waiting for transfers between devices, swap(): return lax.ppermute(x, 'seq', [(i, i ^ by) for i in range(size)])  5.05 us
    pallas_call x2, Pallas kernels, load(): pl.pallas_call(functools.partial(load_kernel, pieces), out_shape=[pltpu.V...  4.51 us
    pallas_call x2, Pallas kernels, attend(): pl.pallas_call(functools.partial(attend_project_kernel, n, js), out_shape...  2.14 us
    pallas_call x2, Pallas kernels, cut(): pl.pallas_call(functools.partial(cut_kernel, js), out_shape=[pltpu.VMEM((...  2.09 us
    pallas_call x1, Pallas kernels, project_second(): pl.pallas_call(functools.partial(project_second_kernel, n, tile), out_sha...  1.93 us
  transfers between devices with their start and end apart: 13, of which 8 were waited for; matrix products, arithmetic and copies ran while one was open for 0% of the time, Pallas kernels for 23%

profile of v7, /device:TPU:0, one launch (start us, length us, event | category | flops | bytes accessed | tf_op | source)
XLA Modules:
  0.0 40.2 jit_solution(11525722913632303035)
XLA Ops:
  0.6 1.0 %cut_slices.2 = (bf16[64,1536]{1,0:T(8,128)(2,1)S(1)}, bf16[64,1536]{1,0:T(8,128)(2,1)S(1)}) custom-call(bf16[1,64,6144]{2,1,0:T(8,128)(2,1)} %src.3), custom_call_target="tpu_custom_call" | custom-call | tf_op jit(solution)/shard_map/cut_slices/pallas_call | solution.py:53
  1.7 3.0 %collective-permute-start.1 = (bf16[64,1536]{1,0:T(8,128)(2,1)S(1)}, bf16[64,1536]{1,0:T(8,128)(2,1)S(1)}, u32[]{:S(2)}, u32[]{:S(2)}) collective-permute-start(bf16[64,1536]{1,0:T(8,128)(2,1)S(1)} %get-tuple-element.28), channel_id=1, source_target_pairs={{0,2},{1,3},{2,0},{3,1},{4,6},{5,7},{6,4},{7,5},{8,10},{9,11},{10,... | collective-permute-start | bytes 589832 | tf_op jit(solution)/shard_map/ppermute | solution.py:25
  4.7 1.0 %cut_slices.3 = (bf16[64,1536]{1,0:T(8,128)(2,1)S(1)}, bf16[64,1536]{1,0:T(8,128)(2,1)S(1)}) custom-call(bf16[1,64,6144]{2,1,0:T(8,128)(2,1)} %src.3, bf16[64,1536]{1,0:T(8,128)(2,1)S(1)} %get-tuple-element.25.refs_0_), custom_call_target="tpu_custom_call" | custom-call | tf_op jit(solution)/shard_map/cut_slices/pallas_call | solution.py:53
  6.0 0.7 %copy-done.1 = s32[1,2,2]{2,1,0:T(2,128)S(1)} copy-done((s32[1,2,2]{2,1,0:T(2,128)S(1)}, s32[1,2,2]{2,1,0:T(2,128)}, u32[]{:S(2)}) %copy-start.1) | copy-done | bytes 40
  6.7 0.7 %copy-done.2 = s32[256]{0:T(256)S(1)} copy-done((s32[256]{0:T(256)S(1)}, s32[256]{0:T(256)}, u32[]{:S(2)}) %copy-start.2) | copy-done | bytes 1048
  7.4 1.0 %mask_bias.1.refs_4_ = f32[256,256]{1,0:T(8,128)S(1)} custom-call(s32[1,2,2]{2,1,0:T(2,128)S(1)} %copy-done.1, s32[256]{0:T(256)S(1)} %copy-done.2), custom_call_target="tpu_custom_call" | custom-call | tf_op jit(solution)/shard_map/mask_bias/pallas_call | solution.py:338
  8.4 1.6 %load_weights.2 = (bf16[1,64,2048]{2,1,0:T(8,128)(2,1)S(1)}, bf16[1,512,2048]{2,1,0:T(8,128)(2,1)S(1)}) custom-call(bf16[1,64,2048]{2,1,0:T(8,128)(2,1)} %refs_0_.2, bf16[1,512,2048]{2,1,0:T(8,128)(2,1)} %refs_1_.1), custom_call_target="tpu_custom_call" | custom-call | bytes 4718592 | tf_op jit(solution)/shard_map/load_weights/pallas_call | solution.py:80
  10.4 2.6 %collective-permute-done.2.refs_3_ = bf16[64,1536]{1,0:T(8,128)(2,1)S(1)} collective-permute-done((bf16[64,1536]{1,0:T(8,128)(2,1)S(1)}, bf16[64,1536]{1,0:T(8,128)(2,1)S(1)}, u32[]{:S(2)}, u32[]{:S(2)}) %collective-permute-start.2) | collective-permute-done | bytes 196640 | tf_op jit(solution)/shard_map/ppermute | solution.py:25
  13.1 1.1 %attend_project.3 = (bf16[64,2048]{1,0:T(8,128)(2,1)S(1)}, bf16[64,2048]{1,0:T(8,128)(2,1)S(1)}) custom-call(bf16[64,1536]{1,0:T(8,128)(2,1)S(1)} %get-tuple-element.26.refs_0_, bf16[64,1536]{1,0:T(8,128)(2,1)S(1)} %collective-permute-done.refs_1_, bf16[64,1536]{1,0:T(8,128)(2,1)S(1)} %collective-permute-done.1.refs_2_, ...), custom_call_target="tpu_custom_call" | custom-call | flops 335544320 | bytes 786432 | tf_op jit(solution)/shard_map/attend_project/pallas_call | solution.py:123
  14.2 0.6 %collective-permute-start.4 = (bf16[64,2048]{1,0:T(8,128)(2,1)S(1)}, bf16[64,2048]{1,0:T(8,128)(2,1)S(1)}, u32[]{:S(2)}, u32[]{:S(2)}) collective-permute-start(bf16[64,2048]{1,0:T(8,128)(2,1)S(1)} %get-tuple-element.34), channel_id=1, source_target_pairs={{0,1},{1,0},{2,3},{3,2},{4,5},{5,4},{6,7},{7,6},{8,9},{9,8},{10,11... | collective-permute-start | bytes 786440 | tf_op jit(solution)/shard_map/ppermute | solution.py:25
  14.9 1.1 %attend_project.2 = (bf16[64,2048]{1,0:T(8,128)(2,1)S(1)}, bf16[64,2048]{1,0:T(8,128)(2,1)S(1)}) custom-call(bf16[64,1536]{1,0:T(8,128)(2,1)S(1)} %get-tuple-element.26.refs_0_, bf16[64,1536]{1,0:T(8,128)(2,1)S(1)} %collective-permute-done.refs_1_, bf16[64,1536]{1,0:T(8,128)(2,1)S(1)} %collective-permute-done.1.refs_2_, ...), custom_call_target="tpu_custom_call" | custom-call | flops 335544320 | bytes 786432 | tf_op jit(solution)/shard_map/attend_project/pallas_call | solution.py:123
  16.0 1.8 %collective-permute-start.6 = (bf16[64,1152]{1,0:T(8,128)(2,1)S(1)}, bf16[64,1152]{1,0:T(8,128)(2,1)S(1)}, u32[]{:S(2)}, u32[]{:S(2)}) collective-permute-start(bf16[64,1152]{1,0:T(8,128)(2,1)S(1)} %get-tuple-element.39), channel_id=1, source_target_pairs={{0,2},{1,3},{2,0},{3,1},{4,6},{5,7},{6,4},{7,5},{8,10},{9,11},{10,... | collective-permute-start | bytes 442376 | tf_op jit(solution)/shard_map/ppermute | solution.py:25
  17.9 1.5 %collective-permute-start.5 = (bf16[128,896]{1,0:T(8,128)(2,1)S(1)}, bf16[128,896]{1,0:T(8,128)(2,1)S(1)}, u32[]{:S(2)}, u32[]{:S(2)}) collective-permute-start(bf16[128,896]{1,0:T(8,128)(2,1)S(1)} %get-tuple-element.36), channel_id=1, source_target_pairs={{0,4},{1,5},{2,6},{3,7},{4,8},{5,9},{6,10},{7,11},{8,12},{9,13},{1... | collective-permute-start | bytes 688136 | tf_op jit(solution)/shard_map/ppermute | solution.py:33
  19.5 2.9 %load_weights.3.refs_5_.weight = bf16[1,2048,1536]{2,1,0:T(8,128)(2,1)S(1)} custom-call(bf16[1,2048,1536]{2,1,0:T(8,128)(2,1)} %refs_0_.3, f32[64,1152]{1,0:T(8,128)S(1)} %get-tuple-element.38.refs_1_), custom_call_target="tpu_custom_call" | custom-call | bytes 12582912 | tf_op jit(solution)/shard_map/load_weights/pallas_call | solution.py:80
  22.4 2.6 %collective-permute-start.10 = (bf16[64,1152]{1,0:T(8,128)(2,1)S(1)}, bf16[64,1152]{1,0:T(8,128)(2,1)S(1)}, u32[]{:S(2)}, u32[]{:S(2)}) collective-permute-start(bf16[64,1152]{1,0:T(8,128)(2,1)S(1)} %add_convert_fusion.after), channel_id=1, source_target_pairs={{0,6},{1,7},{2,4},{3,5},{4,10},{5,11},{6,8},{7,9},{8,14},{9,15},{1... | collective-permute-start | bytes 442376 | tf_op jit(solution)/shard_map/ppermute | solution.py:33
  25.1 1.5 %collective-permute-start.8 = (bf16[64,1152]{1,0:T(8,128)(2,1)S(1)}, bf16[64,1152]{1,0:T(8,128)(2,1)S(1)}, u32[]{:S(2)}, u32[]{:S(2)}) collective-permute-start(bf16[64,1152]{1,0:T(8,128)(2,1)S(1)} %add_convert_fusion.after), channel_id=1, source_target_pairs={{0,4},{1,5},{2,6},{3,7},{4,8},{5,9},{6,10},{7,11},{8,12},{9,13},{1... | collective-permute-start | bytes 442376 | tf_op jit(solution)/shard_map/ppermute | solution.py:33
  26.6 1.8 %collective-permute-done.5.x = bf16[128,896]{1,0:T(8,128)(2,1)S(1)} collective-permute-done((bf16[128,896]{1,0:T(8,128)(2,1)S(1)}, bf16[128,896]{1,0:T(8,128)(2,1)S(1)}, u32[]{:S(2)}, u32[]{:S(2)}) %collective-permute-start.5) | collective-permute-done | bytes 229408 | tf_op jit(solution)/shard_map/ppermute | solution.py:33
  28.5 0.6 %collective-permute-start.7 = (bf16[128,896]{1,0:T(8,128)(2,1)S(1)}, bf16[128,896]{1,0:T(8,128)(2,1)S(1)}, u32[]{:S(2)}, u32[]{:S(2)}) collective-permute-start(bf16[128,896]{1,0:T(8,128)(2,1)S(1)} %settle.1.mine), channel_id=1, source_target_pairs={{0,2},{1,3},{2,0},{3,1},{4,6},{5,7},{6,4},{7,5},{8,10},{9,11},{10,... | collective-permute-start | bytes 688136 | tf_op jit(solution)/shard_map/ppermute | solution.py:25
  29.0 3.7 %collective-permute-done.10.refs_2_ = bf16[64,1152]{1,0:T(8,128)(2,1)S(1)} collective-permute-done((bf16[64,1152]{1,0:T(8,128)(2,1)S(1)}, bf16[64,1152]{1,0:T(8,128)(2,1)S(1)}, u32[]{:S(2)}, u32[]{:S(2)}) %collective-permute-start.10) | collective-permute-done | bytes 147488 | tf_op jit(solution)/shard_map/ppermute | solution.py:33
  32.8 2.0 %collective-permute-done.8.refs_0_.rest = bf16[64,1152]{1,0:T(8,128)(2,1)S(1)} collective-permute-done((bf16[64,1152]{1,0:T(8,128)(2,1)S(1)}, bf16[64,1152]{1,0:T(8,128)(2,1)S(1)}, u32[]{:S(2)}, u32[]{:S(2)}) %collective-permute-start.8) | collective-permute-done | bytes 147488 | tf_op jit(solution)/shard_map/ppermute | solution.py:33
  34.8 1.4 %collective-permute-done.9.refs_1_ = bf16[64,1152]{1,0:T(8,128)(2,1)S(1)} collective-permute-done((bf16[64,1152]{1,0:T(8,128)(2,1)S(1)}, bf16[64,1152]{1,0:T(8,128)(2,1)S(1)}, u32[]{:S(2)}, u32[]{:S(2)}) %collective-permute-start.9) | collective-permute-done | bytes 147488 | tf_op jit(solution)/shard_map/ppermute | solution.py:25
  36.2 0.5 %collective-permute-done.7.refs_0_ = bf16[128,896]{1,0:T(8,128)(2,1)S(1)} collective-permute-done((bf16[128,896]{1,0:T(8,128)(2,1)S(1)}, bf16[128,896]{1,0:T(8,128)(2,1)S(1)}, u32[]{:S(2)}, u32[]{:S(2)}) %collective-permute-start.7) | collective-permute-done | bytes 229408 | tf_op jit(solution)/shard_map/ppermute | solution.py:25
  36.8 1.3 %project_first.1 = (f32[256,1536]{1,0:T(8,128)S(1)}, f32[256,1]{1,0:T(8,128)S(1)}) custom-call(bf16[64,1152]{1,0:T(8,128)(2,1)S(1)} %collective-permute-done.8.refs_0_.rest, bf16[64,1152]{1,0:T(8,128)(2,1)S(1)} %collective-permute-done.9.refs_1_, bf16[64,1152]{1,0:T(8,128)(2,1)S(1)} %collective-permute-done.10.refs_2_, ...), custom_call_target="tpu_custom_call" | custom-call | flops 905969664 | bytes 3538944 | tf_op jit(solution)/shard_map/project_first/pallas_call | solution.py:239
  38.3 1.9 %project_second.1 = (bf16[1,64,2048]{2,1,0:T(8,128)(2,1)}, bf16[1,256,1536]{2,1,0:T(8,128)(2,1)}) custom-call(bf16[128,896]{1,0:T(8,128)(2,1)S(1)} %join_chips.1.even, bf16[128,896]{1,0:T(8,128)(2,1)S(1)} %collective-permute-done.12.odd, bf16[64,1152]{1,0:T(8,128)(2,1)S(1)} %collective-permute-done.8.refs_0_.rest, f32[1,2048]{1,0:T(1,128)S(1)} %copy-done, ...), custom_call_target="tpu_custom_call" | custom-call | flops 704643072 | bytes 2752512 | tf_op jit(solution)/shard_map/project_second/pallas_call | solution.py:287
  (22 shorter events, 1.3 us)
Async XLA Ops:
  1.7 8.8 %collective-permute-start.1 = (bf16[64,1536]{1,0:T(8,128)(2,1)S(1)}, bf16[64,1536]{1,0:T(8,128)(2,1)S(1)}, u32[]{:S(2)}, u32[]{:S(2)}) collective-permute-start(bf16[64,1536]{1,0:T(8,128)(2,1)S(1)} %get-tuple-element.28), channel_id=1, source_target_pairs={{0,2},{1,3},{2,0},{3,1},{4,6},{5,7},{6,4},{7,5},{8,10},{9,11},{10,... | collective-permute-start | bytes 589832 | tf_op jit(solution)/shard_map/ppermute | solution.py:25
  4.7 8.4 %collective-permute-start.2 = (bf16[64,1536]{1,0:T(8,128)(2,1)S(1)}, bf16[64,1536]{1,0:T(8,128)(2,1)S(1)}, u32[]{:S(2)}, u32[]{:S(2)}) collective-permute-start(bf16[64,1536]{1,0:T(8,128)(2,1)S(1)} %get-tuple-element.25.refs_0_), channel_id=1, source_target_pairs={{0,3},{1,2},{2,1},{3,0},{4,7},{5,6},{6,5},{7,4},{8,11},{9,10},{10,... | collective-permute-start | bytes 589832 | tf_op jit(solution)/shard_map/ppermute | solution.py:25
  5.8 7.3 %collective-permute-start = (bf16[64,1536]{1,0:T(8,128)(2,1)S(1)}, bf16[64,1536]{1,0:T(8,128)(2,1)S(1)}, u32[]{:S(2)}, u32[]{:S(2)}) collective-permute-start(bf16[64,1536]{1,0:T(8,128)(2,1)S(1)} %get-tuple-element.27), channel_id=1, source_target_pairs={{0,1},{1,0},{2,3},{3,2},{4,5},{5,4},{6,7},{7,6},{8,9},{9,8},{10,11... | collective-permute-start | bytes 589832 | tf_op jit(solution)/shard_map/ppermute | solution.py:25
  6.0 0.7 %copy-start.1 = (s32[1,2,2]{2,1,0:T(2,128)S(1)}, s32[1,2,2]{2,1,0:T(2,128)}, u32[]{:S(2)}) copy-start(s32[1,2,2]{2,1,0:T(2,128)} %mask.1) | copy-start | bytes 52
  6.7 0.7 %copy-start.2 = (s32[256]{0:T(256)S(1)}, s32[256]{0:T(256)}, u32[]{:S(2)}) copy-start(s32[256]{0:T(256)} %order.1) | copy-start | bytes 3076
  14.2 1.8 %collective-permute-start.4 = (bf16[64,2048]{1,0:T(8,128)(2,1)S(1)}, bf16[64,2048]{1,0:T(8,128)(2,1)S(1)}, u32[]{:S(2)}, u32[]{:S(2)}) collective-permute-start(bf16[64,2048]{1,0:T(8,128)(2,1)S(1)} %get-tuple-element.34), channel_id=1, source_target_pairs={{0,1},{1,0},{2,3},{3,2},{4,5},{5,4},{6,7},{7,6},{8,9},{9,8},{10,11... | collective-permute-start | bytes 786440 | tf_op jit(solution)/shard_map/ppermute | solution.py:25
  14.8 3.0 %collective-permute-start.3 = (bf16[64,2048]{1,0:T(8,128)(2,1)S(1)}, bf16[64,2048]{1,0:T(8,128)(2,1)S(1)}, u32[]{:S(2)}, u32[]{:S(2)}) collective-permute-start(bf16[64,2048]{1,0:T(8,128)(2,1)S(1)} %get-tuple-element.31), channel_id=1, source_target_pairs={{0,1},{1,0},{2,3},{3,2},{4,5},{5,4},{6,7},{7,6},{8,9},{9,8},{10,11... | collective-permute-start | bytes 786440 | tf_op jit(solution)/shard_map/ppermute | solution.py:25
  16.0 6.3 %collective-permute-start.6 = (bf16[64,1152]{1,0:T(8,128)(2,1)S(1)}, bf16[64,1152]{1,0:T(8,128)(2,1)S(1)}, u32[]{:S(2)}, u32[]{:S(2)}) collective-permute-start(bf16[64,1152]{1,0:T(8,128)(2,1)S(1)} %get-tuple-element.39), channel_id=1, source_target_pairs={{0,2},{1,3},{2,0},{3,1},{4,6},{5,7},{6,4},{7,5},{8,10},{9,11},{10,... | collective-permute-start | bytes 442376 | tf_op jit(solution)/shard_map/ppermute | solution.py:25
  17.9 10.5 %collective-permute-start.5 = (bf16[128,896]{1,0:T(8,128)(2,1)S(1)}, bf16[128,896]{1,0:T(8,128)(2,1)S(1)}, u32[]{:S(2)}, u32[]{:S(2)}) collective-permute-start(bf16[128,896]{1,0:T(8,128)(2,1)S(1)} %get-tuple-element.36), channel_id=1, source_target_pairs={{0,4},{1,5},{2,6},{3,7},{4,8},{5,9},{6,10},{7,11},{8,12},{9,13},{1... | collective-permute-start | bytes 688136 | tf_op jit(solution)/shard_map/ppermute | solution.py:33
  19.5 17.3 %copy-start = (f32[1,2048]{1,0:T(1,128)S(1)}, f32[1,2048]{1,0:T(1,128)}, u32[]{:S(2)}) copy-start(f32[1,2048]{1,0:T(1,128)} %gain.1) | copy-start | bytes 24580
  22.4 10.4 %collective-permute-start.10 = (bf16[64,1152]{1,0:T(8,128)(2,1)S(1)}, bf16[64,1152]{1,0:T(8,128)(2,1)S(1)}, u32[]{:S(2)}, u32[]{:S(2)}) collective-permute-start(bf16[64,1152]{1,0:T(8,128)(2,1)S(1)} %add_convert_fusion.after), channel_id=1, source_target_pairs={{0,6},{1,7},{2,4},{3,5},{4,10},{5,11},{6,8},{7,9},{8,14},{9,15},{1... | collective-permute-start | bytes 442376 | tf_op jit(solution)/shard_map/ppermute | solution.py:33
  25.1 9.8 %collective-permute-start.8 = (bf16[64,1152]{1,0:T(8,128)(2,1)S(1)}, bf16[64,1152]{1,0:T(8,128)(2,1)S(1)}, u32[]{:S(2)}, u32[]{:S(2)}) collective-permute-start(bf16[64,1152]{1,0:T(8,128)(2,1)S(1)} %add_convert_fusion.after), channel_id=1, source_target_pairs={{0,4},{1,5},{2,6},{3,7},{4,8},{5,9},{6,10},{7,11},{8,12},{9,13},{1... | collective-permute-start | bytes 442376 | tf_op jit(solution)/shard_map/ppermute | solution.py:33
  28.5 8.2 %collective-permute-start.7 = (bf16[128,896]{1,0:T(8,128)(2,1)S(1)}, bf16[128,896]{1,0:T(8,128)(2,1)S(1)}, u32[]{:S(2)}, u32[]{:S(2)}) collective-permute-start(bf16[128,896]{1,0:T(8,128)(2,1)S(1)} %settle.1.mine), channel_id=1, source_target_pairs={{0,2},{1,3},{2,0},{3,1},{4,6},{5,7},{6,4},{7,5},{8,10},{9,11},{10,... | collective-permute-start | bytes 688136 | tf_op jit(solution)/shard_map/ppermute | solution.py:25
  32.8 2.1 %collective-permute-start.11 = (bf16[64,1152]{1,0:T(8,128)(2,1)S(1)}, bf16[64,1152]{1,0:T(8,128)(2,1)S(1)}, u32[]{:S(2)}, u32[]{:S(2)}) collective-permute-start(bf16[64,1152]{1,0:T(8,128)(2,1)S(1)} %collective-permute-done.10.refs_2_), channel_id=1, source_target_pairs={{0,1},{1,0},{2,3},{3,2},{4,5},{5,4},{6,7},{7,6},{8,9},{9,8},{10,11... | collective-permute-start | bytes 442376 | tf_op jit(solution)/shard_map/ppermute | solution.py:25
  34.8 1.4 %collective-permute-start.9 = (bf16[64,1152]{1,0:T(8,128)(2,1)S(1)}, bf16[64,1152]{1,0:T(8,128)(2,1)S(1)}, u32[]{:S(2)}, u32[]{:S(2)}) collective-permute-start(bf16[64,1152]{1,0:T(8,128)(2,1)S(1)} %collective-permute-done.8.refs_0_.rest), channel_id=1, source_target_pairs={{0,1},{1,0},{2,3},{3,2},{4,5},{5,4},{6,7},{7,6},{8,9},{9,8},{10,11... | collective-permute-start | bytes 442376 | tf_op jit(solution)/shard_map/ppermute | solution.py:25
  36.7 1.6 %collective-permute-start.12 = (bf16[128,896]{1,0:T(8,128)(2,1)S(1)}, bf16[128,896]{1,0:T(8,128)(2,1)S(1)}, u32[]{:S(2)}, u32[]{:S(2)}) collective-permute-start(bf16[128,896]{1,0:T(8,128)(2,1)S(1)} %join_chips.1.even), channel_id=1, source_target_pairs={{0,1},{1,0},{2,3},{3,2},{4,5},{5,4},{6,7},{7,6},{8,9},{9,8},{10,11... | collective-permute-start | bytes 688136 | tf_op jit(solution)/shard_map/ppermute | solution.py:25

commit v8 on v7

--- a/solution.py
+++ b/solution.py
@@ -94,16 +94,20 @@
 def attention(blocks, bias, js):
     rows, width = blocks[0].shape
     seen = jnp.concatenate([bias[j * rows : (j + 1) * rows] for j in js], axis=0)
-    attended = []
+    scores, values = [], []
     for h in range(width // (3 * DH)):
         c = h * 3 * DH
         q = jnp.concatenate([blocks[j][:, c : c + DH] for j in js], axis=0)
         k = jnp.concatenate([b[:, c + DH : c + 2 * DH] for b in blocks], axis=0)
-        v = jnp.concatenate([b[:, c + 2 * DH : c + 3 * DH] for b in blocks], axis=0)
-        s = lax.dot_general(q, k, (((1,), (1,)), ((), ())), preferred_element_type=jnp.float32) + seen
-        e = jnp.exp2((s - jnp.max(s, axis=-1, keepdims=True)) * (DH ** (-0.5) * math.log2(math.e)))
-        mixed = jnp.dot(e.astype(jnp.bfloat16), v, preferred_element_type=jnp.float32)
-        attended.append((mixed * (1.0 / jnp.sum(e, axis=-1, keepdims=True))).astype(jnp.bfloat16))
+        values.append(jnp.concatenate([b[:, c + 2 * DH : c + 3 * DH] for b in blocks], axis=0))
+        scores.append(lax.dot_general(q, k, (((1,), (1,)), ((), ())), preferred_element_type=jnp.float32) + seen)
+    tops = [jnp.max(s, axis=-1, keepdims=True) for s in scores]
+    weights = [jnp.exp2((s - m) * (DH ** (-0.5) * math.log2(math.e))) for s, m in zip(scores, tops)]
+    mixed = [
+        jnp.dot(e.astype(jnp.bfloat16), jnp.concatenate([v, jnp.ones_like(v)], axis=1), preferred_element_type=jnp.float32)
+        for e, v in zip(weights, values)
+    ]
+    attended = [(x[:, :DH] / x[:, DH:]).astype(jnp.bfloat16) for x in mixed]
     return jnp.concatenate(attended, axis=1)
 
 

time: 40.4 us -> 40 us (0.990)
  Pallas kernels: 13.2 us -> 12.7 us
    pallas_call x2, Pallas kernels: 2.14 us -> 1.61 us  [attend(): pl.pallas_call(functools.partial(attend_project_kernel, n, js), out_shape...]
  transfers between devices with their start and end apart: 13 -> 13, of which waited for: 8 -> 9; matrix products, arithmetic and copies ran while one was open for 0% -> 0% of each run, Pallas kernels for 23% -> 22%
where the time goes in v8:
time: 40 us; the launch traced here: 39.8 us
  waiting for transfers between devices  12.9 us (32%)
  Pallas kernels  12.7 us (32%)
  starting transfers between devices  12.1 us (30%)
  local copies, waits for them, and re-layouts  1.36 us (3%)
  between operations  0.74 us (2%)
    ppermute x3, waiting for transfers between devices, onward(): return lax.ppermute(x, ('segment', 'seq'), pairs)  7.56 us
    ppermute x10, starting transfers between devices, swap(): return lax.ppermute(x, 'seq', [(i, i ^ by) for i in range(size)])  6.48 us
    ppermute x3, starting transfers between devices, onward(): return lax.ppermute(x, ('segment', 'seq'), pairs)  5.65 us
    ppermute x10, waiting for transfers between devices, swap(): return lax.ppermute(x, 'seq', [(i, i ^ by) for i in range(size)])  5.3 us
    pallas_call x2, Pallas kernels, load(): pl.pallas_call(functools.partial(load_kernel, pieces), out_shape=[pltpu.V...  4.51 us
    pallas_call x2, Pallas kernels, cut(): pl.pallas_call(functools.partial(cut_kernel, js), out_shape=[pltpu.VMEM((...  2.09 us
    pallas_call x1, Pallas kernels, project_second(): pl.pallas_call(functools.partial(project_second_kernel, n, tile), out_sha...  1.93 us
    pallas_call x2, Pallas kernels, attend(): pl.pallas_call(functools.partial(attend_project_kernel, n, js), out_shape...  1.61 us
  transfers between devices with their start and end apart: 13, of which 9 were waited for; matrix products, arithmetic and copies ran while one was open for 0% of the time, Pallas kernels for 22%

profile of v8, /device:TPU:0, one launch (start us, length us, event | category | flops | bytes accessed | tf_op | source)
XLA Modules:
  0.0 39.8 jit_solution(15862876373741297970)
XLA Ops:
  0.6 1.0 %cut_slices.2 = (bf16[64,1536]{1,0:T(8,128)(2,1)S(1)}, bf16[64,1536]{1,0:T(8,128)(2,1)S(1)}) custom-call(bf16[1,64,6144]{2,1,0:T(8,128)(2,1)} %src.3), custom_call_target="tpu_custom_call" | custom-call | tf_op jit(solution)/shard_map/cut_slices/pallas_call | solution.py:53
  1.7 3.0 %collective-permute-start.1 = (bf16[64,1536]{1,0:T(8,128)(2,1)S(1)}, bf16[64,1536]{1,0:T(8,128)(2,1)S(1)}, u32[]{:S(2)}, u32[]{:S(2)}) collective-permute-start(bf16[64,1536]{1,0:T(8,128)(2,1)S(1)} %get-tuple-element.28), channel_id=1, source_target_pairs={{0,2},{1,3},{2,0},{3,1},{4,6},{5,7},{6,4},{7,5},{8,10},{9,11},{10,... | collective-permute-start | bytes 589832 | tf_op jit(solution)/shard_map/ppermute | solution.py:25
  4.7 1.0 %cut_slices.3 = (bf16[64,1536]{1,0:T(8,128)(2,1)S(1)}, bf16[64,1536]{1,0:T(8,128)(2,1)S(1)}) custom-call(bf16[1,64,6144]{2,1,0:T(8,128)(2,1)} %src.3, bf16[64,1536]{1,0:T(8,128)(2,1)S(1)} %get-tuple-element.25.refs_0_), custom_call_target="tpu_custom_call" | custom-call | tf_op jit(solution)/shard_map/cut_slices/pallas_call | solution.py:53
  6.0 0.7 %copy-done.1 = s32[1,2,2]{2,1,0:T(2,128)S(1)} copy-done((s32[1,2,2]{2,1,0:T(2,128)S(1)}, s32[1,2,2]{2,1,0:T(2,128)}, u32[]{:S(2)}) %copy-start.1) | copy-done | bytes 40
  6.7 0.7 %copy-done.2 = s32[256]{0:T(256)S(1)} copy-done((s32[256]{0:T(256)S(1)}, s32[256]{0:T(256)}, u32[]{:S(2)}) %copy-start.2) | copy-done | bytes 1048
  7.4 1.0 %mask_bias.1.refs_4_ = f32[256,256]{1,0:T(8,128)S(1)} custom-call(s32[1,2,2]{2,1,0:T(2,128)S(1)} %copy-done.1, s32[256]{0:T(256)S(1)} %copy-done.2), custom_call_target="tpu_custom_call" | custom-call | tf_op jit(solution)/shard_map/mask_bias/pallas_call | solution.py:342
  8.4 1.6 %load_weights.2 = (bf16[1,64,2048]{2,1,0:T(8,128)(2,1)S(1)}, bf16[1,512,2048]{2,1,0:T(8,128)(2,1)S(1)}) custom-call(bf16[1,64,2048]{2,1,0:T(8,128)(2,1)} %refs_0_.2, bf16[1,512,2048]{2,1,0:T(8,128)(2,1)} %refs_1_.1), custom_call_target="tpu_custom_call" | custom-call | bytes 4718592 | tf_op jit(solution)/shard_map/load_weights/pallas_call | solution.py:80
  10.4 2.6 %collective-permute-done.2.refs_3_ = bf16[64,1536]{1,0:T(8,128)(2,1)S(1)} collective-permute-done((bf16[64,1536]{1,0:T(8,128)(2,1)S(1)}, bf16[64,1536]{1,0:T(8,128)(2,1)S(1)}, u32[]{:S(2)}, u32[]{:S(2)}) %collective-permute-start.2) | collective-permute-done | bytes 196640 | tf_op jit(solution)/shard_map/ppermute | solution.py:25
  13.1 0.8 %attend_project.3 = (bf16[64,2048]{1,0:T(8,128)(2,1)S(1)}, bf16[64,2048]{1,0:T(8,128)(2,1)S(1)}) custom-call(bf16[64,1536]{1,0:T(8,128)(2,1)S(1)} %get-tuple-element.26.refs_0_, bf16[64,1536]{1,0:T(8,128)(2,1)S(1)} %collective-permute-done.refs_1_, bf16[64,1536]{1,0:T(8,128)(2,1)S(1)} %collective-permute-done.1.refs_2_, ...), custom_call_target="tpu_custom_call" | custom-call | flops 335544320 | bytes 786432 | tf_op jit(solution)/shard_map/attend_project/pallas_call | solution.py:127
  13.9 0.6 %collective-permute-start.4 = (bf16[64,2048]{1,0:T(8,128)(2,1)S(1)}, bf16[64,2048]{1,0:T(8,128)(2,1)S(1)}, u32[]{:S(2)}, u32[]{:S(2)}) collective-permute-start(bf16[64,2048]{1,0:T(8,128)(2,1)S(1)} %get-tuple-element.34), channel_id=1, source_target_pairs={{0,1},{1,0},{2,3},{3,2},{4,5},{5,4},{6,7},{7,6},{8,9},{9,8},{10,11... | collective-permute-start | bytes 786440 | tf_op jit(solution)/shard_map/ppermute | solution.py:25
  14.6 0.8 %attend_project.2 = (bf16[64,2048]{1,0:T(8,128)(2,1)S(1)}, bf16[64,2048]{1,0:T(8,128)(2,1)S(1)}) custom-call(bf16[64,1536]{1,0:T(8,128)(2,1)S(1)} %get-tuple-element.26.refs_0_, bf16[64,1536]{1,0:T(8,128)(2,1)S(1)} %collective-permute-done.refs_1_, bf16[64,1536]{1,0:T(8,128)(2,1)S(1)} %collective-permute-done.1.refs_2_, ...), custom_call_target="tpu_custom_call" | custom-call | flops 335544320 | bytes 786432 | tf_op jit(solution)/shard_map/attend_project/pallas_call | solution.py:127
  15.8 1.8 %collective-permute-start.6 = (bf16[64,1152]{1,0:T(8,128)(2,1)S(1)}, bf16[64,1152]{1,0:T(8,128)(2,1)S(1)}, u32[]{:S(2)}, u32[]{:S(2)}) collective-permute-start(bf16[64,1152]{1,0:T(8,128)(2,1)S(1)} %get-tuple-element.39), channel_id=1, source_target_pairs={{0,2},{1,3},{2,0},{3,1},{4,6},{5,7},{6,4},{7,5},{8,10},{9,11},{10,... | collective-permute-start | bytes 442376 | tf_op jit(solution)/shard_map/ppermute | solution.py:25
  17.7 1.5 %collective-permute-start.5 = (bf16[128,896]{1,0:T(8,128)(2,1)S(1)}, bf16[128,896]{1,0:T(8,128)(2,1)S(1)}, u32[]{:S(2)}, u32[]{:S(2)}) collective-permute-start(bf16[128,896]{1,0:T(8,128)(2,1)S(1)} %get-tuple-element.36), channel_id=1, source_target_pairs={{0,4},{1,5},{2,6},{3,7},{4,8},{5,9},{6,10},{7,11},{8,12},{9,13},{1... | collective-permute-start | bytes 688136 | tf_op jit(solution)/shard_map/ppermute | solution.py:33
  19.2 2.9 %load_weights.3.refs_5_.weight = bf16[1,2048,1536]{2,1,0:T(8,128)(2,1)S(1)} custom-call(bf16[1,2048,1536]{2,1,0:T(8,128)(2,1)} %refs_0_.3, f32[64,1152]{1,0:T(8,128)S(1)} %get-tuple-element.38.refs_1_), custom_call_target="tpu_custom_call" | custom-call | bytes 12582912 | tf_op jit(solution)/shard_map/load_weights/pallas_call | solution.py:80
  22.2 2.6 %collective-permute-start.10 = (bf16[64,1152]{1,0:T(8,128)(2,1)S(1)}, bf16[64,1152]{1,0:T(8,128)(2,1)S(1)}, u32[]{:S(2)}, u32[]{:S(2)}) collective-permute-start(bf16[64,1152]{1,0:T(8,128)(2,1)S(1)} %add_convert_fusion.after), channel_id=1, source_target_pairs={{0,6},{1,7},{2,4},{3,5},{4,10},{5,11},{6,8},{7,9},{8,14},{9,15},{1... | collective-permute-start | bytes 442376 | tf_op jit(solution)/shard_map/ppermute | solution.py:33
  24.7 1.6 %collective-permute-start.8 = (bf16[64,1152]{1,0:T(8,128)(2,1)S(1)}, bf16[64,1152]{1,0:T(8,128)(2,1)S(1)}, u32[]{:S(2)}, u32[]{:S(2)}) collective-permute-start(bf16[64,1152]{1,0:T(8,128)(2,1)S(1)} %add_convert_fusion.after), channel_id=1, source_target_pairs={{0,4},{1,5},{2,6},{3,7},{4,8},{5,9},{6,10},{7,11},{8,12},{9,13},{1... | collective-permute-start | bytes 442376 | tf_op jit(solution)/shard_map/ppermute | solution.py:33
  26.3 1.8 %collective-permute-done.5.x = bf16[128,896]{1,0:T(8,128)(2,1)S(1)} collective-permute-done((bf16[128,896]{1,0:T(8,128)(2,1)S(1)}, bf16[128,896]{1,0:T(8,128)(2,1)S(1)}, u32[]{:S(2)}, u32[]{:S(2)}) %collective-permute-start.5) | collective-permute-done | bytes 229408 | tf_op jit(solution)/shard_map/ppermute | solution.py:33
  28.1 0.6 %collective-permute-start.7 = (bf16[128,896]{1,0:T(8,128)(2,1)S(1)}, bf16[128,896]{1,0:T(8,128)(2,1)S(1)}, u32[]{:S(2)}, u32[]{:S(2)}) collective-permute-start(bf16[128,896]{1,0:T(8,128)(2,1)S(1)} %settle.1.mine), channel_id=1, source_target_pairs={{0,2},{1,3},{2,0},{3,1},{4,6},{5,7},{6,4},{7,5},{8,10},{9,11},{10,... | collective-permute-start | bytes 688136 | tf_op jit(solution)/shard_map/ppermute | solution.py:25
  28.7 3.8 %collective-permute-done.10.refs_2_ = bf16[64,1152]{1,0:T(8,128)(2,1)S(1)} collective-permute-done((bf16[64,1152]{1,0:T(8,128)(2,1)S(1)}, bf16[64,1152]{1,0:T(8,128)(2,1)S(1)}, u32[]{:S(2)}, u32[]{:S(2)}) %collective-permute-start.10) | collective-permute-done | bytes 147488 | tf_op jit(solution)/shard_map/ppermute | solution.py:33
  32.5 1.9 %collective-permute-done.8.refs_0_.rest = bf16[64,1152]{1,0:T(8,128)(2,1)S(1)} collective-permute-done((bf16[64,1152]{1,0:T(8,128)(2,1)S(1)}, bf16[64,1152]{1,0:T(8,128)(2,1)S(1)}, u32[]{:S(2)}, u32[]{:S(2)}) %collective-permute-start.8) | collective-permute-done | bytes 147488 | tf_op jit(solution)/shard_map/ppermute | solution.py:33
  34.4 1.4 %collective-permute-done.9.refs_1_ = bf16[64,1152]{1,0:T(8,128)(2,1)S(1)} collective-permute-done((bf16[64,1152]{1,0:T(8,128)(2,1)S(1)}, bf16[64,1152]{1,0:T(8,128)(2,1)S(1)}, u32[]{:S(2)}, u32[]{:S(2)}) %collective-permute-start.9) | collective-permute-done | bytes 147488 | tf_op jit(solution)/shard_map/ppermute | solution.py:25
  35.8 0.5 %collective-permute-done.7.refs_0_ = bf16[128,896]{1,0:T(8,128)(2,1)S(1)} collective-permute-done((bf16[128,896]{1,0:T(8,128)(2,1)S(1)}, bf16[128,896]{1,0:T(8,128)(2,1)S(1)}, u32[]{:S(2)}, u32[]{:S(2)}) %collective-permute-start.7) | collective-permute-done | bytes 229408 | tf_op jit(solution)/shard_map/ppermute | solution.py:25
  36.4 1.3 %project_first.1 = (f32[256,1536]{1,0:T(8,128)S(1)}, f32[256,1]{1,0:T(8,128)S(1)}) custom-call(bf16[64,1152]{1,0:T(8,128)(2,1)S(1)} %collective-permute-done.8.refs_0_.rest, bf16[64,1152]{1,0:T(8,128)(2,1)S(1)} %collective-permute-done.9.refs_1_, bf16[64,1152]{1,0:T(8,128)(2,1)S(1)} %collective-permute-done.10.refs_2_, ...), custom_call_target="tpu_custom_call" | custom-call | flops 905969664 | bytes 3538944 | tf_op jit(solution)/shard_map/project_first/pallas_call | solution.py:243
  37.9 1.9 %project_second.1 = (bf16[1,64,2048]{2,1,0:T(8,128)(2,1)}, bf16[1,256,1536]{2,1,0:T(8,128)(2,1)}) custom-call(bf16[128,896]{1,0:T(8,128)(2,1)S(1)} %join_chips.1.even, bf16[128,896]{1,0:T(8,128)(2,1)S(1)} %collective-permute-done.12.odd, bf16[64,1152]{1,0:T(8,128)(2,1)S(1)} %collective-permute-done.8.refs_0_.rest, f32[1,2048]{1,0:T(1,128)S(1)} %copy-done, ...), custom_call_target="tpu_custom_call" | custom-call | flops 704643072 | bytes 2752512 | tf_op jit(solution)/shard_map/project_second/pallas_call | solution.py:291
  (22 shorter events, 1.5 us)
Async XLA Ops:
  1.7 8.8 %collective-permute-start.1 = (bf16[64,1536]{1,0:T(8,128)(2,1)S(1)}, bf16[64,1536]{1,0:T(8,128)(2,1)S(1)}, u32[]{:S(2)}, u32[]{:S(2)}) collective-permute-start(bf16[64,1536]{1,0:T(8,128)(2,1)S(1)} %get-tuple-element.28), channel_id=1, source_target_pairs={{0,2},{1,3},{2,0},{3,1},{4,6},{5,7},{6,4},{7,5},{8,10},{9,11},{10,... | collective-permute-start | bytes 589832 | tf_op jit(solution)/shard_map/ppermute | solution.py:25
  4.7 8.4 %collective-permute-start.2 = (bf16[64,1536]{1,0:T(8,128)(2,1)S(1)}, bf16[64,1536]{1,0:T(8,128)(2,1)S(1)}, u32[]{:S(2)}, u32[]{:S(2)}) collective-permute-start(bf16[64,1536]{1,0:T(8,128)(2,1)S(1)} %get-tuple-element.25.refs_0_), channel_id=1, source_target_pairs={{0,3},{1,2},{2,1},{3,0},{4,7},{5,6},{6,5},{7,4},{8,11},{9,10},{10,... | collective-permute-start | bytes 589832 | tf_op jit(solution)/shard_map/ppermute | solution.py:25
  5.8 7.3 %collective-permute-start = (bf16[64,1536]{1,0:T(8,128)(2,1)S(1)}, bf16[64,1536]{1,0:T(8,128)(2,1)S(1)}, u32[]{:S(2)}, u32[]{:S(2)}) collective-permute-start(bf16[64,1536]{1,0:T(8,128)(2,1)S(1)} %get-tuple-element.27), channel_id=1, source_target_pairs={{0,1},{1,0},{2,3},{3,2},{4,5},{5,4},{6,7},{7,6},{8,9},{9,8},{10,11... | collective-permute-start | bytes 589832 | tf_op jit(solution)/shard_map/ppermute | solution.py:25
  6.0 0.7 %copy-start.1 = (s32[1,2,2]{2,1,0:T(2,128)S(1)}, s32[1,2,2]{2,1,0:T(2,128)}, u32[]{:S(2)}) copy-start(s32[1,2,2]{2,1,0:T(2,128)} %mask.1) | copy-start | bytes 52
  6.7 0.7 %copy-start.2 = (s32[256]{0:T(256)S(1)}, s32[256]{0:T(256)}, u32[]{:S(2)}) copy-start(s32[256]{0:T(256)} %order.1) | copy-start | bytes 3076
  13.9 1.8 %collective-permute-start.4 = (bf16[64,2048]{1,0:T(8,128)(2,1)S(1)}, bf16[64,2048]{1,0:T(8,128)(2,1)S(1)}, u32[]{:S(2)}, u32[]{:S(2)}) collective-permute-start(bf16[64,2048]{1,0:T(8,128)(2,1)S(1)} %get-tuple-element.34), channel_id=1, source_target_pairs={{0,1},{1,0},{2,3},{3,2},{4,5},{5,4},{6,7},{7,6},{8,9},{9,8},{10,11... | collective-permute-start | bytes 786440 | tf_op jit(solution)/shard_map/ppermute | solution.py:25
  14.5 3.1 %collective-permute-start.3 = (bf16[64,2048]{1,0:T(8,128)(2,1)S(1)}, bf16[64,2048]{1,0:T(8,128)(2,1)S(1)}, u32[]{:S(2)}, u32[]{:S(2)}) collective-permute-start(bf16[64,2048]{1,0:T(8,128)(2,1)S(1)} %get-tuple-element.31), channel_id=1, source_target_pairs={{0,1},{1,0},{2,3},{3,2},{4,5},{5,4},{6,7},{7,6},{8,9},{9,8},{10,11... | collective-permute-start | bytes 786440 | tf_op jit(solution)/shard_map/ppermute | solution.py:25
  15.8 6.3 %collective-permute-start.6 = (bf16[64,1152]{1,0:T(8,128)(2,1)S(1)}, bf16[64,1152]{1,0:T(8,128)(2,1)S(1)}, u32[]{:S(2)}, u32[]{:S(2)}) collective-permute-start(bf16[64,1152]{1,0:T(8,128)(2,1)S(1)} %get-tuple-element.39), channel_id=1, source_target_pairs={{0,2},{1,3},{2,0},{3,1},{4,6},{5,7},{6,4},{7,5},{8,10},{9,11},{10,... | collective-permute-start | bytes 442376 | tf_op jit(solution)/shard_map/ppermute | solution.py:25
  17.7 10.4 %collective-permute-start.5 = (bf16[128,896]{1,0:T(8,128)(2,1)S(1)}, bf16[128,896]{1,0:T(8,128)(2,1)S(1)}, u32[]{:S(2)}, u32[]{:S(2)}) collective-permute-start(bf16[128,896]{1,0:T(8,128)(2,1)S(1)} %get-tuple-element.36), channel_id=1, source_target_pairs={{0,4},{1,5},{2,6},{3,7},{4,8},{5,9},{6,10},{7,11},{8,12},{9,13},{1... | collective-permute-start | bytes 688136 | tf_op jit(solution)/shard_map/ppermute | solution.py:33
  19.2 17.2 %copy-start = (f32[1,2048]{1,0:T(1,128)S(1)}, f32[1,2048]{1,0:T(1,128)}, u32[]{:S(2)}) copy-start(f32[1,2048]{1,0:T(1,128)} %gain.1) | copy-start | bytes 24580
  22.2 10.4 %collective-permute-start.10 = (bf16[64,1152]{1,0:T(8,128)(2,1)S(1)}, bf16[64,1152]{1,0:T(8,128)(2,1)S(1)}, u32[]{:S(2)}, u32[]{:S(2)}) collective-permute-start(bf16[64,1152]{1,0:T(8,128)(2,1)S(1)} %add_convert_fusion.after), channel_id=1, source_target_pairs={{0,6},{1,7},{2,4},{3,5},{4,10},{5,11},{6,8},{7,9},{8,14},{9,15},{1... | collective-permute-start | bytes 442376 | tf_op jit(solution)/shard_map/ppermute | solution.py:33
  24.7 9.7 %collective-permute-start.8 = (bf16[64,1152]{1,0:T(8,128)(2,1)S(1)}, bf16[64,1152]{1,0:T(8,128)(2,1)S(1)}, u32[]{:S(2)}, u32[]{:S(2)}) collective-permute-start(bf16[64,1152]{1,0:T(8,128)(2,1)S(1)} %add_convert_fusion.after), channel_id=1, source_target_pairs={{0,4},{1,5},{2,6},{3,7},{4,8},{5,9},{6,10},{7,11},{8,12},{9,13},{1... | collective-permute-start | bytes 442376 | tf_op jit(solution)/shard_map/ppermute | solution.py:33
  28.1 8.1 %collective-permute-start.7 = (bf16[128,896]{1,0:T(8,128)(2,1)S(1)}, bf16[128,896]{1,0:T(8,128)(2,1)S(1)}, u32[]{:S(2)}, u32[]{:S(2)}) collective-permute-start(bf16[128,896]{1,0:T(8,128)(2,1)S(1)} %settle.1.mine), channel_id=1, source_target_pairs={{0,2},{1,3},{2,0},{3,1},{4,6},{5,7},{6,4},{7,5},{8,10},{9,11},{10,... | collective-permute-start | bytes 688136 | tf_op jit(solution)/shard_map/ppermute | solution.py:25
  32.5 1.9 %collective-permute-start.11 = (bf16[64,1152]{1,0:T(8,128)(2,1)S(1)}, bf16[64,1152]{1,0:T(8,128)(2,1)S(1)}, u32[]{:S(2)}, u32[]{:S(2)}) collective-permute-start(bf16[64,1152]{1,0:T(8,128)(2,1)S(1)} %collective-permute-done.10.refs_2_), channel_id=1, source_target_pairs={{0,1},{1,0},{2,3},{3,2},{4,5},{5,4},{6,7},{7,6},{8,9},{9,8},{10,11... | collective-permute-start | bytes 442376 | tf_op jit(solution)/shard_map/ppermute | solution.py:25
  34.4 1.4 %collective-permute-start.9 = (bf16[64,1152]{1,0:T(8,128)(2,1)S(1)}, bf16[64,1152]{1,0:T(8,128)(2,1)S(1)}, u32[]{:S(2)}, u32[]{:S(2)}) collective-permute-start(bf16[64,1152]{1,0:T(8,128)(2,1)S(1)} %collective-permute-done.8.refs_0_.rest), channel_id=1, source_target_pairs={{0,1},{1,0},{2,3},{3,2},{4,5},{5,4},{6,7},{7,6},{8,9},{9,8},{10,11... | collective-permute-start | bytes 442376 | tf_op jit(solution)/shard_map/ppermute | solution.py:25
  36.3 1.6 %collective-permute-start.12 = (bf16[128,896]{1,0:T(8,128)(2,1)S(1)}, bf16[128,896]{1,0:T(8,128)(2,1)S(1)}, u32[]{:S(2)}, u32[]{:S(2)}) collective-permute-start(bf16[128,896]{1,0:T(8,128)(2,1)S(1)} %join_chips.1.even), channel_id=1, source_target_pairs={{0,1},{1,0},{2,3},{3,2},{4,5},{5,4},{6,7},{7,6},{8,9},{9,8},{10,11... | collective-permute-start | bytes 688136 | tf_op jit(solution)/shard_map/ppermute | solution.py:25

commit v9 on v8

--- a/solution.py
+++ b/solution.py
@@ -201,8 +201,8 @@
     )(x, after)
 
 
-def join_kernel(rows, mine, *refs):
-    others, out = refs[:-1], refs[-1]
+def join_kernel(rows, spare, mine, *refs):
+    others, out = refs[: -1 - spare], refs[-1]
     for i in range(mine.shape[0] // rows):
         total = mine[i * rows : (i + 1) * rows, :].astype(jnp.float32)
         for k, other in enumerate(others):
@@ -211,54 +211,80 @@
         out[i * rows : (i + 1) * rows, :] = total.astype(jnp.bfloat16)
 
 
-def join(rows, mine, others):
-    return pl.pallas_call(
-        functools.partial(join_kernel, rows),
+def join(rows, mine, others, after):
+    return pl.pallas_call(
+        functools.partial(join_kernel, rows, len(after)),
         out_shape=jax.ShapeDtypeStruct(mine.shape, mine.dtype),
-        in_specs=[VM] * (1 + len(others)),
+        in_specs=[VM] * (1 + len(others)) + [ANY] * len(after),
         out_specs=VM,
         compiler_params=pltpu.CompilerParams(vmem_limit_bytes=SMALL_LIMIT),
         name="join_chips",
-    )(mine, *others)
-
-
-def project_first_kernel(n, *refs):
-    rest, gain, weight, total, squares, scaled = refs[:n], *refs[n:]
-    rows, count = rest[0].shape
-    cols = weight.shape[1] - count
-    me = lax.axis_index("seq")
-    for j in range(n):
-        x = rest[j][...].astype(jnp.float32)
-        here = pl.ds(pl.multiple_of((me ^ j) * rows, rows), rows)
-        squares[here, :] = jnp.sum(x * x, axis=-1, keepdims=True)
-        scaled[here, :] = (x * gain[:, cols:]).astype(jnp.bfloat16)
-    total[...] = jnp.dot(scaled[...], weight[0, cols:, :], preferred_element_type=jnp.float32)
-
-
-def project_first(rest, gain, weight):
-    n = len(rest)
-    rows, count = rest[0].shape
+    )(mine, *others, *after)
+
+
+def project_rows_kernel(count, *refs):
+    blocks, (gain, weight, total, squares, scaled) = refs[:count], refs[count:]
+    rows, cols = blocks[0].shape
+    here = slice(weight.shape[1] - cols, weight.shape[1])
+    for i, block in enumerate(blocks):
+        x = block[...].astype(jnp.float32)
+        at = slice(i * rows, (i + 1) * rows)
+        squares[at, :] = jnp.sum(x * x, axis=-1, keepdims=True)
+        scaled[at, :] = (x * gain[:, here]).astype(jnp.bfloat16)
+    total[...] = jnp.dot(scaled[...], weight[0, here, :], preferred_element_type=jnp.float32)
+
+
+def project_rows(blocks, gain, weight):
+    count = len(blocks)
+    rows, cols = blocks[0].shape
     width = weight.shape[2]
-    tokens = n * rows
-    return pl.pallas_call(
-        functools.partial(project_first_kernel, n),
+    return pl.pallas_call(
+        functools.partial(project_rows_kernel, count),
         out_shape=[
-            jax.ShapeDtypeStruct((tokens, width), jnp.float32),
-            jax.ShapeDtypeStruct((tokens, 1), jnp.float32),
-        ],
-        in_specs=[VM] * (n + 2),
+            jax.ShapeDtypeStruct((count * rows, width), jnp.float32),
+            jax.ShapeDtypeStruct((count * rows, 1), jnp.float32),
+        ],
+        in_specs=[VM] * (count + 2),
         out_specs=[VM, VM],
-        scratch_shapes=[pltpu.VMEM((tokens, count), jnp.bfloat16)],
+        scratch_shapes=[pltpu.VMEM((count * rows, cols), jnp.bfloat16)],
         compiler_params=pltpu.CompilerParams(vmem_limit_bytes=VMEM_LIMIT),
         cost_estimate=pl.CostEstimate(
-            flops=2 * tokens * count * width, bytes_accessed=2 * count * width, transcendentals=0
+            flops=2 * count * rows * cols * width, bytes_accessed=2 * cols * width, transcendentals=0
         ),
-        name="project_first",
-    )(*rest, gain, weight)
-
-
-def project_second_kernel(n, tile, even, odd, rest, gain, weight, total, squares, kept, out, scaled, sums, made, sems):
-    rows, cols = rest.shape[0], even.shape[1]
+        name="project_rows",
+    )(*blocks, gain, weight)
+
+
+def project_even_kernel(even, gain, weight, total, squares):
+    cols = even.shape[1]
+    x = even[...].astype(jnp.float32)
+    squares[...] = jnp.sum(x * x, axis=-1, keepdims=True)
+    scaled = (x * gain[:, :cols]).astype(jnp.bfloat16)
+    total[...] = jnp.dot(scaled, weight[0, :cols, :], preferred_element_type=jnp.float32)
+
+
+def project_even(even, gain, weight):
+    count, cols = even.shape
+    width = weight.shape[2]
+    return pl.pallas_call(
+        project_even_kernel,
+        out_shape=[
+            jax.ShapeDtypeStruct((count, width), jnp.float32),
+            jax.ShapeDtypeStruct((count, 1), jnp.float32),
+        ],
+        in_specs=[VM] * 3,
+        out_specs=[VM, VM],
+        compiler_params=pltpu.CompilerParams(vmem_limit_bytes=VMEM_LIMIT),
+        cost_estimate=pl.CostEstimate(
+            flops=2 * count * cols * width, bytes_accessed=2 * cols * width, transcendentals=0
+        ),
+        name="project_even",
+    )(even, gain, weight)
+
+
+def project_odd_kernel(tile, odd, even, rest, gain, weight, *refs):
+    near, near_squares, far, far_squares, even_total, even_squares, kept, out, made, sems = refs
+    rows, cols = rest.shape[0], odd.shape[1]
     depth, width = weight.shape[1:]
     me = lax.axis_index("seq")
     copies = [
@@ -267,47 +293,52 @@
     ]
     for c in copies:
         c.start()
-    for j in range(n):
-        x = (odd if j % 2 else even)[j // 2 * rows : (j // 2 + 1) * rows, :].astype(jnp.float32)
-        here = pl.ds(pl.multiple_of((me ^ j) * rows, rows), rows)
-        sums[here, :] = squares[here, :] + jnp.sum(x * x, axis=-1, keepdims=True)
-        scaled[here, :] = (x * gain[:, :cols]).astype(jnp.bfloat16)
-    scale = lax.rsqrt(sums[...] / depth + 1e-06)
+    x = odd[...].astype(jnp.float32)
+    odd_squares = jnp.sum(x * x, axis=-1, keepdims=True)
+    scaled = (x * gain[:, :cols]).astype(jnp.bfloat16)
+    places, scales = [], []
+    for j in range(2 * odd.shape[0] // rows):
+        at = pl.ds(pl.multiple_of((me ^ j) * rows, rows), rows)
+        part = slice(j // 2 * rows, (j // 2 + 1) * rows)
+        total, squares = (near, near_squares) if j < 2 else (far, far_squares)
+        here = slice(j % 2 * rows, (j % 2 + 1) * rows) if j < 2 else slice((j - 2) * rows, (j - 1) * rows)
+        mine = odd_squares[part] if j % 2 else even_squares[part, :]
+        places.append((at, part, total, here))
+        scales.append(lax.rsqrt((squares[here, :] + mine) / depth + 1e-06))
     for i in range(width // tile):
-        part = pl.ds(i * tile, tile)
-        mine = jnp.dot(scaled[...], weight[0, :cols, part], preferred_element_type=jnp.float32)
-        made[:, part] = ((total[:, part] + mine) * scale).astype(jnp.bfloat16)
-        copies.append(pltpu.make_async_copy(made.at[:, part], out.at[0, :, part], sems.at[2 + i]))
+        lanes = pl.ds(i * tile, tile)
+        product = jnp.dot(scaled, weight[0, :cols, lanes], preferred_element_type=jnp.float32)
+        for j, (at, part, total, here) in enumerate(places):
+            mine = product[part] if j % 2 else even_total[part, lanes]
+            made[at, lanes] = ((total[here, lanes] + mine) * scales[j]).astype(jnp.bfloat16)
+        copies.append(pltpu.make_async_copy(made.at[:, lanes], out.at[0, :, lanes], sems.at[2 + i]))
         copies[-1].start()
     for c in copies:
         c.wait()
 
 
-def project_second(n, even, odd, rest, gain, weight, total, squares):
+def project_odd(n, odd, even, rest, gain, weight, near, far, evens):
     rows = rest.shape[0]
-    cols = even.shape[1]
     _, depth, width = weight.shape
     tile = 256 if width % 256 == 0 else 128
     return pl.pallas_call(
-        functools.partial(project_second_kernel, n, tile),
+        functools.partial(project_odd_kernel, tile),
         out_shape=[
             jax.ShapeDtypeStruct((1, rows, depth), jnp.bfloat16),
             jax.ShapeDtypeStruct((1, n * rows, width), jnp.bfloat16),
         ],
-        in_specs=[VM] * 7,
+        in_specs=[VM] * 11,
         out_specs=[ANY, ANY],
         scratch_shapes=[
-            pltpu.VMEM((n * rows, cols), jnp.bfloat16),
-            pltpu.VMEM((n * rows, 1), jnp.float32),
             pltpu.VMEM((n * rows, width), jnp.bfloat16),
             pltpu.SemaphoreType.DMA((2 + width // tile,)),
         ],
         compiler_params=pltpu.CompilerParams(vmem_limit_bytes=VMEM_LIMIT),
         cost_estimate=pl.CostEstimate(
-            flops=2 * n * rows * cols * width, bytes_accessed=2 * cols * width, transcendentals=0
+            flops=n * rows * odd.shape[1] * width, bytes_accessed=2 * odd.shape[1] * width, transcendentals=0
         ),
-        name="project_second",
-    )(even, odd, rest, gain, weight, total, squares)
+        name="project_odd",
+    )(odd, even, rest, gain, weight, *near, *far, *evens)
 
 
 def mask_kernel(rows, mask, order, out):
@@ -373,12 +404,12 @@
     partial = settle(partial, total)
     swapped = [swap(partial, j) for j in range(2, n, 2)]
     rest = [r for x in rest for r in (x, swap(x, 1))]
-    swapped, rest = lax.optimization_barrier((swapped, rest))
-    even = join(rows, partial, swapped)
+    far_total = project_rows(rest[2:], norm_gain, proj_weight)
+    even = join(rows, partial, swapped, (*far_total, *rest[:2]))
     odd = swap(even, 1)
-    total, squares = project_first(rest, norm_gain, proj_weight)
-    kept, following = project_second(n, even, odd, rest[0], norm_gain, proj_weight, total, squares)
-    return (kept, following)
+    near_total = project_rows(rest[:2], norm_gain, proj_weight)
+    even_total = project_even(even, norm_gain, proj_weight)
+    return project_odd(n, odd, even, rest[0], norm_gain, proj_weight, near_total, far_total, even_total)
 
 
 def solution(mesh):

time: 40 us -> 39.5 us (0.988)
  waiting for transfers between devices: 12.9 us -> 12.2 us
    ppermute x10, waiting for transfers between devices: 5.3 us -> 4.65 us  [swap(): return lax.ppermute(x, 'seq', [(i, i ^ by) for i in range(size)])]
    pallas_call x3 -> x5, Pallas kernels: 3.32 us -> 3.41 us  [the longest x1 1.39 us: project_odd(): pl.pallas_call(functools.partial(project_odd_kernel, tile), out_shape=[ja...]
  transfers between devices with their start and end apart: 13 -> 13, of which waited for: 9 -> 9; matrix products, arithmetic and copies ran while one was open for 0% -> 0% of each run, Pallas kernels for 22% -> 24%
where the time goes in v9:
time: 39.5 us; the launch traced here: 39.3 us
  Pallas kernels  12.8 us (32%)
  waiting for transfers between devices  12.2 us (31%)
  starting transfers between devices  12.1 us (31%)
  local copies, waits for them, and re-layouts  1.36 us (3%)
  between operations  0.76 us (2%)
    ppermute x3, waiting for transfers between devices, onward(): return lax.ppermute(x, ('segment', 'seq'), pairs)  7.56 us
    ppermute x10, starting transfers between devices, swap(): return lax.ppermute(x, 'seq', [(i, i ^ by) for i in range(size)])  6.48 us
    ppermute x3, starting transfers between devices, onward(): return lax.ppermute(x, ('segment', 'seq'), pairs)  5.65 us
    ppermute x10, waiting for transfers between devices, swap(): return lax.ppermute(x, 'seq', [(i, i ^ by) for i in range(size)])  4.65 us
    pallas_call x2, Pallas kernels, load(): pl.pallas_call(functools.partial(load_kernel, pieces), out_shape=[pltpu.V...  4.51 us
    pallas_call x2, Pallas kernels, cut(): pl.pallas_call(functools.partial(cut_kernel, js), out_shape=[pltpu.VMEM((...  2.09 us
    pallas_call x2, Pallas kernels, attend(): pl.pallas_call(functools.partial(attend_project_kernel, n, js), out_shape...  1.61 us
    pallas_call x1, Pallas kernels, project_odd(): pl.pallas_call(functools.partial(project_odd_kernel, tile), out_shape=[ja...  1.39 us
  transfers between devices with their start and end apart: 13, of which 9 were waited for; matrix products, arithmetic and copies ran while one was open for 0% of the time, Pallas kernels for 24%

profile of v9, /device:TPU:0, one launch (start us, length us, event | category | flops | bytes accessed | tf_op | source)
XLA Modules:
  0.0 39.3 jit_solution(8558884529418874825)
XLA Ops:
  0.6 1.0 %cut_slices.2 = (bf16[64,1536]{1,0:T(8,128)(2,1)S(1)}, bf16[64,1536]{1,0:T(8,128)(2,1)S(1)}) custom-call(bf16[1,64,6144]{2,1,0:T(8,128)(2,1)} %src.3), custom_call_target="tpu_custom_call" | custom-call | tf_op jit(solution)/shard_map/cut_slices/pallas_call | solution.py:53
  1.7 3.0 %collective-permute-start.1 = (bf16[64,1536]{1,0:T(8,128)(2,1)S(1)}, bf16[64,1536]{1,0:T(8,128)(2,1)S(1)}, u32[]{:S(2)}, u32[]{:S(2)}) collective-permute-start(bf16[64,1536]{1,0:T(8,128)(2,1)S(1)} %get-tuple-element.27), channel_id=1, source_target_pairs={{0,2},{1,3},{2,0},{3,1},{4,6},{5,7},{6,4},{7,5},{8,10},{9,11},{10,... | collective-permute-start | bytes 589832 | tf_op jit(solution)/shard_map/ppermute | solution.py:25
  4.7 1.0 %cut_slices.3 = (bf16[64,1536]{1,0:T(8,128)(2,1)S(1)}, bf16[64,1536]{1,0:T(8,128)(2,1)S(1)}) custom-call(bf16[1,64,6144]{2,1,0:T(8,128)(2,1)} %src.3, bf16[64,1536]{1,0:T(8,128)(2,1)S(1)} %get-tuple-element.24.refs_0_), custom_call_target="tpu_custom_call" | custom-call | tf_op jit(solution)/shard_map/cut_slices/pallas_call | solution.py:53
  6.0 0.7 %copy-done.1 = s32[1,2,2]{2,1,0:T(2,128)S(1)} copy-done((s32[1,2,2]{2,1,0:T(2,128)S(1)}, s32[1,2,2]{2,1,0:T(2,128)}, u32[]{:S(2)}) %copy-start.1) | copy-done | bytes 40
  6.7 0.7 %copy-done.2 = s32[256]{0:T(256)S(1)} copy-done((s32[256]{0:T(256)S(1)}, s32[256]{0:T(256)}, u32[]{:S(2)}) %copy-start.2) | copy-done | bytes 1048
  7.4 1.0 %mask_bias.1.refs_4_ = f32[256,256]{1,0:T(8,128)S(1)} custom-call(s32[1,2,2]{2,1,0:T(2,128)S(1)} %copy-done.1, s32[256]{0:T(256)S(1)} %copy-done.2), custom_call_target="tpu_custom_call" | custom-call | tf_op jit(solution)/shard_map/mask_bias/pallas_call | solution.py:373
  8.4 1.6 %load_weights.2 = (bf16[1,64,2048]{2,1,0:T(8,128)(2,1)S(1)}, bf16[1,512,2048]{2,1,0:T(8,128)(2,1)S(1)}) custom-call(bf16[1,64,2048]{2,1,0:T(8,128)(2,1)} %refs_0_.2, bf16[1,512,2048]{2,1,0:T(8,128)(2,1)} %refs_1_.1), custom_call_target="tpu_custom_call" | custom-call | bytes 4718592 | tf_op jit(solution)/shard_map/load_weights/pallas_call | solution.py:80
  10.4 2.6 %collective-permute-done.2.refs_3_ = bf16[64,1536]{1,0:T(8,128)(2,1)S(1)} collective-permute-done((bf16[64,1536]{1,0:T(8,128)(2,1)S(1)}, bf16[64,1536]{1,0:T(8,128)(2,1)S(1)}, u32[]{:S(2)}, u32[]{:S(2)}) %collective-permute-start.2) | collective-permute-done | bytes 196640 | tf_op jit(solution)/shard_map/ppermute | solution.py:25
  13.1 0.8 %attend_project.3 = (bf16[64,2048]{1,0:T(8,128)(2,1)S(1)}, bf16[64,2048]{1,0:T(8,128)(2,1)S(1)}) custom-call(bf16[64,1536]{1,0:T(8,128)(2,1)S(1)} %get-tuple-element.25.refs_0_, bf16[64,1536]{1,0:T(8,128)(2,1)S(1)} %collective-permute-done.refs_1_, bf16[64,1536]{1,0:T(8,128)(2,1)S(1)} %collective-permute-done.1.refs_2_, ...), custom_call_target="tpu_custom_call" | custom-call | flops 335544320 | bytes 786432 | tf_op jit(solution)/shard_map/attend_project/pallas_call | solution.py:127
  13.9 0.6 %collective-permute-start.4 = (bf16[64,2048]{1,0:T(8,128)(2,1)S(1)}, bf16[64,2048]{1,0:T(8,128)(2,1)S(1)}, u32[]{:S(2)}, u32[]{:S(2)}) collective-permute-start(bf16[64,2048]{1,0:T(8,128)(2,1)S(1)} %get-tuple-element.33), channel_id=1, source_target_pairs={{0,1},{1,0},{2,3},{3,2},{4,5},{5,4},{6,7},{7,6},{8,9},{9,8},{10,11... | collective-permute-start | bytes 786440 | tf_op jit(solution)/shard_map/ppermute | solution.py:25
  14.6 0.8 %attend_project.2 = (bf16[64,2048]{1,0:T(8,128)(2,1)S(1)}, bf16[64,2048]{1,0:T(8,128)(2,1)S(1)}) custom-call(bf16[64,1536]{1,0:T(8,128)(2,1)S(1)} %get-tuple-element.25.refs_0_, bf16[64,1536]{1,0:T(8,128)(2,1)S(1)} %collective-permute-done.refs_1_, bf16[64,1536]{1,0:T(8,128)(2,1)S(1)} %collective-permute-done.1.refs_2_, ...), custom_call_target="tpu_custom_call" | custom-call | flops 335544320 | bytes 786432 | tf_op jit(solution)/shard_map/attend_project/pallas_call | solution.py:127
  15.8 1.8 %collective-permute-start.6 = (bf16[64,1152]{1,0:T(8,128)(2,1)S(1)}, bf16[64,1152]{1,0:T(8,128)(2,1)S(1)}, u32[]{:S(2)}, u32[]{:S(2)}) collective-permute-start(bf16[64,1152]{1,0:T(8,128)(2,1)S(1)} %get-tuple-element.38), channel_id=1, source_target_pairs={{0,2},{1,3},{2,0},{3,1},{4,6},{5,7},{6,4},{7,5},{8,10},{9,11},{10,... | collective-permute-start | bytes 442376 | tf_op jit(solution)/shard_map/ppermute | solution.py:25
  17.7 1.5 %collective-permute-start.5 = (bf16[128,896]{1,0:T(8,128)(2,1)S(1)}, bf16[128,896]{1,0:T(8,128)(2,1)S(1)}, u32[]{:S(2)}, u32[]{:S(2)}) collective-permute-start(bf16[128,896]{1,0:T(8,128)(2,1)S(1)} %get-tuple-element.35), channel_id=1, source_target_pairs={{0,4},{1,5},{2,6},{3,7},{4,8},{5,9},{6,10},{7,11},{8,12},{9,13},{1... | collective-permute-start | bytes 688136 | tf_op jit(solution)/shard_map/ppermute | solution.py:33
  19.2 2.9 %load_weights.3.refs_3_.weight = bf16[1,2048,1536]{2,1,0:T(8,128)(2,1)S(1)} custom-call(bf16[1,2048,1536]{2,1,0:T(8,128)(2,1)} %refs_0_.3, f32[64,1152]{1,0:T(8,128)S(1)} %get-tuple-element.37.refs_1_), custom_call_target="tpu_custom_call" | custom-call | bytes 12582912 | tf_op jit(solution)/shard_map/load_weights/pallas_call | solution.py:80
  22.2 2.6 %collective-permute-start.8 = (bf16[64,1152]{1,0:T(8,128)(2,1)S(1)}, bf16[64,1152]{1,0:T(8,128)(2,1)S(1)}, u32[]{:S(2)}, u32[]{:S(2)}) collective-permute-start(bf16[64,1152]{1,0:T(8,128)(2,1)S(1)} %add_convert_fusion.after), channel_id=1, source_target_pairs={{0,6},{1,7},{2,4},{3,5},{4,10},{5,11},{6,8},{7,9},{8,14},{9,15},{1... | collective-permute-start | bytes 442376 | tf_op jit(solution)/shard_map/ppermute | solution.py:33
  24.7 1.6 %collective-permute-start.10 = (bf16[64,1152]{1,0:T(8,128)(2,1)S(1)}, bf16[64,1152]{1,0:T(8,128)(2,1)S(1)}, u32[]{:S(2)}, u32[]{:S(2)}) collective-permute-start(bf16[64,1152]{1,0:T(8,128)(2,1)S(1)} %add_convert_fusion.after), channel_id=1, source_target_pairs={{0,4},{1,5},{2,6},{3,7},{4,8},{5,9},{6,10},{7,11},{8,12},{9,13},{1... | collective-permute-start | bytes 442376 | tf_op jit(solution)/shard_map/ppermute | solution.py:33
  26.3 1.8 %collective-permute-done.5.x = bf16[128,896]{1,0:T(8,128)(2,1)S(1)} collective-permute-done((bf16[128,896]{1,0:T(8,128)(2,1)S(1)}, bf16[128,896]{1,0:T(8,128)(2,1)S(1)}, u32[]{:S(2)}, u32[]{:S(2)}) %collective-permute-start.5) | collective-permute-done | bytes 229408 | tf_op jit(solution)/shard_map/ppermute | solution.py:33
  28.7 3.8 %collective-permute-done.8.refs_0_ = bf16[64,1152]{1,0:T(8,128)(2,1)S(1)} collective-permute-done((bf16[64,1152]{1,0:T(8,128)(2,1)S(1)}, bf16[64,1152]{1,0:T(8,128)(2,1)S(1)}, u32[]{:S(2)}, u32[]{:S(2)}) %collective-permute-start.8) | collective-permute-done | bytes 147488 | tf_op jit(solution)/shard_map/ppermute | solution.py:33
  32.5 1.9 %collective-permute-done.10.refs_3_.refs_0_.rest = bf16[64,1152]{1,0:T(8,128)(2,1)S(1)} collective-permute-done((bf16[64,1152]{1,0:T(8,128)(2,1)S(1)}, bf16[64,1152]{1,0:T(8,128)(2,1)S(1)}, u32[]{:S(2)}, u32[]{:S(2)}) %collective-permute-start.10) | collective-permute-done | bytes 147488 | tf_op jit(solution)/shard_map/ppermute | solution.py:33
  34.4 0.7 %project_rows.2 = (f32[128,1536]{1,0:T(8,128)S(1)}, f32[128,1]{1,0:T(8,128)S(1)}) custom-call(bf16[64,1152]{1,0:T(8,128)(2,1)S(1)} %collective-permute-done.8.refs_0_, bf16[64,1152]{1,0:T(8,128)(2,1)S(1)} %collective-permute-done.9.refs_1_, f32[1,2048]{1,0:T(1,128)S(1)} %copy-done, bf16[1,2048,1536]{2,1,0:T(8,128)(2,1)S(1)} %load_weights.3.refs_3_.weight), custom_call_target="tpu_custom_call" | custom-call | flops 452984832 | bytes 3538944 | tf_op jit(solution)/shard_map/project_rows/pallas_call | solution.py:241
  35.1 0.7 %collective-permute-done.11.refs_4_.refs_1_ = bf16[64,1152]{1,0:T(8,128)(2,1)S(1)} collective-permute-done((bf16[64,1152]{1,0:T(8,128)(2,1)S(1)}, bf16[64,1152]{1,0:T(8,128)(2,1)S(1)}, u32[]{:S(2)}, u32[]{:S(2)}) %collective-permute-start.11) | collective-permute-done | bytes 147488 | tf_op jit(solution)/shard_map/ppermute | solution.py:25
  36.4 0.7 %project_rows.3 = (f32[128,1536]{1,0:T(8,128)S(1)}, f32[128,1]{1,0:T(8,128)S(1)}) custom-call(bf16[64,1152]{1,0:T(8,128)(2,1)S(1)} %collective-permute-done.10.refs_3_.refs_0_.rest, bf16[64,1152]{1,0:T(8,128)(2,1)S(1)} %collective-permute-done.11.refs_4_.refs_1_, f32[1,2048]{1,0:T(1,128)S(1)} %copy-done, bf16[1,2048,1536]{2,1,0:T(8,128)(2,1)S(1)} %load_weights.3.refs_3_.weight), custom_call_target="tpu_custom_call" | custom-call | flops 452984832 | bytes 3538944 | tf_op jit(solution)/shard_map/project_rows/pallas_call | solution.py:241
  37.1 0.6 %project_even.1 = (f32[128,1536]{1,0:T(8,128)S(1)}, f32[128,1]{1,0:T(8,128)S(1)}) custom-call(bf16[128,896]{1,0:T(8,128)(2,1)S(1)} %join_chips.1.even, f32[1,2048]{1,0:T(1,128)S(1)} %copy-done, bf16[1,2048,1536]{2,1,0:T(8,128)(2,1)S(1)} %load_weights.3.refs_3_.weight), custom_call_target="tpu_custom_call" | custom-call | flops 352321536 | bytes 2752512 | tf_op jit(solution)/shard_map/project_even/pallas_call | solution.py:269
  37.9 1.4 %project_odd.1 = (bf16[1,64,2048]{2,1,0:T(8,128)(2,1)}, bf16[1,256,1536]{2,1,0:T(8,128)(2,1)}) custom-call(bf16[128,896]{1,0:T(8,128)(2,1)S(1)} %collective-permute-done.12.odd, bf16[128,896]{1,0:T(8,128)(2,1)S(1)} %join_chips.1.even, bf16[64,1152]{1,0:T(8,128)(2,1)S(1)} %collective-permute-done.10.refs_3_.refs_0_.rest, f32[1,2048]{1,0:T(1,128)S(1)} %copy-done, ...), custom_call_target="tpu_custom_call" | custom-call | flops 352321536 | bytes 2752512 | tf_op jit(solution)/shard_map/project_odd/pallas_call | solution.py:324
  (24 shorter events, 2.6 us)
Async XLA Ops:
  1.7 8.8 %collective-permute-start.1 = (bf16[64,1536]{1,0:T(8,128)(2,1)S(1)}, bf16[64,1536]{1,0:T(8,128)(2,1)S(1)}, u32[]{:S(2)}, u32[]{:S(2)}) collective-permute-start(bf16[64,1536]{1,0:T(8,128)(2,1)S(1)} %get-tuple-element.27), channel_id=1, source_target_pairs={{0,2},{1,3},{2,0},{3,1},{4,6},{5,7},{6,4},{7,5},{8,10},{9,11},{10,... | collective-permute-start | bytes 589832 | tf_op jit(solution)/shard_map/ppermute | solution.py:25
  4.7 8.4 %collective-permute-start.2 = (bf16[64,1536]{1,0:T(8,128)(2,1)S(1)}, bf16[64,1536]{1,0:T(8,128)(2,1)S(1)}, u32[]{:S(2)}, u32[]{:S(2)}) collective-permute-start(bf16[64,1536]{1,0:T(8,128)(2,1)S(1)} %get-tuple-element.24.refs_0_), channel_id=1, source_target_pairs={{0,3},{1,2},{2,1},{3,0},{4,7},{5,6},{6,5},{7,4},{8,11},{9,10},{10,... | collective-permute-start | bytes 589832 | tf_op jit(solution)/shard_map/ppermute | solution.py:25
  5.8 7.3 %collective-permute-start = (bf16[64,1536]{1,0:T(8,128)(2,1)S(1)}, bf16[64,1536]{1,0:T(8,128)(2,1)S(1)}, u32[]{:S(2)}, u32[]{:S(2)}) collective-permute-start(bf16[64,1536]{1,0:T(8,128)(2,1)S(1)} %get-tuple-element.26), channel_id=1, source_target_pairs={{0,1},{1,0},{2,3},{3,2},{4,5},{5,4},{6,7},{7,6},{8,9},{9,8},{10,11... | collective-permute-start | bytes 589832 | tf_op jit(solution)/shard_map/ppermute | solution.py:25
  6.0 0.7 %copy-start.1 = (s32[1,2,2]{2,1,0:T(2,128)S(1)}, s32[1,2,2]{2,1,0:T(2,128)}, u32[]{:S(2)}) copy-start(s32[1,2,2]{2,1,0:T(2,128)} %mask.1) | copy-start | bytes 52
  6.7 0.7 %copy-start.2 = (s32[256]{0:T(256)S(1)}, s32[256]{0:T(256)}, u32[]{:S(2)}) copy-start(s32[256]{0:T(256)} %order.1) | copy-start | bytes 3076
  13.9 1.8 %collective-permute-start.4 = (bf16[64,2048]{1,0:T(8,128)(2,1)S(1)}, bf16[64,2048]{1,0:T(8,128)(2,1)S(1)}, u32[]{:S(2)}, u32[]{:S(2)}) collective-permute-start(bf16[64,2048]{1,0:T(8,128)(2,1)S(1)} %get-tuple-element.33), channel_id=1, source_target_pairs={{0,1},{1,0},{2,3},{3,2},{4,5},{5,4},{6,7},{7,6},{8,9},{9,8},{10,11... | collective-permute-start | bytes 786440 | tf_op jit(solution)/shard_map/ppermute | solution.py:25
  14.5 3.1 %collective-permute-start.3 = (bf16[64,2048]{1,0:T(8,128)(2,1)S(1)}, bf16[64,2048]{1,0:T(8,128)(2,1)S(1)}, u32[]{:S(2)}, u32[]{:S(2)}) collective-permute-start(bf16[64,2048]{1,0:T(8,128)(2,1)S(1)} %get-tuple-element.30), channel_id=1, source_target_pairs={{0,1},{1,0},{2,3},{3,2},{4,5},{5,4},{6,7},{7,6},{8,9},{9,8},{10,11... | collective-permute-start | bytes 786440 | tf_op jit(solution)/shard_map/ppermute | solution.py:25
  15.8 6.3 %collective-permute-start.6 = (bf16[64,1152]{1,0:T(8,128)(2,1)S(1)}, bf16[64,1152]{1,0:T(8,128)(2,1)S(1)}, u32[]{:S(2)}, u32[]{:S(2)}) collective-permute-start(bf16[64,1152]{1,0:T(8,128)(2,1)S(1)} %get-tuple-element.38), channel_id=1, source_target_pairs={{0,2},{1,3},{2,0},{3,1},{4,6},{5,7},{6,4},{7,5},{8,10},{9,11},{10,... | collective-permute-start | bytes 442376 | tf_op jit(solution)/shard_map/ppermute | solution.py:25
  17.7 10.4 %collective-permute-start.5 = (bf16[128,896]{1,0:T(8,128)(2,1)S(1)}, bf16[128,896]{1,0:T(8,128)(2,1)S(1)}, u32[]{:S(2)}, u32[]{:S(2)}) collective-permute-start(bf16[128,896]{1,0:T(8,128)(2,1)S(1)} %get-tuple-element.35), channel_id=1, source_target_pairs={{0,4},{1,5},{2,6},{3,7},{4,8},{5,9},{6,10},{7,11},{8,12},{9,13},{1... | collective-permute-start | bytes 688136 | tf_op jit(solution)/shard_map/ppermute | solution.py:33
  19.2 15.2 %copy-start = (f32[1,2048]{1,0:T(1,128)S(1)}, f32[1,2048]{1,0:T(1,128)}, u32[]{:S(2)}) copy-start(f32[1,2048]{1,0:T(1,128)} %gain.3) | copy-start | bytes 24580
  22.2 10.4 %collective-permute-start.8 = (bf16[64,1152]{1,0:T(8,128)(2,1)S(1)}, bf16[64,1152]{1,0:T(8,128)(2,1)S(1)}, u32[]{:S(2)}, u32[]{:S(2)}) collective-permute-start(bf16[64,1152]{1,0:T(8,128)(2,1)S(1)} %add_convert_fusion.after), channel_id=1, source_target_pairs={{0,6},{1,7},{2,4},{3,5},{4,10},{5,11},{6,8},{7,9},{8,14},{9,15},{1... | collective-permute-start | bytes 442376 | tf_op jit(solution)/shard_map/ppermute | solution.py:33
  24.7 9.7 %collective-permute-start.10 = (bf16[64,1152]{1,0:T(8,128)(2,1)S(1)}, bf16[64,1152]{1,0:T(8,128)(2,1)S(1)}, u32[]{:S(2)}, u32[]{:S(2)}) collective-permute-start(bf16[64,1152]{1,0:T(8,128)(2,1)S(1)} %add_convert_fusion.after), channel_id=1, source_target_pairs={{0,4},{1,5},{2,6},{3,7},{4,8},{5,9},{6,10},{7,11},{8,12},{9,13},{1... | collective-permute-start | bytes 442376 | tf_op jit(solution)/shard_map/ppermute | solution.py:33
  28.1 8.1 %collective-permute-start.7 = (bf16[128,896]{1,0:T(8,128)(2,1)S(1)}, bf16[128,896]{1,0:T(8,128)(2,1)S(1)}, u32[]{:S(2)}, u32[]{:S(2)}) collective-permute-start(bf16[128,896]{1,0:T(8,128)(2,1)S(1)} %settle.1.mine), channel_id=1, source_target_pairs={{0,2},{1,3},{2,0},{3,1},{4,6},{5,7},{6,4},{7,5},{8,10},{9,11},{10,... | collective-permute-start | bytes 688136 | tf_op jit(solution)/shard_map/ppermute | solution.py:25
  32.5 1.9 %collective-permute-start.9 = (bf16[64,1152]{1,0:T(8,128)(2,1)S(1)}, bf16[64,1152]{1,0:T(8,128)(2,1)S(1)}, u32[]{:S(2)}, u32[]{:S(2)}) collective-permute-start(bf16[64,1152]{1,0:T(8,128)(2,1)S(1)} %collective-permute-done.8.refs_0_), channel_id=1, source_target_pairs={{0,1},{1,0},{2,3},{3,2},{4,5},{5,4},{6,7},{7,6},{8,9},{9,8},{10,11... | collective-permute-start | bytes 442376 | tf_op jit(solution)/shard_map/ppermute | solution.py:25
  34.4 1.4 %collective-permute-start.11 = (bf16[64,1152]{1,0:T(8,128)(2,1)S(1)}, bf16[64,1152]{1,0:T(8,128)(2,1)S(1)}, u32[]{:S(2)}, u32[]{:S(2)}) collective-permute-start(bf16[64,1152]{1,0:T(8,128)(2,1)S(1)} %collective-permute-done.10.refs_3_.refs_0_.rest), channel_id=1, source_target_pairs={{0,1},{1,0},{2,3},{3,2},{4,5},{5,4},{6,7},{7,6},{8,9},{9,8},{10,11... | collective-permute-start | bytes 442376 | tf_op jit(solution)/shard_map/ppermute | solution.py:25
  36.3 1.6 %collective-permute-start.12 = (bf16[128,896]{1,0:T(8,128)(2,1)S(1)}, bf16[128,896]{1,0:T(8,128)(2,1)S(1)}, u32[]{:S(2)}, u32[]{:S(2)}) collective-permute-start(bf16[128,896]{1,0:T(8,128)(2,1)S(1)} %join_chips.1.even), channel_id=1, source_target_pairs={{0,1},{1,0},{2,3},{3,2},{4,5},{5,4},{6,7},{7,6},{8,9},{9,8},{10,11... | collective-permute-start | bytes 688136 | tf_op jit(solution)/shard_map/ppermute | solution.py:25

commit v10 on v9

--- a/solution.py
+++ b/solution.py
@@ -113,10 +113,13 @@
 
 def attend_project_kernel(n, js, *refs):
     blocks, bias, weight, near, far = refs[:n], refs[n], refs[n + 1], refs[n + 2], refs[n + 3]
-    term = jnp.dot(attention(blocks, bias, js), weight[0], preferred_element_type=jnp.float32).astype(jnp.bfloat16)
-    rows = near.shape[0]
-    near[...] = term[:rows]
-    far[...] = term[rows:]
+    attended = attention(blocks, bias, js)
+    rows, depth = near.shape
+    for i in range(4):
+        part = slice(i * depth // 4, (i + 1) * depth // 4)
+        term = jnp.dot(attended, weight[0, :, part], preferred_element_type=jnp.float32).astype(jnp.bfloat16)
+        near[:, part] = term[:rows]
+        far[:, part] = term[rows:]
 
 
 def attend(blocks, bias, js, weight):

time: 39.5 us -> 39.5 us (level)
  no operation moved by 1% of the time
where the time goes in v10:
time: 39.5 us; the launch traced here: 39.3 us
  Pallas kernels  12.8 us (32%)
  waiting for transfers between devices  12.2 us (31%)
  starting transfers between devices  12.1 us (31%)
  local copies, waits for them, and re-layouts  1.36 us (3%)
  between operations  0.76 us (2%)
    ppermute x3, waiting for transfers between devices, onward(): return lax.ppermute(x, ('segment', 'seq'), pairs)  7.56 us
    ppermute x10, starting transfers between devices, swap(): return lax.ppermute(x, 'seq', [(i, i ^ by) for i in range(size)])  6.48 us
    ppermute x3, starting transfers between devices, onward(): return lax.ppermute(x, ('segment', 'seq'), pairs)  5.65 us
    ppermute x10, waiting for transfers between devices, swap(): return lax.ppermute(x, 'seq', [(i, i ^ by) for i in range(size)])  4.65 us
    pallas_call x2, Pallas kernels, load(): pl.pallas_call(functools.partial(load_kernel, pieces), out_shape=[pltpu.V...  4.51 us
    pallas_call x2, Pallas kernels, cut(): pl.pallas_call(functools.partial(cut_kernel, js), out_shape=[pltpu.VMEM((...  2.09 us
    pallas_call x2, Pallas kernels, attend(): pl.pallas_call(functools.partial(attend_project_kernel, n, js), out_shape...  1.61 us
    pallas_call x1, Pallas kernels, project_odd(): pl.pallas_call(functools.partial(project_odd_kernel, tile), out_shape=[ja...  1.39 us
  transfers between devices with their start and end apart: 13, of which 9 were waited for; matrix products, arithmetic and copies ran while one was open for 0% of the time, Pallas kernels for 24%

profile of v10, /device:TPU:0, one launch (start us, length us, event | category | flops | bytes accessed | tf_op | source)
XLA Modules:
  0.0 39.3 jit_solution(8558884529418874825)
XLA Ops:
  0.6 1.0 %cut_slices.2 = (bf16[64,1536]{1,0:T(8,128)(2,1)S(1)}, bf16[64,1536]{1,0:T(8,128)(2,1)S(1)}) custom-call(bf16[1,64,6144]{2,1,0:T(8,128)(2,1)} %src.3), custom_call_target="tpu_custom_call" | custom-call | tf_op jit(solution)/shard_map/cut_slices/pallas_call | solution.py:53
  1.7 3.0 %collective-permute-start.1 = (bf16[64,1536]{1,0:T(8,128)(2,1)S(1)}, bf16[64,1536]{1,0:T(8,128)(2,1)S(1)}, u32[]{:S(2)}, u32[]{:S(2)}) collective-permute-start(bf16[64,1536]{1,0:T(8,128)(2,1)S(1)} %get-tuple-element.27), channel_id=1, source_target_pairs={{0,2},{1,3},{2,0},{3,1},{4,6},{5,7},{6,4},{7,5},{8,10},{9,11},{10,... | collective-permute-start | bytes 589832 | tf_op jit(solution)/shard_map/ppermute | solution.py:25
  4.7 1.0 %cut_slices.3 = (bf16[64,1536]{1,0:T(8,128)(2,1)S(1)}, bf16[64,1536]{1,0:T(8,128)(2,1)S(1)}) custom-call(bf16[1,64,6144]{2,1,0:T(8,128)(2,1)} %src.3, bf16[64,1536]{1,0:T(8,128)(2,1)S(1)} %get-tuple-element.24.refs_0_), custom_call_target="tpu_custom_call" | custom-call | tf_op jit(solution)/shard_map/cut_slices/pallas_call | solution.py:53
  6.0 0.7 %copy-done.1 = s32[1,2,2]{2,1,0:T(2,128)S(1)} copy-done((s32[1,2,2]{2,1,0:T(2,128)S(1)}, s32[1,2,2]{2,1,0:T(2,128)}, u32[]{:S(2)}) %copy-start.1) | copy-done | bytes 40
  6.7 0.7 %copy-done.2 = s32[256]{0:T(256)S(1)} copy-done((s32[256]{0:T(256)S(1)}, s32[256]{0:T(256)}, u32[]{:S(2)}) %copy-start.2) | copy-done | bytes 1048
  7.4 1.0 %mask_bias.1.refs_4_ = f32[256,256]{1,0:T(8,128)S(1)} custom-call(s32[1,2,2]{2,1,0:T(2,128)S(1)} %copy-done.1, s32[256]{0:T(256)S(1)} %copy-done.2), custom_call_target="tpu_custom_call" | custom-call | tf_op jit(solution)/shard_map/mask_bias/pallas_call | solution.py:376
  8.4 1.6 %load_weights.2 = (bf16[1,64,2048]{2,1,0:T(8,128)(2,1)S(1)}, bf16[1,512,2048]{2,1,0:T(8,128)(2,1)S(1)}) custom-call(bf16[1,64,2048]{2,1,0:T(8,128)(2,1)} %refs_0_.2, bf16[1,512,2048]{2,1,0:T(8,128)(2,1)} %refs_1_.1), custom_call_target="tpu_custom_call" | custom-call | bytes 4718592 | tf_op jit(solution)/shard_map/load_weights/pallas_call | solution.py:80
  10.4 2.6 %collective-permute-done.2.refs_3_ = bf16[64,1536]{1,0:T(8,128)(2,1)S(1)} collective-permute-done((bf16[64,1536]{1,0:T(8,128)(2,1)S(1)}, bf16[64,1536]{1,0:T(8,128)(2,1)S(1)}, u32[]{:S(2)}, u32[]{:S(2)}) %collective-permute-start.2) | collective-permute-done | bytes 196640 | tf_op jit(solution)/shard_map/ppermute | solution.py:25
  13.1 0.8 %attend_project.3 = (bf16[64,2048]{1,0:T(8,128)(2,1)S(1)}, bf16[64,2048]{1,0:T(8,128)(2,1)S(1)}) custom-call(bf16[64,1536]{1,0:T(8,128)(2,1)S(1)} %get-tuple-element.25.refs_0_, bf16[64,1536]{1,0:T(8,128)(2,1)S(1)} %collective-permute-done.refs_1_, bf16[64,1536]{1,0:T(8,128)(2,1)S(1)} %collective-permute-done.1.refs_2_, ...), custom_call_target="tpu_custom_call" | custom-call | flops 335544320 | bytes 786432 | tf_op jit(solution)/shard_map/attend_project/pallas_call | solution.py:130
  13.9 0.6 %collective-permute-start.4 = (bf16[64,2048]{1,0:T(8,128)(2,1)S(1)}, bf16[64,2048]{1,0:T(8,128)(2,1)S(1)}, u32[]{:S(2)}, u32[]{:S(2)}) collective-permute-start(bf16[64,2048]{1,0:T(8,128)(2,1)S(1)} %get-tuple-element.33), channel_id=1, source_target_pairs={{0,1},{1,0},{2,3},{3,2},{4,5},{5,4},{6,7},{7,6},{8,9},{9,8},{10,11... | collective-permute-start | bytes 786440 | tf_op jit(solution)/shard_map/ppermute | solution.py:25
  14.6 0.8 %attend_project.2 = (bf16[64,2048]{1,0:T(8,128)(2,1)S(1)}, bf16[64,2048]{1,0:T(8,128)(2,1)S(1)}) custom-call(bf16[64,1536]{1,0:T(8,128)(2,1)S(1)} %get-tuple-element.25.refs_0_, bf16[64,1536]{1,0:T(8,128)(2,1)S(1)} %collective-permute-done.refs_1_, bf16[64,1536]{1,0:T(8,128)(2,1)S(1)} %collective-permute-done.1.refs_2_, ...), custom_call_target="tpu_custom_call" | custom-call | flops 335544320 | bytes 786432 | tf_op jit(solution)/shard_map/attend_project/pallas_call | solution.py:130
  15.8 1.8 %collective-permute-start.6 = (bf16[64,1152]{1,0:T(8,128)(2,1)S(1)}, bf16[64,1152]{1,0:T(8,128)(2,1)S(1)}, u32[]{:S(2)}, u32[]{:S(2)}) collective-permute-start(bf16[64,1152]{1,0:T(8,128)(2,1)S(1)} %get-tuple-element.38), channel_id=1, source_target_pairs={{0,2},{1,3},{2,0},{3,1},{4,6},{5,7},{6,4},{7,5},{8,10},{9,11},{10,... | collective-permute-start | bytes 442376 | tf_op jit(solution)/shard_map/ppermute | solution.py:25
  17.7 1.5 %collective-permute-start.5 = (bf16[128,896]{1,0:T(8,128)(2,1)S(1)}, bf16[128,896]{1,0:T(8,128)(2,1)S(1)}, u32[]{:S(2)}, u32[]{:S(2)}) collective-permute-start(bf16[128,896]{1,0:T(8,128)(2,1)S(1)} %get-tuple-element.35), channel_id=1, source_target_pairs={{0,4},{1,5},{2,6},{3,7},{4,8},{5,9},{6,10},{7,11},{8,12},{9,13},{1... | collective-permute-start | bytes 688136 | tf_op jit(solution)/shard_map/ppermute | solution.py:33
  19.2 2.9 %load_weights.3.refs_3_.weight = bf16[1,2048,1536]{2,1,0:T(8,128)(2,1)S(1)} custom-call(bf16[1,2048,1536]{2,1,0:T(8,128)(2,1)} %refs_0_.3, f32[64,1152]{1,0:T(8,128)S(1)} %get-tuple-element.37.refs_1_), custom_call_target="tpu_custom_call" | custom-call | bytes 12582912 | tf_op jit(solution)/shard_map/load_weights/pallas_call | solution.py:80
  22.2 2.6 %collective-permute-start.8 = (bf16[64,1152]{1,0:T(8,128)(2,1)S(1)}, bf16[64,1152]{1,0:T(8,128)(2,1)S(1)}, u32[]{:S(2)}, u32[]{:S(2)}) collective-permute-start(bf16[64,1152]{1,0:T(8,128)(2,1)S(1)} %add_convert_fusion.after), channel_id=1, source_target_pairs={{0,6},{1,7},{2,4},{3,5},{4,10},{5,11},{6,8},{7,9},{8,14},{9,15},{1... | collective-permute-start | bytes 442376 | tf_op jit(solution)/shard_map/ppermute | solution.py:33
  24.7 1.6 %collective-permute-start.10 = (bf16[64,1152]{1,0:T(8,128)(2,1)S(1)}, bf16[64,1152]{1,0:T(8,128)(2,1)S(1)}, u32[]{:S(2)}, u32[]{:S(2)}) collective-permute-start(bf16[64,1152]{1,0:T(8,128)(2,1)S(1)} %add_convert_fusion.after), channel_id=1, source_target_pairs={{0,4},{1,5},{2,6},{3,7},{4,8},{5,9},{6,10},{7,11},{8,12},{9,13},{1... | collective-permute-start | bytes 442376 | tf_op jit(solution)/shard_map/ppermute | solution.py:33
  26.3 1.8 %collective-permute-done.5.x = bf16[128,896]{1,0:T(8,128)(2,1)S(1)} collective-permute-done((bf16[128,896]{1,0:T(8,128)(2,1)S(1)}, bf16[128,896]{1,0:T(8,128)(2,1)S(1)}, u32[]{:S(2)}, u32[]{:S(2)}) %collective-permute-start.5) | collective-permute-done | bytes 229408 | tf_op jit(solution)/shard_map/ppermute | solution.py:33
  28.7 3.8 %collective-permute-done.8.refs_0_ = bf16[64,1152]{1,0:T(8,128)(2,1)S(1)} collective-permute-done((bf16[64,1152]{1,0:T(8,128)(2,1)S(1)}, bf16[64,1152]{1,0:T(8,128)(2,1)S(1)}, u32[]{:S(2)}, u32[]{:S(2)}) %collective-permute-start.8) | collective-permute-done | bytes 147488 | tf_op jit(solution)/shard_map/ppermute | solution.py:33
  32.5 1.9 %collective-permute-done.10.refs_3_.refs_0_.rest = bf16[64,1152]{1,0:T(8,128)(2,1)S(1)} collective-permute-done((bf16[64,1152]{1,0:T(8,128)(2,1)S(1)}, bf16[64,1152]{1,0:T(8,128)(2,1)S(1)}, u32[]{:S(2)}, u32[]{:S(2)}) %collective-permute-start.10) | collective-permute-done | bytes 147488 | tf_op jit(solution)/shard_map/ppermute | solution.py:33
  34.4 0.7 %project_rows.2 = (f32[128,1536]{1,0:T(8,128)S(1)}, f32[128,1]{1,0:T(8,128)S(1)}) custom-call(bf16[64,1152]{1,0:T(8,128)(2,1)S(1)} %collective-permute-done.8.refs_0_, bf16[64,1152]{1,0:T(8,128)(2,1)S(1)} %collective-permute-done.9.refs_1_, f32[1,2048]{1,0:T(1,128)S(1)} %copy-done, bf16[1,2048,1536]{2,1,0:T(8,128)(2,1)S(1)} %load_weights.3.refs_3_.weight), custom_call_target="tpu_custom_call" | custom-call | flops 452984832 | bytes 3538944 | tf_op jit(solution)/shard_map/project_rows/pallas_call | solution.py:244
  35.1 0.7 %collective-permute-done.11.refs_4_.refs_1_ = bf16[64,1152]{1,0:T(8,128)(2,1)S(1)} collective-permute-done((bf16[64,1152]{1,0:T(8,128)(2,1)S(1)}, bf16[64,1152]{1,0:T(8,128)(2,1)S(1)}, u32[]{:S(2)}, u32[]{:S(2)}) %collective-permute-start.11) | collective-permute-done | bytes 147488 | tf_op jit(solution)/shard_map/ppermute | solution.py:25
  36.4 0.7 %project_rows.3 = (f32[128,1536]{1,0:T(8,128)S(1)}, f32[128,1]{1,0:T(8,128)S(1)}) custom-call(bf16[64,1152]{1,0:T(8,128)(2,1)S(1)} %collective-permute-done.10.refs_3_.refs_0_.rest, bf16[64,1152]{1,0:T(8,128)(2,1)S(1)} %collective-permute-done.11.refs_4_.refs_1_, f32[1,2048]{1,0:T(1,128)S(1)} %copy-done, bf16[1,2048,1536]{2,1,0:T(8,128)(2,1)S(1)} %load_weights.3.refs_3_.weight), custom_call_target="tpu_custom_call" | custom-call | flops 452984832 | bytes 3538944 | tf_op jit(solution)/shard_map/project_rows/pallas_call | solution.py:244
  37.1 0.6 %project_even.1 = (f32[128,1536]{1,0:T(8,128)S(1)}, f32[128,1]{1,0:T(8,128)S(1)}) custom-call(bf16[128,896]{1,0:T(8,128)(2,1)S(1)} %join_chips.1.even, f32[1,2048]{1,0:T(1,128)S(1)} %copy-done, bf16[1,2048,1536]{2,1,0:T(8,128)(2,1)S(1)} %load_weights.3.refs_3_.weight), custom_call_target="tpu_custom_call" | custom-call | flops 352321536 | bytes 2752512 | tf_op jit(solution)/shard_map/project_even/pallas_call | solution.py:272
  37.9 1.4 %project_odd.1 = (bf16[1,64,2048]{2,1,0:T(8,128)(2,1)}, bf16[1,256,1536]{2,1,0:T(8,128)(2,1)}) custom-call(bf16[128,896]{1,0:T(8,128)(2,1)S(1)} %collective-permute-done.12.odd, bf16[128,896]{1,0:T(8,128)(2,1)S(1)} %join_chips.1.even, bf16[64,1152]{1,0:T(8,128)(2,1)S(1)} %collective-permute-done.10.refs_3_.refs_0_.rest, f32[1,2048]{1,0:T(1,128)S(1)} %copy-done, ...), custom_call_target="tpu_custom_call" | custom-call | flops 352321536 | bytes 2752512 | tf_op jit(solution)/shard_map/project_odd/pallas_call | solution.py:327
  (24 shorter events, 2.6 us)
Async XLA Ops:
  1.7 8.8 %collective-permute-start.1 = (bf16[64,1536]{1,0:T(8,128)(2,1)S(1)}, bf16[64,1536]{1,0:T(8,128)(2,1)S(1)}, u32[]{:S(2)}, u32[]{:S(2)}) collective-permute-start(bf16[64,1536]{1,0:T(8,128)(2,1)S(1)} %get-tuple-element.27), channel_id=1, source_target_pairs={{0,2},{1,3},{2,0},{3,1},{4,6},{5,7},{6,4},{7,5},{8,10},{9,11},{10,... | collective-permute-start | bytes 589832 | tf_op jit(solution)/shard_map/ppermute | solution.py:25
  4.7 8.4 %collective-permute-start.2 = (bf16[64,1536]{1,0:T(8,128)(2,1)S(1)}, bf16[64,1536]{1,0:T(8,128)(2,1)S(1)}, u32[]{:S(2)}, u32[]{:S(2)}) collective-permute-start(bf16[64,1536]{1,0:T(8,128)(2,1)S(1)} %get-tuple-element.24.refs_0_), channel_id=1, source_target_pairs={{0,3},{1,2},{2,1},{3,0},{4,7},{5,6},{6,5},{7,4},{8,11},{9,10},{10,... | collective-permute-start | bytes 589832 | tf_op jit(solution)/shard_map/ppermute | solution.py:25
  5.8 7.3 %collective-permute-start = (bf16[64,1536]{1,0:T(8,128)(2,1)S(1)}, bf16[64,1536]{1,0:T(8,128)(2,1)S(1)}, u32[]{:S(2)}, u32[]{:S(2)}) collective-permute-start(bf16[64,1536]{1,0:T(8,128)(2,1)S(1)} %get-tuple-element.26), channel_id=1, source_target_pairs={{0,1},{1,0},{2,3},{3,2},{4,5},{5,4},{6,7},{7,6},{8,9},{9,8},{10,11... | collective-permute-start | bytes 589832 | tf_op jit(solution)/shard_map/ppermute | solution.py:25
  6.0 0.7 %copy-start.1 = (s32[1,2,2]{2,1,0:T(2,128)S(1)}, s32[1,2,2]{2,1,0:T(2,128)}, u32[]{:S(2)}) copy-start(s32[1,2,2]{2,1,0:T(2,128)} %mask.1) | copy-start | bytes 52
  6.7 0.7 %copy-start.2 = (s32[256]{0:T(256)S(1)}, s32[256]{0:T(256)}, u32[]{:S(2)}) copy-start(s32[256]{0:T(256)} %order.1) | copy-start | bytes 3076
  13.9 1.8 %collective-permute-start.4 = (bf16[64,2048]{1,0:T(8,128)(2,1)S(1)}, bf16[64,2048]{1,0:T(8,128)(2,1)S(1)}, u32[]{:S(2)}, u32[]{:S(2)}) collective-permute-start(bf16[64,2048]{1,0:T(8,128)(2,1)S(1)} %get-tuple-element.33), channel_id=1, source_target_pairs={{0,1},{1,0},{2,3},{3,2},{4,5},{5,4},{6,7},{7,6},{8,9},{9,8},{10,11... | collective-permute-start | bytes 786440 | tf_op jit(solution)/shard_map/ppermute | solution.py:25
  14.5 3.1 %collective-permute-start.3 = (bf16[64,2048]{1,0:T(8,128)(2,1)S(1)}, bf16[64,2048]{1,0:T(8,128)(2,1)S(1)}, u32[]{:S(2)}, u32[]{:S(2)}) collective-permute-start(bf16[64,2048]{1,0:T(8,128)(2,1)S(1)} %get-tuple-element.30), channel_id=1, source_target_pairs={{0,1},{1,0},{2,3},{3,2},{4,5},{5,4},{6,7},{7,6},{8,9},{9,8},{10,11... | collective-permute-start | bytes 786440 | tf_op jit(solution)/shard_map/ppermute | solution.py:25
  15.8 6.3 %collective-permute-start.6 = (bf16[64,1152]{1,0:T(8,128)(2,1)S(1)}, bf16[64,1152]{1,0:T(8,128)(2,1)S(1)}, u32[]{:S(2)}, u32[]{:S(2)}) collective-permute-start(bf16[64,1152]{1,0:T(8,128)(2,1)S(1)} %get-tuple-element.38), channel_id=1, source_target_pairs={{0,2},{1,3},{2,0},{3,1},{4,6},{5,7},{6,4},{7,5},{8,10},{9,11},{10,... | collective-permute-start | bytes 442376 | tf_op jit(solution)/shard_map/ppermute | solution.py:25
  17.7 10.4 %collective-permute-start.5 = (bf16[128,896]{1,0:T(8,128)(2,1)S(1)}, bf16[128,896]{1,0:T(8,128)(2,1)S(1)}, u32[]{:S(2)}, u32[]{:S(2)}) collective-permute-start(bf16[128,896]{1,0:T(8,128)(2,1)S(1)} %get-tuple-element.35), channel_id=1, source_target_pairs={{0,4},{1,5},{2,6},{3,7},{4,8},{5,9},{6,10},{7,11},{8,12},{9,13},{1... | collective-permute-start | bytes 688136 | tf_op jit(solution)/shard_map/ppermute | solution.py:33
  19.2 15.2 %copy-start = (f32[1,2048]{1,0:T(1,128)S(1)}, f32[1,2048]{1,0:T(1,128)}, u32[]{:S(2)}) copy-start(f32[1,2048]{1,0:T(1,128)} %gain.3) | copy-start | bytes 24580
  22.2 10.4 %collective-permute-start.8 = (bf16[64,1152]{1,0:T(8,128)(2,1)S(1)}, bf16[64,1152]{1,0:T(8,128)(2,1)S(1)}, u32[]{:S(2)}, u32[]{:S(2)}) collective-permute-start(bf16[64,1152]{1,0:T(8,128)(2,1)S(1)} %add_convert_fusion.after), channel_id=1, source_target_pairs={{0,6},{1,7},{2,4},{3,5},{4,10},{5,11},{6,8},{7,9},{8,14},{9,15},{1... | collective-permute-start | bytes 442376 | tf_op jit(solution)/shard_map/ppermute | solution.py:33
  24.7 9.7 %collective-permute-start.10 = (bf16[64,1152]{1,0:T(8,128)(2,1)S(1)}, bf16[64,1152]{1,0:T(8,128)(2,1)S(1)}, u32[]{:S(2)}, u32[]{:S(2)}) collective-permute-start(bf16[64,1152]{1,0:T(8,128)(2,1)S(1)} %add_convert_fusion.after), channel_id=1, source_target_pairs={{0,4},{1,5},{2,6},{3,7},{4,8},{5,9},{6,10},{7,11},{8,12},{9,13},{1... | collective-permute-start | bytes 442376 | tf_op jit(solution)/shard_map/ppermute | solution.py:33
  28.1 8.1 %collective-permute-start.7 = (bf16[128,896]{1,0:T(8,128)(2,1)S(1)}, bf16[128,896]{1,0:T(8,128)(2,1)S(1)}, u32[]{:S(2)}, u32[]{:S(2)}) collective-permute-start(bf16[128,896]{1,0:T(8,128)(2,1)S(1)} %settle.1.mine), channel_id=1, source_target_pairs={{0,2},{1,3},{2,0},{3,1},{4,6},{5,7},{6,4},{7,5},{8,10},{9,11},{10,... | collective-permute-start | bytes 688136 | tf_op jit(solution)/shard_map/ppermute | solution.py:25
  32.5 1.9 %collective-permute-start.9 = (bf16[64,1152]{1,0:T(8,128)(2,1)S(1)}, bf16[64,1152]{1,0:T(8,128)(2,1)S(1)}, u32[]{:S(2)}, u32[]{:S(2)}) collective-permute-start(bf16[64,1152]{1,0:T(8,128)(2,1)S(1)} %collective-permute-done.8.refs_0_), channel_id=1, source_target_pairs={{0,1},{1,0},{2,3},{3,2},{4,5},{5,4},{6,7},{7,6},{8,9},{9,8},{10,11... | collective-permute-start | bytes 442376 | tf_op jit(solution)/shard_map/ppermute | solution.py:25
  34.4 1.4 %collective-permute-start.11 = (bf16[64,1152]{1,0:T(8,128)(2,1)S(1)}, bf16[64,1152]{1,0:T(8,128)(2,1)S(1)}, u32[]{:S(2)}, u32[]{:S(2)}) collective-permute-start(bf16[64,1152]{1,0:T(8,128)(2,1)S(1)} %collective-permute-done.10.refs_3_.refs_0_.rest), channel_id=1, source_target_pairs={{0,1},{1,0},{2,3},{3,2},{4,5},{5,4},{6,7},{7,6},{8,9},{9,8},{10,11... | collective-permute-start | bytes 442376 | tf_op jit(solution)/shard_map/ppermute | solution.py:25
  36.3 1.6 %collective-permute-start.12 = (bf16[128,896]{1,0:T(8,128)(2,1)S(1)}, bf16[128,896]{1,0:T(8,128)(2,1)S(1)}, u32[]{:S(2)}, u32[]{:S(2)}) collective-permute-start(bf16[128,896]{1,0:T(8,128)(2,1)S(1)} %join_chips.1.even), channel_id=1, source_target_pairs={{0,1},{1,0},{2,3},{3,2},{4,5},{5,4},{6,7},{7,6},{8,9},{9,8},{10,11... | collective-permute-start | bytes 688136 | tf_op jit(solution)/shard_map/ppermute | solution.py:25

commit v11 on v9

--- a/solution.py
+++ b/solution.py
@@ -389,14 +389,15 @@
     blocks = [near_cut[0], swap(near_cut[1], 1)] + far
     stream, out_weight = load((stream_before, out_weight), (1, 4))
     bias = mask_bias(block_mask, token_order, n, rows)
+    (proj_weight,) = load((proj_weight,), (8,), (out_weight,))
+    bias, proj_weight = lax.optimization_barrier((bias, proj_weight))
     near_out, far_out = attend(blocks, bias, tuple(range(1, n, 2)), out_weight)
     near_own, far_own = attend(blocks, bias, tuple(range(0, n, 2)), out_weight)
     cols = out_weight.shape[2] * 7 // 16
     far_partial, *others = far_sum(far_own, swap(far_out, 1), rows, cols)
     partial, own = near_sum(near_own, swap(near_out, 1), stream, far_partial)
     partial = onward(partial, 0)
-    (proj_weight,) = load((proj_weight,), (8,), (own,))
-    total, proj_weight = lax.optimization_barrier((own, proj_weight))
+    total = own
     for k, x in enumerate(others):
         total = total + swap(x, 2 * k + 2).astype(jnp.float32)
     total = total.astype(jnp.bfloat16)

time: 39.5 us -> 39.5 us (level)
  no operation moved by 1% of the time
where the time goes in v11:
time: 39.5 us; the launch traced here: 39.2 us
  Pallas kernels  12.8 us (32%)
  starting transfers between devices  12.3 us (31%)
  waiting for transfers between devices  12 us (30%)
  local copies, waits for them, and re-layouts  1.36 us (3%)
  between operations  0.76 us (2%)
    ppermute x3, waiting for transfers between devices, onward(): return lax.ppermute(x, ('segment', 'seq'), pairs)  7.56 us
    ppermute x10, starting transfers between devices, swap(): return lax.ppermute(x, 'seq', [(i, i ^ by) for i in range(size)])  6.48 us
    ppermute x3, starting transfers between devices, onward(): return lax.ppermute(x, ('segment', 'seq'), pairs)  5.8 us
    pallas_call x2, Pallas kernels, load(): pl.pallas_call(functools.partial(load_kernel, pieces), out_shape=[pltpu.V...  4.51 us
    ppermute x10, waiting for transfers between devices, swap(): return lax.ppermute(x, 'seq', [(i, i ^ by) for i in range(size)])  4.48 us
    pallas_call x2, Pallas kernels, cut(): pl.pallas_call(functools.partial(cut_kernel, js), out_shape=[pltpu.VMEM((...  2.09 us
    pallas_call x2, Pallas kernels, attend(): pl.pallas_call(functools.partial(attend_project_kernel, n, js), out_shape...  1.61 us
    pallas_call x1, Pallas kernels, project_odd(): pl.pallas_call(functools.partial(project_odd_kernel, tile), out_shape=[ja...  1.39 us
  transfers between devices with their start and end apart: 13, of which 9 were waited for; matrix products, arithmetic and copies ran while one was open for 0% of the time, Pallas kernels for 24%

profile of v11, /device:TPU:0, one launch (start us, length us, event | category | flops | bytes accessed | tf_op | source)
XLA Modules:
  0.0 39.2 jit_solution(8803468774258493067)
XLA Ops:
  0.6 1.0 %cut_slices.2 = (bf16[64,1536]{1,0:T(8,128)(2,1)S(1)}, bf16[64,1536]{1,0:T(8,128)(2,1)S(1)}) custom-call(bf16[1,64,6144]{2,1,0:T(8,128)(2,1)} %src.3), custom_call_target="tpu_custom_call" | custom-call | tf_op jit(solution)/shard_map/cut_slices/pallas_call | solution.py:53
  1.7 3.0 %collective-permute-start.1 = (bf16[64,1536]{1,0:T(8,128)(2,1)S(1)}, bf16[64,1536]{1,0:T(8,128)(2,1)S(1)}, u32[]{:S(2)}, u32[]{:S(2)}) collective-permute-start(bf16[64,1536]{1,0:T(8,128)(2,1)S(1)} %get-tuple-element.27), channel_id=1, source_target_pairs={{0,2},{1,3},{2,0},{3,1},{4,6},{5,7},{6,4},{7,5},{8,10},{9,11},{10,... | collective-permute-start | bytes 589832 | tf_op jit(solution)/shard_map/ppermute | solution.py:25
  4.7 1.0 %cut_slices.3 = (bf16[64,1536]{1,0:T(8,128)(2,1)S(1)}, bf16[64,1536]{1,0:T(8,128)(2,1)S(1)}) custom-call(bf16[1,64,6144]{2,1,0:T(8,128)(2,1)} %src.3, bf16[64,1536]{1,0:T(8,128)(2,1)S(1)} %get-tuple-element.24.refs_0_), custom_call_target="tpu_custom_call" | custom-call | tf_op jit(solution)/shard_map/cut_slices/pallas_call | solution.py:53
  6.0 0.7 %copy-done.1 = s32[1,2,2]{2,1,0:T(2,128)S(1)} copy-done((s32[1,2,2]{2,1,0:T(2,128)S(1)}, s32[1,2,2]{2,1,0:T(2,128)}, u32[]{:S(2)}) %copy-start.1) | copy-done | bytes 40
  6.7 0.7 %copy-done.2 = s32[256]{0:T(256)S(1)} copy-done((s32[256]{0:T(256)S(1)}, s32[256]{0:T(256)}, u32[]{:S(2)}) %copy-start.2) | copy-done | bytes 1048
  7.4 1.0 %mask_bias.1.refs_4_ = f32[256,256]{1,0:T(8,128)S(1)} custom-call(s32[1,2,2]{2,1,0:T(2,128)S(1)} %copy-done.1, s32[256]{0:T(256)S(1)} %copy-done.2), custom_call_target="tpu_custom_call" | custom-call | tf_op jit(solution)/shard_map/mask_bias/pallas_call | solution.py:373
  8.4 1.6 %load_weights.2 = (bf16[1,64,2048]{2,1,0:T(8,128)(2,1)S(1)}, bf16[1,512,2048]{2,1,0:T(8,128)(2,1)S(1)}) custom-call(bf16[1,64,2048]{2,1,0:T(8,128)(2,1)} %refs_0_.2, bf16[1,512,2048]{2,1,0:T(8,128)(2,1)} %refs_1_.1), custom_call_target="tpu_custom_call" | custom-call | bytes 4718592 | tf_op jit(solution)/shard_map/load_weights/pallas_call | solution.py:80
  10.0 2.9 %load_weights.3.refs_3_.weight = bf16[1,2048,1536]{2,1,0:T(8,128)(2,1)S(1)} custom-call(bf16[1,2048,1536]{2,1,0:T(8,128)(2,1)} %refs_0_.3, bf16[1,512,2048]{2,1,0:T(8,128)(2,1)S(1)} %get-tuple-element.28.refs_1_.refs_5_), custom_call_target="tpu_custom_call" | custom-call | bytes 12582912 | tf_op jit(solution)/shard_map/load_weights/pallas_call | solution.py:80
  13.1 0.8 %attend_project.3 = (bf16[64,2048]{1,0:T(8,128)(2,1)S(1)}, bf16[64,2048]{1,0:T(8,128)(2,1)S(1)}) custom-call(bf16[64,1536]{1,0:T(8,128)(2,1)S(1)} %get-tuple-element.25.refs_0_, bf16[64,1536]{1,0:T(8,128)(2,1)S(1)} %collective-permute-done.refs_1_, bf16[64,1536]{1,0:T(8,128)(2,1)S(1)} %collective-permute-done.1.refs_2_, ...), custom_call_target="tpu_custom_call" | custom-call | flops 335544320 | bytes 786432 | tf_op jit(solution)/shard_map/attend_project/pallas_call | solution.py:127
  13.9 0.6 %collective-permute-start.4 = (bf16[64,2048]{1,0:T(8,128)(2,1)S(1)}, bf16[64,2048]{1,0:T(8,128)(2,1)S(1)}, u32[]{:S(2)}, u32[]{:S(2)}) collective-permute-start(bf16[64,2048]{1,0:T(8,128)(2,1)S(1)} %get-tuple-element.34), channel_id=1, source_target_pairs={{0,1},{1,0},{2,3},{3,2},{4,5},{5,4},{6,7},{7,6},{8,9},{9,8},{10,11... | collective-permute-start | bytes 786440 | tf_op jit(solution)/shard_map/ppermute | solution.py:25
  14.6 0.8 %attend_project.2 = (bf16[64,2048]{1,0:T(8,128)(2,1)S(1)}, bf16[64,2048]{1,0:T(8,128)(2,1)S(1)}) custom-call(bf16[64,1536]{1,0:T(8,128)(2,1)S(1)} %get-tuple-element.25.refs_0_, bf16[64,1536]{1,0:T(8,128)(2,1)S(1)} %collective-permute-done.refs_1_, bf16[64,1536]{1,0:T(8,128)(2,1)S(1)} %collective-permute-done.1.refs_2_, ...), custom_call_target="tpu_custom_call" | custom-call | flops 335544320 | bytes 786432 | tf_op jit(solution)/shard_map/attend_project/pallas_call | solution.py:127
  15.8 1.8 %collective-permute-start.6 = (bf16[64,1152]{1,0:T(8,128)(2,1)S(1)}, bf16[64,1152]{1,0:T(8,128)(2,1)S(1)}, u32[]{:S(2)}, u32[]{:S(2)}) collective-permute-start(bf16[64,1152]{1,0:T(8,128)(2,1)S(1)} %get-tuple-element.38), channel_id=1, source_target_pairs={{0,2},{1,3},{2,0},{3,1},{4,6},{5,7},{6,4},{7,5},{8,10},{9,11},{10,... | collective-permute-start | bytes 442376 | tf_op jit(solution)/shard_map/ppermute | solution.py:25
  17.7 1.5 %collective-permute-start.5 = (bf16[128,896]{1,0:T(8,128)(2,1)S(1)}, bf16[128,896]{1,0:T(8,128)(2,1)S(1)}, u32[]{:S(2)}, u32[]{:S(2)}) collective-permute-start(bf16[128,896]{1,0:T(8,128)(2,1)S(1)} %get-tuple-element.36), channel_id=1, source_target_pairs={{0,4},{1,5},{2,6},{3,7},{4,8},{5,9},{6,10},{7,11},{8,12},{9,13},{1... | collective-permute-start | bytes 688136 | tf_op jit(solution)/shard_map/ppermute | solution.py:33
  19.2 2.7 %collective-permute-done.6 = bf16[64,1152]{1,0:T(8,128)(2,1)S(1)} collective-permute-done((bf16[64,1152]{1,0:T(8,128)(2,1)S(1)}, bf16[64,1152]{1,0:T(8,128)(2,1)S(1)}, u32[]{:S(2)}, u32[]{:S(2)}) %collective-permute-start.6) | collective-permute-done | bytes 147488 | tf_op jit(solution)/shard_map/ppermute | solution.py:25
  22.0 2.7 %collective-permute-start.8 = (bf16[64,1152]{1,0:T(8,128)(2,1)S(1)}, bf16[64,1152]{1,0:T(8,128)(2,1)S(1)}, u32[]{:S(2)}, u32[]{:S(2)}) collective-permute-start(bf16[64,1152]{1,0:T(8,128)(2,1)S(1)} %add_convert_fusion.after), channel_id=1, source_target_pairs={{0,6},{1,7},{2,4},{3,5},{4,10},{5,11},{6,8},{7,9},{8,14},{9,15},{1... | collective-permute-start | bytes 442376 | tf_op jit(solution)/shard_map/ppermute | solution.py:33
  24.7 1.6 %collective-permute-start.10 = (bf16[64,1152]{1,0:T(8,128)(2,1)S(1)}, bf16[64,1152]{1,0:T(8,128)(2,1)S(1)}, u32[]{:S(2)}, u32[]{:S(2)}) collective-permute-start(bf16[64,1152]{1,0:T(8,128)(2,1)S(1)} %add_convert_fusion.after), channel_id=1, source_target_pairs={{0,4},{1,5},{2,6},{3,7},{4,8},{5,9},{6,10},{7,11},{8,12},{9,13},{1... | collective-permute-start | bytes 442376 | tf_op jit(solution)/shard_map/ppermute | solution.py:33
  26.3 1.8 %collective-permute-done.5.x = bf16[128,896]{1,0:T(8,128)(2,1)S(1)} collective-permute-done((bf16[128,896]{1,0:T(8,128)(2,1)S(1)}, bf16[128,896]{1,0:T(8,128)(2,1)S(1)}, u32[]{:S(2)}, u32[]{:S(2)}) %collective-permute-start.5) | collective-permute-done | bytes 229408 | tf_op jit(solution)/shard_map/ppermute | solution.py:33
  28.1 0.6 %collective-permute-start.7 = (bf16[128,896]{1,0:T(8,128)(2,1)S(1)}, bf16[128,896]{1,0:T(8,128)(2,1)S(1)}, u32[]{:S(2)}, u32[]{:S(2)}) collective-permute-start(bf16[128,896]{1,0:T(8,128)(2,1)S(1)} %settle.1.mine), channel_id=1, source_target_pairs={{0,2},{1,3},{2,0},{3,1},{4,6},{5,7},{6,4},{7,5},{8,10},{9,11},{10,... | collective-permute-start | bytes 688136 | tf_op jit(solution)/shard_map/ppermute | solution.py:25
  28.7 3.7 %collective-permute-done.8.refs_0_ = bf16[64,1152]{1,0:T(8,128)(2,1)S(1)} collective-permute-done((bf16[64,1152]{1,0:T(8,128)(2,1)S(1)}, bf16[64,1152]{1,0:T(8,128)(2,1)S(1)}, u32[]{:S(2)}, u32[]{:S(2)}) %collective-permute-start.8) | collective-permute-done | bytes 147488 | tf_op jit(solution)/shard_map/ppermute | solution.py:33
  32.5 2.0 %collective-permute-done.10.refs_3_.refs_0_.rest = bf16[64,1152]{1,0:T(8,128)(2,1)S(1)} collective-permute-done((bf16[64,1152]{1,0:T(8,128)(2,1)S(1)}, bf16[64,1152]{1,0:T(8,128)(2,1)S(1)}, u32[]{:S(2)}, u32[]{:S(2)}) %collective-permute-start.10) | collective-permute-done | bytes 147488 | tf_op jit(solution)/shard_map/ppermute | solution.py:33
  34.4 0.7 %project_rows.2 = (f32[128,1536]{1,0:T(8,128)S(1)}, f32[128,1]{1,0:T(8,128)S(1)}) custom-call(bf16[64,1152]{1,0:T(8,128)(2,1)S(1)} %collective-permute-done.8.refs_0_, bf16[64,1152]{1,0:T(8,128)(2,1)S(1)} %collective-permute-done.9.refs_1_, f32[1,2048]{1,0:T(1,128)S(1)} %copy-done, bf16[1,2048,1536]{2,1,0:T(8,128)(2,1)S(1)} %load_weights.3.refs_3_.weight), custom_call_target="tpu_custom_call" | custom-call | flops 452984832 | bytes 3538944 | tf_op jit(solution)/shard_map/project_rows/pallas_call | solution.py:241
  35.1 0.7 %collective-permute-done.11.refs_4_.refs_1_ = bf16[64,1152]{1,0:T(8,128)(2,1)S(1)} collective-permute-done((bf16[64,1152]{1,0:T(8,128)(2,1)S(1)}, bf16[64,1152]{1,0:T(8,128)(2,1)S(1)}, u32[]{:S(2)}, u32[]{:S(2)}) %collective-permute-start.11) | collective-permute-done | bytes 147488 | tf_op jit(solution)/shard_map/ppermute | solution.py:25
  36.4 0.7 %project_rows.3 = (f32[128,1536]{1,0:T(8,128)S(1)}, f32[128,1]{1,0:T(8,128)S(1)}) custom-call(bf16[64,1152]{1,0:T(8,128)(2,1)S(1)} %collective-permute-done.10.refs_3_.refs_0_.rest, bf16[64,1152]{1,0:T(8,128)(2,1)S(1)} %collective-permute-done.11.refs_4_.refs_1_, f32[1,2048]{1,0:T(1,128)S(1)} %copy-done, bf16[1,2048,1536]{2,1,0:T(8,128)(2,1)S(1)} %load_weights.3.refs_3_.weight), custom_call_target="tpu_custom_call" | custom-call | flops 452984832 | bytes 3538944 | tf_op jit(solution)/shard_map/project_rows/pallas_call | solution.py:241
  37.9 1.4 %project_odd.1 = (bf16[1,64,2048]{2,1,0:T(8,128)(2,1)}, bf16[1,256,1536]{2,1,0:T(8,128)(2,1)}) custom-call(bf16[128,896]{1,0:T(8,128)(2,1)S(1)} %collective-permute-done.12.odd, bf16[128,896]{1,0:T(8,128)(2,1)S(1)} %join_chips.1.even, bf16[64,1152]{1,0:T(8,128)(2,1)S(1)} %collective-permute-done.10.refs_3_.refs_0_.rest, f32[1,2048]{1,0:T(1,128)S(1)} %copy-done, ...), custom_call_target="tpu_custom_call" | custom-call | flops 352321536 | bytes 2752512 | tf_op jit(solution)/shard_map/project_odd/pallas_call | solution.py:324
  (24 shorter events, 2.3 us)
Async XLA Ops:
  1.7 11.2 %collective-permute-start.1 = (bf16[64,1536]{1,0:T(8,128)(2,1)S(1)}, bf16[64,1536]{1,0:T(8,128)(2,1)S(1)}, u32[]{:S(2)}, u32[]{:S(2)}) collective-permute-start(bf16[64,1536]{1,0:T(8,128)(2,1)S(1)} %get-tuple-element.27), channel_id=1, source_target_pairs={{0,2},{1,3},{2,0},{3,1},{4,6},{5,7},{6,4},{7,5},{8,10},{9,11},{10,... | collective-permute-start | bytes 589832 | tf_op jit(solution)/shard_map/ppermute | solution.py:25
  4.7 8.4 %collective-permute-start.2 = (bf16[64,1536]{1,0:T(8,128)(2,1)S(1)}, bf16[64,1536]{1,0:T(8,128)(2,1)S(1)}, u32[]{:S(2)}, u32[]{:S(2)}) collective-permute-start(bf16[64,1536]{1,0:T(8,128)(2,1)S(1)} %get-tuple-element.24.refs_0_), channel_id=1, source_target_pairs={{0,3},{1,2},{2,1},{3,0},{4,7},{5,6},{6,5},{7,4},{8,11},{9,10},{10,... | collective-permute-start | bytes 589832 | tf_op jit(solution)/shard_map/ppermute | solution.py:25
  5.8 7.3 %collective-permute-start = (bf16[64,1536]{1,0:T(8,128)(2,1)S(1)}, bf16[64,1536]{1,0:T(8,128)(2,1)S(1)}, u32[]{:S(2)}, u32[]{:S(2)}) collective-permute-start(bf16[64,1536]{1,0:T(8,128)(2,1)S(1)} %get-tuple-element.26), channel_id=1, source_target_pairs={{0,1},{1,0},{2,3},{3,2},{4,5},{5,4},{6,7},{7,6},{8,9},{9,8},{10,11... | collective-permute-start | bytes 589832 | tf_op jit(solution)/shard_map/ppermute | solution.py:25
  6.0 0.7 %copy-start.1 = (s32[1,2,2]{2,1,0:T(2,128)S(1)}, s32[1,2,2]{2,1,0:T(2,128)}, u32[]{:S(2)}) copy-start(s32[1,2,2]{2,1,0:T(2,128)} %mask.1) | copy-start | bytes 52
  6.7 0.7 %copy-start.2 = (s32[256]{0:T(256)S(1)}, s32[256]{0:T(256)}, u32[]{:S(2)}) copy-start(s32[256]{0:T(256)} %order.1) | copy-start | bytes 3076
  12.9 21.5 %copy-start = (f32[1,2048]{1,0:T(1,128)S(1)}, f32[1,2048]{1,0:T(1,128)}, u32[]{:S(2)}) copy-start(f32[1,2048]{1,0:T(1,128)} %gain.3) | copy-start | bytes 24580
  13.9 1.8 %collective-permute-start.4 = (bf16[64,2048]{1,0:T(8,128)(2,1)S(1)}, bf16[64,2048]{1,0:T(8,128)(2,1)S(1)}, u32[]{:S(2)}, u32[]{:S(2)}) collective-permute-start(bf16[64,2048]{1,0:T(8,128)(2,1)S(1)} %get-tuple-element.34), channel_id=1, source_target_pairs={{0,1},{1,0},{2,3},{3,2},{4,5},{5,4},{6,7},{7,6},{8,9},{9,8},{10,11... | collective-permute-start | bytes 786440 | tf_op jit(solution)/shard_map/ppermute | solution.py:25
  14.5 3.1 %collective-permute-start.3 = (bf16[64,2048]{1,0:T(8,128)(2,1)S(1)}, bf16[64,2048]{1,0:T(8,128)(2,1)S(1)}, u32[]{:S(2)}, u32[]{:S(2)}) collective-permute-start(bf16[64,2048]{1,0:T(8,128)(2,1)S(1)} %get-tuple-element.31), channel_id=1, source_target_pairs={{0,1},{1,0},{2,3},{3,2},{4,5},{5,4},{6,7},{7,6},{8,9},{9,8},{10,11... | collective-permute-start | bytes 786440 | tf_op jit(solution)/shard_map/ppermute | solution.py:25
  15.8 6.2 %collective-permute-start.6 = (bf16[64,1152]{1,0:T(8,128)(2,1)S(1)}, bf16[64,1152]{1,0:T(8,128)(2,1)S(1)}, u32[]{:S(2)}, u32[]{:S(2)}) collective-permute-start(bf16[64,1152]{1,0:T(8,128)(2,1)S(1)} %get-tuple-element.38), channel_id=1, source_target_pairs={{0,2},{1,3},{2,0},{3,1},{4,6},{5,7},{6,4},{7,5},{8,10},{9,11},{10,... | collective-permute-start | bytes 442376 | tf_op jit(solution)/shard_map/ppermute | solution.py:25
  17.7 10.4 %collective-permute-start.5 = (bf16[128,896]{1,0:T(8,128)(2,1)S(1)}, bf16[128,896]{1,0:T(8,128)(2,1)S(1)}, u32[]{:S(2)}, u32[]{:S(2)}) collective-permute-start(bf16[128,896]{1,0:T(8,128)(2,1)S(1)} %get-tuple-element.36), channel_id=1, source_target_pairs={{0,4},{1,5},{2,6},{3,7},{4,8},{5,9},{6,10},{7,11},{8,12},{9,13},{1... | collective-permute-start | bytes 688136 | tf_op jit(solution)/shard_map/ppermute | solution.py:33
  22.0 10.5 %collective-permute-start.8 = (bf16[64,1152]{1,0:T(8,128)(2,1)S(1)}, bf16[64,1152]{1,0:T(8,128)(2,1)S(1)}, u32[]{:S(2)}, u32[]{:S(2)}) collective-permute-start(bf16[64,1152]{1,0:T(8,128)(2,1)S(1)} %add_convert_fusion.after), channel_id=1, source_target_pairs={{0,6},{1,7},{2,4},{3,5},{4,10},{5,11},{6,8},{7,9},{8,14},{9,15},{1... | collective-permute-start | bytes 442376 | tf_op jit(solution)/shard_map/ppermute | solution.py:33
  24.7 9.7 %collective-permute-start.10 = (bf16[64,1152]{1,0:T(8,128)(2,1)S(1)}, bf16[64,1152]{1,0:T(8,128)(2,1)S(1)}, u32[]{:S(2)}, u32[]{:S(2)}) collective-permute-start(bf16[64,1152]{1,0:T(8,128)(2,1)S(1)} %add_convert_fusion.after), channel_id=1, source_target_pairs={{0,4},{1,5},{2,6},{3,7},{4,8},{5,9},{6,10},{7,11},{8,12},{9,13},{1... | collective-permute-start | bytes 442376 | tf_op jit(solution)/shard_map/ppermute | solution.py:33
  28.1 8.1 %collective-permute-start.7 = (bf16[128,896]{1,0:T(8,128)(2,1)S(1)}, bf16[128,896]{1,0:T(8,128)(2,1)S(1)}, u32[]{:S(2)}, u32[]{:S(2)}) collective-permute-start(bf16[128,896]{1,0:T(8,128)(2,1)S(1)} %settle.1.mine), channel_id=1, source_target_pairs={{0,2},{1,3},{2,0},{3,1},{4,6},{5,7},{6,4},{7,5},{8,10},{9,11},{10,... | collective-permute-start | bytes 688136 | tf_op jit(solution)/shard_map/ppermute | solution.py:25
  32.5 2.0 %collective-permute-start.9 = (bf16[64,1152]{1,0:T(8,128)(2,1)S(1)}, bf16[64,1152]{1,0:T(8,128)(2,1)S(1)}, u32[]{:S(2)}, u32[]{:S(2)}) collective-permute-start(bf16[64,1152]{1,0:T(8,128)(2,1)S(1)} %collective-permute-done.8.refs_0_), channel_id=1, source_target_pairs={{0,1},{1,0},{2,3},{3,2},{4,5},{5,4},{6,7},{7,6},{8,9},{9,8},{10,11... | collective-permute-start | bytes 442376 | tf_op jit(solution)/shard_map/ppermute | solution.py:25
  34.4 1.4 %collective-permute-start.11 = (bf16[64,1152]{1,0:T(8,128)(2,1)S(1)}, bf16[64,1152]{1,0:T(8,128)(2,1)S(1)}, u32[]{:S(2)}, u32[]{:S(2)}) collective-permute-start(bf16[64,1152]{1,0:T(8,128)(2,1)S(1)} %collective-permute-done.10.refs_3_.refs_0_.rest), channel_id=1, source_target_pairs={{0,1},{1,0},{2,3},{3,2},{4,5},{5,4},{6,7},{7,6},{8,9},{9,8},{10,11... | collective-permute-start | bytes 442376 | tf_op jit(solution)/shard_map/ppermute | solution.py:25
  36.3 1.6 %collective-permute-start.12 = (bf16[128,896]{1,0:T(8,128)(2,1)S(1)}, bf16[128,896]{1,0:T(8,128)(2,1)S(1)}, u32[]{:S(2)}, u32[]{:S(2)}) collective-permute-start(bf16[128,896]{1,0:T(8,128)(2,1)S(1)} %join_chips.1.even), channel_id=1, source_target_pairs={{0,1},{1,0},{2,3},{3,2},{4,5},{5,4},{6,7},{7,6},{8,9},{9,8},{10,11... | collective-permute-start | bytes 688136 | tf_op jit(solution)/shard_map/ppermute | solution.py:25
